TPU v7x, 32 devices: a whole 2x2x4 slice. The times are simulated.
32 devices in a mesh: pair: 8 (over y, x, core), row: 4 (over z).
Axes of the slice: x: 2, y: 2, z: 4, core: 2. Of those that a mesh axis runs over, the one named last changes fastest.
Arguments:
- r_factor: float32 [4096, 4096], P(('row', 'pair')), may hold values from -40 to 40, as said below
- block_slots: int32 [64], replicated, may hold values from 0 to 63, as said below
Outputs:
- rotated: float32 [4096, 4096], P('row', 'pair')
- off_ratio: float32 [], replicated
Inputs may be any that keep to these rules, and one draw needn't show every extreme that they name: `block_slots`: each of the 64 column blocks appears exactly once. `r_factor`: entries below the diagonal are zero and the diagonal is positive.
All inputs are finite; a program needn't handle non-finite values.
Results may differ from a plain program's by a relative error of at most 0.0001.
Values sent between devices are 32-bit elements; how exact they have to be, the bound alone decides.
No kernel may reach another device: no remote copies, remote signals or barrier semaphores. Data moves between devices by JAX's collectives and lax.ppermute only.
A program may use at most 64 MiB of HBM per device.

v0:
```python
import jax
import jax.numpy as jnp
from jax import lax
from jax.sharding import PartitionSpec as P

BLOCK = 64
ITERS = 3


def passed_along(value, axis, by):
    count = lax.axis_size(axis)
    pairs = [(i, i + by) for i in range(count) if 0 <= i + by < count]
    return lax.ppermute(value, axis, pairs)


def cayley(pair_gram):
    size_n = pair_gram.shape[0]
    diag_vals = jnp.diagonal(pair_gram)
    spread = diag_vals[:, None] - diag_vals[None, :]
    denom = 2.0 * (diag_vals[:, None] ** 2 + diag_vals[None, :] ** 2)
    skew_part = pair_gram * spread / denom
    unit_matrix = jnp.eye(size_n, dtype=pair_gram.dtype)
    minus_part = unit_matrix - skew_part
    system = unit_matrix - jnp.dot(skew_part, skew_part, precision=lax.Precision.HIGHEST)
    product = jnp.dot(minus_part, minus_part, precision=lax.Precision.HIGHEST)
    factor = jnp.linalg.cholesky(system)
    return jax.scipy.linalg.cho_solve((factor, True), product.T).T


def square_sums(rows_part):
    row_ids = jnp.arange(rows_part.shape[1], dtype=jnp.int32)[:, None]
    col_ids = jnp.arange(rows_part.shape[2], dtype=jnp.int32)[None, :]
    on_diag = (row_ids == col_ids)[None, :, :]
    squares = rows_part * rows_part
    return (jnp.sum(jnp.where(on_diag, 0.0, squares)), jnp.sum(jnp.where(on_diag, squares, 0.0)))


def on_device(r_factor, block_slots):
    rows_in, total_cols = r_factor.shape
    blocks = total_cols // BLOCK
    pair_width = 2 * BLOCK
    arranged = jnp.take(r_factor.reshape(rows_in, blocks, BLOCK), block_slots, axis=1)
    arranged = arranged.reshape(rows_in, blocks // 2, pair_width)
    received = lax.all_to_all(arranged, "pair", split_axis=1, concat_axis=0, tiled=True)
    column = jnp.transpose(received, (1, 0, 2))
    local_pairs = column.shape[0]
    rows_here = column.shape[1]
    totals = None
    for sweep in range(ITERS):
        partial_value = jnp.einsum("pri,prj->pij", column, column, precision=lax.Precision.HIGHEST)
        pair_gram = lax.psum(partial_value, "row")
        if sweep == 0:
            off_part, diag_part = square_sums(pair_gram)
            totals = lax.psum((off_part, diag_part), "pair")
        rotation = jax.vmap(cayley)(pair_gram)
        column = jnp.einsum("pri,pij->prj", column, rotation, precision=lax.Precision.HIGHEST)
    upper_half = column[:, :, :BLOCK]
    lower_half = column[:, :, BLOCK:]
    pair_index = lax.axis_index("pair")
    pair_count = lax.axis_size("pair")
    global_ids = pair_index * local_pairs + jnp.arange(local_pairs, dtype=jnp.int32)
    last_id = pair_count * local_pairs - 1
    first_mask = (global_ids == 0)[:, None, None]
    last_mask = (global_ids == last_id)[:, None, None]
    forward = jnp.where(first_mask, lower_half, upper_half)
    came_up = passed_along(forward[local_pairs - 1], "pair", 1)
    came_down = passed_along(lower_half[0], "pair", -1)
    before = jnp.concatenate([came_up[None], forward[: local_pairs - 1]], axis=0)
    after = jnp.concatenate([lower_half[1:], came_down[None]], axis=0)
    new_upper = jnp.where(first_mask, upper_half, before)
    new_lower = jnp.where(last_mask, upper_half, after)
    joined = jnp.concatenate([new_upper, new_lower], axis=2)
    rotated = jnp.transpose(joined, (1, 0, 2)).reshape(rows_here, local_pairs * pair_width)
    off_ratio = jnp.sqrt(totals[0] / totals[1])
    return (rotated, off_ratio)


def solution(mesh):
    in_specs = (P(("row", "pair"), None), P())
    out_specs = (P("row", "pair"), P())
    return jax.shard_map(
        on_device, mesh=mesh, in_specs=in_specs, out_specs=out_specs, check_vma=False
    )
```

profile of v0, /device:TPU:0, one launch (start us, length us, event | category | flops | bytes accessed | tf_op | source)
XLA Modules:
  0.0 513.3 jit_solution(1502132101207758613)
XLA Ops:
  7.2 0.7 compare_and_fusion
  7.8 0.7 compare_select_fusion
  8.5 0.1 broadcast_in_dim.98
  8.8 2.9 copy.118
  11.7 2.3 gather_fusion
  14.0 1.7 broadcast_select_fusion
  15.6 5.2 %all-to-all-start = ((f32[128,32,128]{0,2,1:T(8,128)}), f32[128,32,128]{0,2,1:T(8,128)S(1)}, u32[]{:S(2)}, u32[]{:S(2)}) async-start(f32[128,32,128]{0,2,1:T(8,128)} %broadcast_select_fusion), calls=%async_computation | async-start | bytes 4194304 | tf_op jit(solution)/shard_map/all_to_all | solution.py:44
  20.9 26.6 %all-to-all-done = f32[128,32,128]{0,2,1:T(8,128)S(1)} async-done(((f32[128,32,128]{0,2,1:T(8,128)}), f32[128,32,128]{0,2,1:T(8,128)S(1)}, u32[]{:S(2)}, u32[]{:S(2)}) %all-to-all-start) | async-done | bytes 2097184 | tf_op jit(solution)/shard_map/all_to_all | solution.py:44
  47.5 1.3 copy-done.3
  48.8 1.9 copy.120
  50.7 4.3 fusion.33
  55.0 0.3 all-reduce.7.cloned.1.call-start
  55.3 34.6 %all-reduce.5.cloned.1.call-done = f32[4,128,128]{1,2,0:T(8,128)} async-done(((f32[4,128,128]{1,2,0:T(8,128)}), f32[4,128,128]{1,2,0:T(8,128)}) %all-reduce.5.cloned.1.call-update) | async-done | bytes 262160 | tf_op jit(solution)/shard_map/psum | solution.py:51
  89.9 8.5 %copy.123 = f32[4,128,128]{0,2,1:T(8,128)} copy(f32[4,128,128]{1,2,0:T(8,128)} %all-reduce.5.cloned.1.call-done) | data formatting | bytes 524288 | tf_op jit(solution)/shard_map/psum | solution.py:51
  98.3 1.8 gather_fusion.1
  100.2 0.7 convolution_subtract_fusion.2
  100.8 0.1 copy.128
  101.0 46.9 %custom-call.18 = f32[4,128,128]{2,1,0:T(8,128)S(1)} custom-call(f32[4,128,128]{2,1,0:T(8,128)S(1)} %fusion.14), custom_call_target="Cholesky" | custom-call | tf_op jit(solution)/shard_map/vmap(jit(cholesky))/cholesky | solution.py:26
  148.0 0.1 compare_reduce_fusion.2
  148.1 0.1 select_bitcast_fusion.2
  148.2 39.6 %custom-call.19 = f32[4,1,128,128]{2,3,1,0:T(8,128)S(1)} custom-call(f32[4,1,128,128]{3,2,1,0:T(8,128)S(1)} %select_bitcast_fusion.2), custom_call_target="InvertDiagBlocksLowerTriangular" | custom-call | tf_op jit(solution)/shard_map/vmap(jit(_cho_solve))/triangular_solve | solution.py:27
  187.8 0.6 fusion.19
  188.4 0.6 fusion.12
  189.0 0.4 fusion.10
  189.4 1.9 fusion.34
  191.4 1.3 copy-done
  192.7 4.3 fusion.35
  197.0 35.2 %all-reduce.7.cloned.1.call-done = f32[4,128,128]{1,2,0:T(8,128)} async-done(((f32[4,128,128]{1,2,0:T(8,128)}), f32[4,128,128]{1,2,0:T(8,128)}) %all-reduce.7.cloned.1.call-update) | async-done | bytes 262160 | tf_op jit(solution)/shard_map/psum | solution.py:51
  232.2 8.8 %copy.133 = f32[4,128,128]{0,2,1:T(8,128)} copy(f32[4,128,128]{1,2,0:T(8,128)} %all-reduce.7.cloned.1.call-done) | data formatting | bytes 524288 | tf_op jit(solution)/shard_map/psum | solution.py:51
  241.0 1.8 gather_fusion.2
  242.9 0.7 convolution_subtract_fusion.1
  243.6 0.1 copy.138
  243.7 46.9 %custom-call.20 = f32[4,128,128]{2,1,0:T(8,128)S(1)} custom-call(f32[4,128,128]{2,1,0:T(8,128)S(1)} %fusion.9), custom_call_target="Cholesky" | custom-call | tf_op jit(solution)/shard_map/vmap(jit(cholesky))/cholesky | solution.py:26
  290.7 0.1 compare_reduce_fusion.1
  290.9 39.5 %custom-call.21 = f32[4,1,128,128]{2,3,1,0:T(8,128)S(1)} custom-call(f32[4,1,128,128]{3,2,1,0:T(8,128)S(1)} %select_bitcast_fusion.1), custom_call_target="InvertDiagBlocksLowerTriangular" | custom-call | tf_op jit(solution)/shard_map/vmap(jit(_cho_solve))/triangular_solve | solution.py:27
  330.4 0.6 fusion.17
  331.1 0.6 fusion.7
  331.7 0.4 fusion.5
  332.1 3.5 fusion.36
  335.6 4.3 fusion.37
  339.9 35.2 %all-reduce.9.cloned.1.call-done = f32[4,128,128]{1,2,0:T(8,128)} async-done(((f32[4,128,128]{1,2,0:T(8,128)}), f32[4,128,128]{1,2,0:T(8,128)}) %all-reduce.9.cloned.1.call-update) | async-done | bytes 262160 | tf_op jit(solution)/shard_map/psum | solution.py:51
  375.1 8.5 %copy.143 = f32[4,128,128]{0,2,1:T(8,128)} copy(f32[4,128,128]{1,2,0:T(8,128)} %all-reduce.9.cloned.1.call-done) | data formatting | bytes 524288 | tf_op jit(solution)/shard_map/psum | solution.py:51
  383.5 1.8 gather_fusion.3
  385.4 0.7 convolution_subtract_fusion
  386.0 0.1 copy.148
  386.2 0.7 fusion.4
  386.9 47.9 %custom-call.22 = f32[4,128,128]{2,1,0:T(8,128)S(1)} custom-call(f32[4,128,128]{2,1,0:T(8,128)} %fusion.4), custom_call_target="Cholesky" | custom-call | tf_op jit(solution)/shard_map/vmap(jit(cholesky))/cholesky | solution.py:26
  434.8 0.1 compare_reduce_fusion
  435.1 39.3 %custom-call.23 = f32[4,1,128,128]{2,3,1,0:T(8,128)S(1)} custom-call(f32[4,1,128,128]{3,2,1,0:T(8,128)S(1)} %select_bitcast_fusion), custom_call_target="InvertDiagBlocksLowerTriangular" | custom-call | tf_op jit(solution)/shard_map/vmap(jit(_cho_solve))/triangular_solve | solution.py:27
  474.4 0.7 fusion.15
  475.0 0.6 fusion.2
  475.7 0.4 fusion
  476.1 2.0 fusion.38
  478.1 0.8 slice_bitcast_fusion
  478.8 1.3 collective-permute-start.1
  480.1 0.2 slice_select_fusion
  480.3 0.7 slice_bitcast_fusion.1
  481.1 3.7 collective-permute-start
  484.8 0.8 select_reduce_fusion.3
  485.6 13.8 %all-reduce = (f32[]{:T(128)}, f32[]{:T(128)}) all-reduce(f32[]{:T(128)} %get-tuple-element.13, f32[]{:T(128)} %get-tuple-element.12), channel_id=1, replica_groups=mesh['pair'=8,'row'=4] {'pair'}, use_global_device_ids=true, to_apply=%region_6.9 | all-reduce | flops 2 | bytes 16 | tf_op jit(solution)/shard_map/psum | solution.py:54
  500.7 1.2 slice.50
  502.0 1.4 maximum_select_fusion
  503.4 0.1 pad_maximum_fusion
  503.6 1.8 copy.151
  (43 shorter events, 1.1 us)
Async XLA Ops:
  15.6 31.8 %all-to-all-start = ((f32[128,32,128]{0,2,1:T(8,128)}), f32[128,32,128]{0,2,1:T(8,128)S(1)}, u32[]{:S(2)}, u32[]{:S(2)}) async-start(f32[128,32,128]{0,2,1:T(8,128)} %broadcast_select_fusion), calls=%async_computation | async-start | bytes 4194304 | tf_op jit(solution)/shard_map/all_to_all | solution.py:44
  20.8 69.1 %all-reduce.5.cloned.1.call-start = ((), (), s32[]{:S(2)}) async-start(), calls=%async_computation.1 | async-start | bytes 524288 | tf_op jit(solution)/shard_map/psum | solution.py:51
  47.5 1.3 copy-start.3
  55.0 177.2 %all-reduce.7.cloned.1.call-start = ((), (), s32[]{:S(2)}) async-start(), calls=%async_computation.2 | async-start | bytes 524288 | tf_op jit(solution)/shard_map/psum | solution.py:51
  89.9 10.3 %copy-start.4 = (f32[4,128,128]{1,2,0:T(8,128)S(1)}, f32[4,128,128]{1,2,0:T(8,128)}, u32[]{:S(2)}) copy-start(f32[4,128,128]{1,2,0:T(8,128)} %all-reduce.5.cloned.1.call-done) | copy-start | bytes 786436
  191.4 1.3 copy-start
  197.0 178.1 %all-reduce.9.cloned.1.call-start = ((), (), s32[]{:S(2)}) async-start(), calls=%async_computation.3 | async-start | bytes 524288 | tf_op jit(solution)/shard_map/psum | solution.py:51
  232.2 10.7 %copy-start.6 = (f32[4,128,128]{1,2,0:T(8,128)S(1)}, f32[4,128,128]{1,2,0:T(8,128)}, u32[]{:S(2)}) copy-start(f32[4,128,128]{1,2,0:T(8,128)} %all-reduce.7.cloned.1.call-done) | copy-start | bytes 786436
  375.1 10.3 %copy-start.5 = (f32[4,128,128]{1,2,0:T(8,128)S(1)}, f32[4,128,128]{1,2,0:T(8,128)}, u32[]{:S(2)}) copy-start(f32[4,128,128]{1,2,0:T(8,128)} %all-reduce.9.cloned.1.call-done) | copy-start | bytes 786436
  478.0 3.0 copy-start.1
  478.8 23.1 %collective-permute-start.1 = (f32[1024,64]{0,1:T(8,128)}, f32[1024,64]{0,1:T(8,128)}, u32[]{:S(2)}, u32[]{:S(2)}) collective-permute-start(f32[1024,64]{0,1:T(8,128)} %slice_bitcast_fusion), channel_id=1, source_target_pairs={{4,0},{8,4},{12,8},{16,12},{20,16},{24,20},{28,24},{5,1},{9,5},{13... | collective-permute-start | bytes 786440 | tf_op jit(solution)/shard_map/ppermute | solution.py:13
  481.1 20.9 %collective-permute-start = (f32[1024,64]{0,1:T(8,128)}, f32[1024,64]{0,1:T(8,128)}, u32[]{:S(2)}, u32[]{:S(2)}) collective-permute-start(f32[1024,64]{0,1:T(8,128)} %slice_bitcast_fusion.1), channel_id=1, source_target_pairs={{0,4},{4,8},{8,12},{12,16},{16,20},{20,24},{24,28},{1,5},{5,9},{9,... | collective-permute-start | bytes 786440 | tf_op jit(solution)/shard_map/ppermute | solution.py:13
  484.8 17.1 %copy-start.2 = (f32[4,1024,128]{1,2,0:T(8,128)S(1)}, f32[4,1024,128]{1,2,0:T(8,128)}, u32[]{:S(2)}) copy-start(f32[4,1024,128]{1,2,0:T(8,128)} %copy-done.1) | copy-start | bytes 6291460
Sparse Core Ops, SparseCore 0:
  55.1 34.7 all-reduce.4
  197.1 35.0 all-reduce.6
  340.0 35.0 all-reduce.8
where the time goes:
time: 518 us; the launch traced here: 513 us
  other arithmetic  267 us (52%)
  waiting for transfers between devices  132 us (25%)
  local copies, waits for them, and re-layouts  46.2 us (9%)
  matrix products  27.1 us (5%)
  between operations  16.8 us (3%)
  blocking collectives  13.8 us (3%)
  starting transfers between devices  10.5 us (2%)
    another operation x10, other arithmetic, cayley(): factor = jnp.linalg.cholesky(system)  142 us
    another operation x7, other arithmetic, cayley(): return jax.scipy.linalg.cho_solve((factor, True), product.T).T  119 us
    psum x3, waiting for transfers between devices, on_device(): pair_gram = lax.psum(partial_value, 'row')  105 us
    all_to_all x1, waiting for transfers between devices, on_device(): lax.all_to_all(arranged, 'pair', split_axis=1, concat_axis=0, tiled=True)  26.6 us
    psum x3, local copies, waits for them, and re-layouts, on_device(): pair_gram = lax.psum(partial_value, 'row')  25.7 us
    psum x1, blocking collectives, on_device(): totals = lax.psum((off_part, diag_part), 'pair')  13.8 us
    dot_general x3, matrix products, on_device(): jnp.einsum('pri,prj->pij', column, column, precision=lax.Precision.HIGHEST)  12.8 us
  transfers between devices with their start and end apart: 6, of which 4 were waited for; matrix products, arithmetic and copies ran while one was open for 1% of the time, Pallas kernels for 0%

commit v1 on v0

v1 whole, which is shorter than its diff:
```python
import functools

import jax
import jax.numpy as jnp
from jax import lax
from jax.experimental import pallas as pl
from jax.experimental.pallas import tpu as pltpu
from jax.sharding import PartitionSpec as P

BLOCK = 64
WIDTH = 2 * BLOCK
ITERS = 3
TOLERANCE = 1e-8
VMEM = pl.BlockSpec(memory_space=pltpu.VMEM)
SMEM = pl.BlockSpec(memory_space=pltpu.SMEM)
PARAMS = pltpu.CompilerParams(vmem_limit_bytes=48 * 1024 * 1024)


def split(value):
    high = value.astype(jnp.bfloat16)
    low = (value - high.astype(jnp.float32)).astype(jnp.bfloat16)
    return jnp.concatenate([high, low], axis=1)


def product(left, right):
    both = jnp.dot(left, jnp.concatenate([right, right], axis=0), preferred_element_type=jnp.float32)
    half = both.shape[1] // 2
    return both[:, :half] + both[:, half:]


def unit(size):
    row_ids = lax.broadcasted_iota(jnp.int32, (size, size), 0)
    col_ids = lax.broadcasted_iota(jnp.int32, (size, size), 1)
    return row_ids == col_ids


def total(value):
    return jnp.sum(jnp.sum(value, axis=1, keepdims=True), axis=0, keepdims=True)


def gather_kernel(slots, source, out):
    groups, rows, cols = out.shape
    pairs = cols // WIDTH
    low_lanes = lax.broadcasted_iota(jnp.int32, (rows, WIDTH), 1) < BLOCK

    def tile(block, lane_half):
        start = pl.multiple_of((block // 2) * WIDTH, WIDTH)
        value = source[:, pl.ds(start, WIDTH)]
        return jnp.where(block % 2 == lane_half, value, pltpu.roll(value, BLOCK, 1))

    def one_group(group, carry):
        for pair in range(pairs):
            slot = 2 * (group * pairs + pair)
            upper = tile(slots[slot], 0)
            lower = tile(slots[slot + 1], 1)
            out[group, :, pair * WIDTH : (pair + 1) * WIDTH] = jnp.where(low_lanes, upper, lower)
        return carry

    lax.fori_loop(0, groups, one_group, 0)


def gather(r_factor, block_slots, groups):
    rows, cols = r_factor.shape
    return pl.pallas_call(
        gather_kernel,
        out_shape=jax.ShapeDtypeStruct((groups, rows, cols // groups), jnp.float32),
        in_specs=[SMEM, VMEM],
        out_specs=VMEM,
        compiler_params=PARAMS,
        name="gather",
    )(block_slots, r_factor)


def gram_kernel(shift, column, out):
    pairs = out.shape[0]
    for pair in range(pairs):
        parts = split(column[:, pair * WIDTH : (pair + 1) * WIDTH])
        four = lax.dot_general(parts, parts, (((0,), (0,)), ((), ())), preferred_element_type=jnp.float32)
        half = four[:WIDTH] + four[WIDTH:]
        out[lax.rem(pair + shift[0], pairs)] = half[:, :WIDTH] + half[:, WIDTH:]


def grams(column, shift):
    pairs = column.shape[1] // WIDTH
    return pl.pallas_call(
        gram_kernel,
        out_shape=jax.ShapeDtypeStruct((pairs, WIDTH, WIDTH), jnp.float32),
        in_specs=[SMEM, VMEM],
        out_specs=VMEM,
        compiler_params=PARAMS,
        name="grams",
    )(shift, column)


def rotation(gram, on_diag, even, odd, power):
    diag_part = jnp.where(on_diag, gram, 0.0)
    across = jnp.sum(diag_part, axis=1, keepdims=True)
    down = jnp.sum(diag_part, axis=0, keepdims=True)
    skew = gram * (across - down) / (2.0 * (across * across + down * down))
    skew_parts = split(skew)
    square = product(skew_parts, skew_parts)
    bound = jnp.sqrt(0.5 * total(square * square))
    scale = 2.0 / (2.0 + bound)
    rate = bound / (2.0 + bound)
    diag_one = jnp.where(on_diag, 1.0, 0.0)
    rest = (1.0 - scale) * diag_one + scale * square
    rest_parts = split(rest)
    size = gram.shape[0]
    first = product(jnp.concatenate([skew_parts, rest_parts], axis=0), rest_parts)
    even_now = scale * (diag_one + rest)
    odd_now = scale * (skew + first[:size])
    rest_parts = split(first[size:])
    second = product(jnp.concatenate([split(even_now), split(odd_now), rest_parts], axis=0), rest_parts)
    even_now = even_now + second[:size]
    odd_now = odd_now + second[size : 2 * size]
    rest_parts = split(second[2 * size :])
    third = product(jnp.concatenate([split(even_now), split(odd_now)], axis=0), rest_parts)
    even[...] = even_now + third[:size]
    odd[...] = odd_now + third[size:]
    power[...] = rest_parts

    def more(left):
        return left > TOLERANCE

    def step(left):
        old = power[...]
        parts = split(product(old, old))
        power[...] = parts
        even[...] += product(split(even[...]), parts)
        odd[...] += product(split(odd[...]), parts)
        return left * left

    rate = rate * rate
    rate = rate * rate
    lax.while_loop(more, step, (rate * rate)[0, 0])
    even_now = 2.0 * even[...] - diag_one
    odd_now = 2.0 * odd[...]
    return split(even_now - odd_now), split(even_now + odd_now)


def solve_kernel(count, *refs):
    parts, out, sums, even, odd, power = refs[:count], *refs[count:]
    on_diag = unit(WIDTH)
    off_total = jnp.zeros((1, 1), jnp.float32)
    diag_total = jnp.zeros((1, 1), jnp.float32)
    for pair in range(out.shape[0]):
        gram = parts[0][pair]
        for part in parts[1:]:
            gram = gram + part[pair]
        squares = gram * gram
        off_total += total(jnp.where(on_diag, 0.0, squares))
        diag_total += total(jnp.where(on_diag, squares, 0.0))
        so_far = None
        for sweep in range(ITERS):
            turn, back = rotation(gram, on_diag, even, odd, power)
            if sweep < ITERS - 1:
                gram = product(back, split(product(split(gram), turn)))
            so_far = turn if so_far is None else split(product(so_far, turn))
        out[pair] = so_far[:, :WIDTH].astype(jnp.float32) + so_far[:, WIDTH:].astype(jnp.float32)
    first_lane = lax.broadcasted_iota(jnp.int32, sums.shape, 1) == 0
    sums[...] = jnp.where(first_lane, off_total, diag_total)


def solve(parts):
    pairs = parts[0].shape[0]
    return pl.pallas_call(
        functools.partial(solve_kernel, len(parts)),
        out_shape=(
            jax.ShapeDtypeStruct((pairs, WIDTH, WIDTH), jnp.float32),
            jax.ShapeDtypeStruct((8, 128), jnp.float32),
        ),
        in_specs=[VMEM] * len(parts),
        out_specs=(VMEM, VMEM),
        scratch_shapes=[
            pltpu.VMEM((WIDTH, WIDTH), jnp.float32),
            pltpu.VMEM((WIDTH, WIDTH), jnp.float32),
            pltpu.VMEM((WIDTH, 2 * WIDTH), jnp.bfloat16),
        ],
        compiler_params=PARAMS,
        name="solve",
    )(*parts)


def load_turns(where, turns, held):
    count = len(turns)
    each = turns[0].shape[0]
    for step in range(count):
        held[pl.ds(lax.rem(where[1] + count - step, count) * each, each)] = turns[step][...]


def edge_kernel(count, where, column, *refs):
    turns, up, down, held = refs[:count], *refs[count:]
    load_turns(where, turns, held)
    pairs = held.shape[0]
    rows = column.shape[0]
    half = rows // 2
    low_lanes = lax.broadcasted_iota(jnp.int32, (half, WIDTH), 1) < BLOCK
    last = product(split(column[:, (pairs - 1) * WIDTH :]), split(held[pairs - 1]))
    up[...] = jnp.where(low_lanes, last[:half], pltpu.roll(last[half:], BLOCK, 1))
    first = product(split(column[:, :WIDTH]), split(held[0]))
    down[...] = jnp.where(low_lanes, pltpu.roll(first[:half], BLOCK, 1), first[half:])


def edges(where, column, turns):
    rows = column.shape[0]
    pairs = column.shape[1] // WIDTH
    shape = jax.ShapeDtypeStruct((rows // 2, WIDTH), jnp.float32)
    return pl.pallas_call(
        functools.partial(edge_kernel, len(turns)),
        out_shape=(shape, shape),
        in_specs=[SMEM] + [VMEM] * (1 + len(turns)),
        out_specs=(VMEM, VMEM),
        scratch_shapes=[pltpu.VMEM((pairs, WIDTH, WIDTH), jnp.float32)],
        compiler_params=PARAMS,
        name="edges",
    )(where, column, *turns)


def place_kernel(count, where, column, came_up, came_down, *refs):
    turns, out, held = refs[:count], *refs[count:]
    load_turns(where, turns, held)
    pairs = held.shape[0]
    rows = column.shape[0]
    half = rows // 2
    is_first = where[0] == 0
    is_last = where[0] == where[2] - 1
    low_lanes = lax.broadcasted_iota(jnp.int32, (half, WIDTH), 1) < BLOCK
    rotated = []
    for pair in range(pairs):
        rotated.append(product(split(column[:, pair * WIDTH : (pair + 1) * WIDTH]), split(held[pair])))
    for part in range(2):
        span = slice(part * half, (part + 1) * half)
        for pair in range(pairs):
            if pair == 0:
                arrived = came_up[...] if part == 0 else pltpu.roll(came_up[...], BLOCK, 1)
                upper = jnp.where(is_first, rotated[0][span], arrived)
            else:
                upper = rotated[pair - 1][span]
                if pair == 1:
                    upper = jnp.where(is_first, pltpu.roll(upper, BLOCK, 1), upper)
            if pair == pairs - 1:
                arrived = came_down[...] if part == 1 else pltpu.roll(came_down[...], BLOCK, 1)
                lower = jnp.where(is_last, pltpu.roll(rotated[pair][span], BLOCK, 1), arrived)
            else:
                lower = rotated[pair + 1][span]
            out[span, pair * WIDTH : (pair + 1) * WIDTH] = jnp.where(low_lanes, upper, lower)


def place(where, column, came_up, came_down, turns):
    pairs = column.shape[1] // WIDTH
    return pl.pallas_call(
        functools.partial(place_kernel, len(turns)),
        out_shape=jax.ShapeDtypeStruct(column.shape, jnp.float32),
        in_specs=[SMEM] + [VMEM] * (3 + len(turns)),
        out_specs=VMEM,
        scratch_shapes=[pltpu.VMEM((pairs, WIDTH, WIDTH), jnp.float32)],
        compiler_params=PARAMS,
        name="place",
    )(where, column, came_up, came_down, *turns)


def passed_along(value, axis, by):
    count = lax.axis_size(axis)
    pairs = [(i, i + by) for i in range(count) if 0 <= i + by < count]
    return lax.ppermute(value, axis, pairs)


def passed_round(value, axis, by):
    count = lax.axis_size(axis)
    return lax.ppermute(value, axis, [(i, (i + by) % count) for i in range(count)])


def summed(value, axis):
    count = lax.axis_size(axis)
    if count & (count - 1):
        return lax.psum(value, axis)
    step = 1
    while step < count:
        value = value + lax.ppermute(value, axis, [(i, i ^ step) for i in range(count)])
        step *= 2
    return value


def on_device(r_factor, block_slots):
    pair_count = lax.axis_size("pair")
    row_count = lax.axis_size("row")
    pair_index = lax.axis_index("pair")
    row_index = lax.axis_index("row")
    arranged = gather(r_factor, block_slots, pair_count)
    received = lax.all_to_all(arranged, "pair", split_axis=0, concat_axis=0, tiled=True)
    column = received.reshape(-1, received.shape[2])
    local_pairs = column.shape[1] // WIDTH
    shared = local_pairs % row_count == 0
    if shared:
        each = local_pairs // row_count
        shift = (row_count - row_index) * each
    else:
        shift = jnp.zeros((), jnp.int32)
    partial_grams = grams(column, shift.astype(jnp.int32).reshape(1))
    if shared:
        parts = [partial_grams[:each]]
        for by in range(1, row_count):
            parts.append(passed_round(partial_grams[by * each : (by + 1) * each], "row", by))
        turn, sums = solve(parts)
        turns = [turn] + [passed_round(turn, "row", by) for by in range(1, row_count)]
        sums = summed(sums, "row")
    else:
        turn, sums = solve([lax.psum(partial_grams, "row")])
        turns = [turn]
    where = jnp.stack([pair_index, row_index if shared else jnp.zeros_like(row_index), jnp.int32(pair_count)]).astype(jnp.int32)
    up, down = edges(where, column, turns)
    came_up = passed_along(up, "pair", 1)
    came_down = passed_along(down, "pair", -1)
    rotated = place(where, column, came_up, came_down, turns)
    sums = summed(sums, "pair")
    off_ratio = jnp.sqrt(sums[0, 0] / sums[0, 1])
    return (rotated, off_ratio)


def solution(mesh):
    in_specs = (P(("row", "pair"), None), P())
    out_specs = (P("row", "pair"), P())
    return jax.shard_map(
        on_device, mesh=mesh, in_specs=in_specs, out_specs=out_specs, check_vma=False
    )
```

time: 518 us -> 90 us (0.17)
  other arithmetic: 267 us -> 0.09 us
  waiting for transfers between devices: 132 us -> 48.3 us
  local copies, waits for them, and re-layouts: 46.2 us -> 4.16 us
  matrix products: 27.1 us -> 0 us
  blocking collectives: 13.8 us -> 0 us
  between operations: 16.8 us -> 3.25 us
  starting transfers between devices: 10.5 us -> 23.2 us
  Pallas kernels: 0 us -> 10.8 us
    another operation x17 -> x1, other arithmetic: 261 us -> 0.08 us  [on_device(): jnp.stack([pair_index, row_index if shared else jnp.zeros_like(row_index)...]
    psum x3 -> x0, waiting for transfers between devices: 105 us -> none  [on_device(): pair_gram = lax.psum(partial_value, 'row')]
    psum x3 -> x0, local copies, waits for them, and re-layouts: 25.7 us -> none  [on_device(): pair_gram = lax.psum(partial_value, 'row')]
    dot_general x12 -> x0, matrix products: 24.1 us -> none  [the longest x3 12.8 us: on_device(): jnp.einsum('pri,prj->pij', column, column, precision=lax.Precision.HIGHEST)]
    ppermute x0 -> x11, waiting for transfers between devices: none -> 21.6 us  [the longest x5 12.3 us: summed(): lax.ppermute(value, axis, [(i, i ^ step) for i in range(count)])]
    ppermute x0 -> x11, starting transfers between devices: none -> 15.4 us  [the longest x6 7.87 us: passed_round(): lax.ppermute(value, axis, [(i, (i + by) % count) for i in range(count)])]
    psum x1 -> x0, blocking collectives: 13.8 us -> none  [on_device(): totals = lax.psum((off_part, diag_part), 'pair')]
    pallas_call x0 -> x5, Pallas kernels: none -> 10.8 us  [the longest x1 4.02 us: solve(): pl.pallas_call(functools.partial(solve_kernel, len(parts)), out_shape=(ja...]
  transfers between devices with their start and end apart: 6 -> 14, of which waited for: 4 -> 11; matrix products, arithmetic and copies ran while one was open for 1% -> 1% of each run, Pallas kernels for 0% -> 0%
where the time goes in v1:
time: 90 us; the launch traced here: 89.7 us
  waiting for transfers between devices  48.3 us (54%)
  starting transfers between devices  23.2 us (26%)
  Pallas kernels  10.8 us (12%)
  local copies, waits for them, and re-layouts  4.16 us (5%)
  between operations  3.25 us (4%)
    all_to_all x1, waiting for transfers between devices, on_device(): lax.all_to_all(arranged, 'pair', split_axis=0, concat_axis=0, tiled=True)  26.6 us
    ppermute x5, waiting for transfers between devices, summed(): lax.ppermute(value, axis, [(i, i ^ step) for i in range(count)])  12.3 us
    ppermute x6, waiting for transfers between devices, passed_round(): lax.ppermute(value, axis, [(i, (i + by) % count) for i in range(count)])  9.35 us
    ppermute x6, starting transfers between devices, passed_round(): lax.ppermute(value, axis, [(i, (i + by) % count) for i in range(count)])  7.87 us
    ppermute x5, starting transfers between devices, summed(): lax.ppermute(value, axis, [(i, i ^ step) for i in range(count)])  7.56 us
    all_to_all x1, starting transfers between devices, on_device(): lax.all_to_all(arranged, 'pair', split_axis=0, concat_axis=0, tiled=True)  5.17 us
    pallas_call x1, Pallas kernels, solve(): pl.pallas_call(functools.partial(solve_kernel, len(parts)), out_shape=(ja...  4.02 us
    unnamed x6, local copies, waits for them, and re-layouts  3.55 us
  transfers between devices with their start and end apart: 14, of which 11 were waited for; matrix products, arithmetic and copies ran while one was open for 1% of the time, Pallas kernels for 0%

profile of v1, /device:TPU:0, one launch (start us, length us, event | category | flops | bytes accessed | tf_op | source)
XLA Modules:
  0.0 89.7 jit_solution(6518173740321124404)
XLA Ops:
  0.6 0.0 copy-start.1
  0.6 1.6 %copy-done.1 = f32[128,4096]{1,0:T(8,128)S(1)} copy-done((f32[128,4096]{1,0:T(8,128)S(1)}, f32[128,4096]{1,0:T(8,128)}, u32[]{:S(2)}) %copy-start.1) | copy-done | bytes 2097176
  2.2 0.0 copy-start.2
  2.2 0.7 copy-done.2
  2.9 2.2 %gather.1 = f32[8,128,512]{2,1,0:T(8,128)S(1)} custom-call(s32[64]{0:T(128)S(1)} %copy-done.2, f32[128,4096]{1,0:T(8,128)S(1)} %copy-done.1), custom_call_target="tpu_custom_call" | custom-call | tf_op jit(solution)/shard_map/gather/pallas_call | solution.py:64
  5.1 0.0 copy-start
  5.1 1.3 %copy-done = f32[8,128,512]{2,1,0:T(8,128)} copy-done((f32[8,128,512]{2,1,0:T(8,128)}, f32[8,128,512]{2,1,0:T(8,128)S(1)}, u32[]{:S(2)}) %copy-start) | copy-done | bytes 2097176
  6.4 5.2 %all-to-all-start = ((f32[8,128,512]{2,1,0:T(8,128)}), f32[8,128,512]{2,1,0:T(8,128)S(1)}, u32[]{:S(2)}, u32[]{:S(2)}) async-start(f32[8,128,512]{2,1,0:T(8,128)} %copy-done), calls=%async_computation | async-start | bytes 4194304 | tf_op jit(solution)/shard_map/all_to_all | solution.py:290
  11.6 26.6 %all-to-all-done = f32[8,128,512]{2,1,0:T(8,128)S(1)} async-done(((f32[8,128,512]{2,1,0:T(8,128)}), f32[8,128,512]{2,1,0:T(8,128)S(1)}, u32[]{:S(2)}, u32[]{:S(2)}) %all-to-all-start) | async-done | bytes 2097184 | tf_op jit(solution)/shard_map/all_to_all | solution.py:290
  38.3 0.7 grams.1
  39.0 3.7 %collective-permute-start.2 = (f32[1,128,128]{2,1,0:T(8,128)S(1)}, f32[1,128,128]{2,1,0:T(8,128)S(1)}, u32[]{:S(2)}, u32[]{:S(2)}) collective-permute-start(f32[1,128,128]{2,1,0:T(8,128)S(1)} %get-tuple-element.10), channel_id=1, source_target_pairs={{0,3},{1,0},{2,1},{3,2},{4,7},{5,4},{6,5},{7,6},{8,11},{9,8},{10,9... | collective-permute-start | bytes 196616 | tf_op jit(solution)/shard_map/ppermute | solution.py:270
  42.7 0.0 collective-permute-start.1
  42.7 1.0 %collective-permute-start = (f32[1,128,128]{2,1,0:T(8,128)S(1)}, f32[1,128,128]{2,1,0:T(8,128)S(1)}, u32[]{:S(2)}, u32[]{:S(2)}) collective-permute-start(f32[1,128,128]{2,1,0:T(8,128)S(1)} %get-tuple-element.12), channel_id=1, source_target_pairs={{0,1},{1,2},{2,3},{3,0},{4,5},{5,6},{6,7},{7,4},{8,9},{9,10},{10,1... | collective-permute-start | bytes 196616 | tf_op jit(solution)/shard_map/ppermute | solution.py:270
  43.7 1.1 %collective-permute-done.2.refs_3_ = f32[1,128,128]{2,1,0:T(8,128)S(1)} collective-permute-done((f32[1,128,128]{2,1,0:T(8,128)S(1)}, f32[1,128,128]{2,1,0:T(8,128)S(1)}, u32[]{:S(2)}, u32[]{:S(2)}) %collective-permute-start.2) | collective-permute-done | bytes 65568 | tf_op jit(solution)/shard_map/ppermute | solution.py:270
  44.8 3.1 %collective-permute-done.1.refs_2_ = f32[1,128,128]{2,1,0:T(8,128)S(1)} collective-permute-done((f32[1,128,128]{2,1,0:T(8,128)S(1)}, f32[1,128,128]{2,1,0:T(8,128)S(1)}, u32[]{:S(2)}, u32[]{:S(2)}) %collective-permute-start.1) | collective-permute-done | bytes 65568 | tf_op jit(solution)/shard_map/ppermute | solution.py:270
  47.9 0.9 %collective-permute-done.refs_1_ = f32[1,128,128]{2,1,0:T(8,128)S(1)} collective-permute-done((f32[1,128,128]{2,1,0:T(8,128)S(1)}, f32[1,128,128]{2,1,0:T(8,128)S(1)}, u32[]{:S(2)}, u32[]{:S(2)}) %collective-permute-start) | collective-permute-done | bytes 65568 | tf_op jit(solution)/shard_map/ppermute | solution.py:270
  48.8 4.0 %solve.1 = (f32[1,128,128]{2,1,0:T(8,128)S(1)}, f32[8,128]{1,0:T(8,128)S(1)}) custom-call(f32[1,128,128]{2,1,0:T(8,128)S(1)} %get-tuple-element.13.refs_0_, f32[1,128,128]{2,1,0:T(8,128)S(1)} %collective-permute-done.refs_1_, f32[1,128,128]{2,1,0:T(8,128)S(1)} %collective-permute-done.1.refs_2_, f32[1,128,128]{2,1,0:T(8,128)S(1)} %collective-permute-done.2.refs_3_), custom_call_target="tpu_custom_call" | custom-call | tf_op jit(solution)/shard_map/solve/pallas_call | solution.py:166
  52.8 1.0 %collective-permute-start.5 = (f32[1,128,128]{2,1,0:T(8,128)S(1)}, f32[1,128,128]{2,1,0:T(8,128)S(1)}, u32[]{:S(2)}, u32[]{:S(2)}) collective-permute-start(f32[1,128,128]{2,1,0:T(8,128)S(1)} %get-tuple-element.6.refs_0_), channel_id=1, source_target_pairs={{0,3},{1,0},{2,1},{3,2},{4,7},{5,4},{6,5},{7,6},{8,11},{9,8},{10,9... | collective-permute-start | bytes 196616 | tf_op jit(solution)/shard_map/ppermute | solution.py:270
  53.8 0.3 collective-permute-start.4
  54.0 1.9 %collective-permute-start.3 = (f32[1,128,128]{2,1,0:T(8,128)S(1)}, f32[1,128,128]{2,1,0:T(8,128)S(1)}, u32[]{:S(2)}, u32[]{:S(2)}) collective-permute-start(f32[1,128,128]{2,1,0:T(8,128)S(1)} %get-tuple-element.6.refs_0_), channel_id=1, source_target_pairs={{0,1},{1,2},{2,3},{3,0},{4,5},{5,6},{6,7},{7,4},{8,9},{9,10},{10,1... | collective-permute-start | bytes 196616 | tf_op jit(solution)/shard_map/ppermute | solution.py:270
  56.0 0.1 pad_add_fusion.where
  56.1 1.0 %collective-permute-done.5.refs_3_ = f32[1,128,128]{2,1,0:T(8,128)S(1)} collective-permute-done((f32[1,128,128]{2,1,0:T(8,128)S(1)}, f32[1,128,128]{2,1,0:T(8,128)S(1)}, u32[]{:S(2)}, u32[]{:S(2)}) %collective-permute-start.5) | collective-permute-done | bytes 65568 | tf_op jit(solution)/shard_map/ppermute | solution.py:270
  57.1 3.3 %collective-permute-done.4.refs_2_ = f32[1,128,128]{2,1,0:T(8,128)S(1)} collective-permute-done((f32[1,128,128]{2,1,0:T(8,128)S(1)}, f32[1,128,128]{2,1,0:T(8,128)S(1)}, u32[]{:S(2)}, u32[]{:S(2)}) %collective-permute-start.4) | collective-permute-done | bytes 65568 | tf_op jit(solution)/shard_map/ppermute | solution.py:270
  60.4 0.0 collective-permute-done.3.refs_1_
  60.4 1.1 %edges.1 = (f32[512,128]{1,0:T(8,128)S(1)}, f32[512,128]{1,0:T(8,128)S(1)}) custom-call(s32[3]{0:T(128)S(1)} %pad_add_fusion.where, f32[1024,512]{1,0:T(8,128)S(1)} %bitcast.6, f32[1,128,128]{2,1,0:T(8,128)S(1)} %get-tuple-element.6.refs_0_, f32[1,128,128]{2,1,0:T(8,128)S(1)} %collective-permute-done.3.refs_1_, ...), custom_call_target="tpu_custom_call" | custom-call | tf_op jit(solution)/shard_map/edges/pallas_call | solution.py:208
  61.5 1.3 %collective-permute-start.6 = (f32[512,128]{1,0:T(8,128)S(1)}, f32[512,128]{1,0:T(8,128)S(1)}, u32[]{:S(2)}, u32[]{:S(2)}) collective-permute-start(f32[512,128]{1,0:T(8,128)S(1)} %get-tuple-element.7), channel_id=1, source_target_pairs={{0,4},{4,8},{8,12},{12,16},{16,20},{20,24},{24,28},{1,5},{5,9},{9,... | collective-permute-start | bytes 786440 | tf_op jit(solution)/shard_map/ppermute | solution.py:265
  62.8 1.3 %collective-permute-start.7 = (f32[512,128]{1,0:T(8,128)S(1)}, f32[512,128]{1,0:T(8,128)S(1)}, u32[]{:S(2)}, u32[]{:S(2)}) collective-permute-start(f32[512,128]{1,0:T(8,128)S(1)} %get-tuple-element.8), channel_id=1, source_target_pairs={{4,0},{8,4},{12,8},{16,12},{20,16},{24,20},{28,24},{5,1},{9,5},{13... | collective-permute-start | bytes 786440 | tf_op jit(solution)/shard_map/ppermute | solution.py:265
  64.1 0.1 collective-permute-start.8
  64.1 3.6 %collective-permute-done.8 = f32[8,128]{1,0:T(8,128)S(1)} collective-permute-done((f32[8,128]{1,0:T(8,128)S(1)}, f32[8,128]{1,0:T(8,128)S(1)}, u32[]{:S(2)}, u32[]{:S(2)}) %collective-permute-start.8) | collective-permute-done | bytes 4128 | tf_op jit(solution)/shard_map/ppermute | solution.py:279
  67.7 0.7 collective-permute-start.9
  68.4 3.8 %collective-permute-done.9 = f32[8,128]{1,0:T(8,128)S(1)} collective-permute-done((f32[8,128]{1,0:T(8,128)S(1)}, f32[8,128]{1,0:T(8,128)S(1)}, u32[]{:S(2)}, u32[]{:S(2)}) %collective-permute-start.9) | collective-permute-done | bytes 4128 | tf_op jit(solution)/shard_map/ppermute | solution.py:279
  72.3 1.4 %collective-permute-start.10 = (f32[8,128]{1,0:T(8,128)S(1)}, f32[8,128]{1,0:T(8,128)S(1)}, u32[]{:S(2)}, u32[]{:S(2)}) collective-permute-start(f32[8,128]{1,0:T(8,128)S(1)} %add.16), channel_id=1, source_target_pairs={{0,4},{4,0},{8,12},{12,8},{16,20},{20,16},{24,28},{28,24},{1,5},{5... | collective-permute-start | bytes 12296 | tf_op jit(solution)/shard_map/ppermute | solution.py:279
  73.6 0.8 collective-permute-done.10
  74.5 4.3 %collective-permute-start.11 = (f32[8,128]{1,0:T(8,128)S(1)}, f32[8,128]{1,0:T(8,128)S(1)}, u32[]{:S(2)}, u32[]{:S(2)}) collective-permute-start(f32[8,128]{1,0:T(8,128)S(1)} %add.17), channel_id=1, source_target_pairs={{0,8},{4,12},{8,0},{12,4},{16,24},{20,28},{24,16},{28,20},{1,9},{5... | collective-permute-start | bytes 12296 | tf_op jit(solution)/shard_map/ppermute | solution.py:279
  78.7 1.6 %collective-permute-done.11 = f32[8,128]{1,0:T(8,128)S(1)} collective-permute-done((f32[8,128]{1,0:T(8,128)S(1)}, f32[8,128]{1,0:T(8,128)S(1)}, u32[]{:S(2)}, u32[]{:S(2)}) %collective-permute-start.11) | collective-permute-done | bytes 4128 | tf_op jit(solution)/shard_map/ppermute | solution.py:279
  80.3 1.1 %collective-permute-start.12 = (f32[8,128]{1,0:T(8,128)S(1)}, f32[8,128]{1,0:T(8,128)S(1)}, u32[]{:S(2)}, u32[]{:S(2)}) collective-permute-start(f32[8,128]{1,0:T(8,128)S(1)} %add.18), channel_id=1, source_target_pairs={{0,16},{4,20},{8,24},{12,28},{16,0},{20,4},{24,8},{28,12},{1,17},{... | collective-permute-start | bytes 12296 | tf_op jit(solution)/shard_map/ppermute | solution.py:279
  81.5 2.5 %collective-permute-done.12 = f32[8,128]{1,0:T(8,128)S(1)} collective-permute-done((f32[8,128]{1,0:T(8,128)S(1)}, f32[8,128]{1,0:T(8,128)S(1)}, u32[]{:S(2)}, u32[]{:S(2)}) %collective-permute-start.12) | collective-permute-done | bytes 4128 | tf_op jit(solution)/shard_map/ppermute | solution.py:279
  83.9 0.6 fusion.1
  85.9 0.0 collective-permute-done.6.came_up
  85.9 0.0 collective-permute-done.7.came_down
  85.9 2.7 %place.1 = f32[1024,512]{1,0:T(8,128)} custom-call(s32[3]{0:T(128)S(1)} %pad_add_fusion.where, f32[1024,512]{1,0:T(8,128)S(1)} %bitcast.7, f32[512,128]{1,0:T(8,128)S(1)} %collective-permute-done.6.came_up, f32[512,128]{1,0:T(8,128)S(1)} %collective-permute-done.7.came_down, f32[1,128,128]{2,1,0:T(8,128)S(1)} %get-tuple-element.6.refs_0_, ...), custom_call_target="tpu_custom_call" | custom-call | tf_op jit(solution)/shard_map/place/pallas_call | solution.py:251
  (6 shorter events, 0.0 us)
Async XLA Ops:
  0.6 1.6 %copy-start.1 = (f32[128,4096]{1,0:T(8,128)S(1)}, f32[128,4096]{1,0:T(8,128)}, u32[]{:S(2)}) copy-start(f32[128,4096]{1,0:T(8,128)} %source.1) | copy-start | bytes 6291460
  2.2 0.7 copy-start.2
  5.1 1.3 %copy-start = (f32[8,128,512]{2,1,0:T(8,128)}, f32[8,128,512]{2,1,0:T(8,128)S(1)}, u32[]{:S(2)}) copy-start(f32[8,128,512]{2,1,0:T(8,128)S(1)} %gather.1) | copy-start | bytes 6291460
  6.4 31.8 %all-to-all-start = ((f32[8,128,512]{2,1,0:T(8,128)}), f32[8,128,512]{2,1,0:T(8,128)S(1)}, u32[]{:S(2)}, u32[]{:S(2)}) async-start(f32[8,128,512]{2,1,0:T(8,128)} %copy-done), calls=%async_computation | async-start | bytes 4194304 | tf_op jit(solution)/shard_map/all_to_all | solution.py:290
  39.0 5.7 %collective-permute-start.2 = (f32[1,128,128]{2,1,0:T(8,128)S(1)}, f32[1,128,128]{2,1,0:T(8,128)S(1)}, u32[]{:S(2)}, u32[]{:S(2)}) collective-permute-start(f32[1,128,128]{2,1,0:T(8,128)S(1)} %get-tuple-element.10), channel_id=1, source_target_pairs={{0,3},{1,0},{2,1},{3,2},{4,7},{5,4},{6,5},{7,6},{8,11},{9,8},{10,9... | collective-permute-start | bytes 196616 | tf_op jit(solution)/shard_map/ppermute | solution.py:270
  42.7 5.2 %collective-permute-start.1 = (f32[1,128,128]{2,1,0:T(8,128)S(1)}, f32[1,128,128]{2,1,0:T(8,128)S(1)}, u32[]{:S(2)}, u32[]{:S(2)}) collective-permute-start(f32[1,128,128]{2,1,0:T(8,128)S(1)} %get-tuple-element.11), channel_id=1, source_target_pairs={{0,2},{1,3},{2,0},{3,1},{4,6},{5,7},{6,4},{7,5},{8,10},{9,11},{10,... | collective-permute-start | bytes 196616 | tf_op jit(solution)/shard_map/ppermute | solution.py:270
  42.7 6.1 %collective-permute-start = (f32[1,128,128]{2,1,0:T(8,128)S(1)}, f32[1,128,128]{2,1,0:T(8,128)S(1)}, u32[]{:S(2)}, u32[]{:S(2)}) collective-permute-start(f32[1,128,128]{2,1,0:T(8,128)S(1)} %get-tuple-element.12), channel_id=1, source_target_pairs={{0,1},{1,2},{2,3},{3,0},{4,5},{5,6},{6,7},{7,4},{8,9},{9,10},{10,1... | collective-permute-start | bytes 196616 | tf_op jit(solution)/shard_map/ppermute | solution.py:270
  52.8 4.3 %collective-permute-start.5 = (f32[1,128,128]{2,1,0:T(8,128)S(1)}, f32[1,128,128]{2,1,0:T(8,128)S(1)}, u32[]{:S(2)}, u32[]{:S(2)}) collective-permute-start(f32[1,128,128]{2,1,0:T(8,128)S(1)} %get-tuple-element.6.refs_0_), channel_id=1, source_target_pairs={{0,3},{1,0},{2,1},{3,2},{4,7},{5,4},{6,5},{7,6},{8,11},{9,8},{10,9... | collective-permute-start | bytes 196616 | tf_op jit(solution)/shard_map/ppermute | solution.py:270
  53.8 6.6 %collective-permute-start.4 = (f32[1,128,128]{2,1,0:T(8,128)S(1)}, f32[1,128,128]{2,1,0:T(8,128)S(1)}, u32[]{:S(2)}, u32[]{:S(2)}) collective-permute-start(f32[1,128,128]{2,1,0:T(8,128)S(1)} %get-tuple-element.6.refs_0_), channel_id=1, source_target_pairs={{0,2},{1,3},{2,0},{3,1},{4,6},{5,7},{6,4},{7,5},{8,10},{9,11},{10,... | collective-permute-start | bytes 196616 | tf_op jit(solution)/shard_map/ppermute | solution.py:270
  54.0 6.3 %collective-permute-start.3 = (f32[1,128,128]{2,1,0:T(8,128)S(1)}, f32[1,128,128]{2,1,0:T(8,128)S(1)}, u32[]{:S(2)}, u32[]{:S(2)}) collective-permute-start(f32[1,128,128]{2,1,0:T(8,128)S(1)} %get-tuple-element.6.refs_0_), channel_id=1, source_target_pairs={{0,1},{1,2},{2,3},{3,0},{4,5},{5,6},{6,7},{7,4},{8,9},{9,10},{10,1... | collective-permute-start | bytes 196616 | tf_op jit(solution)/shard_map/ppermute | solution.py:270
  61.5 24.4 %collective-permute-start.6 = (f32[512,128]{1,0:T(8,128)S(1)}, f32[512,128]{1,0:T(8,128)S(1)}, u32[]{:S(2)}, u32[]{:S(2)}) collective-permute-start(f32[512,128]{1,0:T(8,128)S(1)} %get-tuple-element.7), channel_id=1, source_target_pairs={{0,4},{4,8},{8,12},{12,16},{16,20},{20,24},{24,28},{1,5},{5,9},{9,... | collective-permute-start | bytes 786440 | tf_op jit(solution)/shard_map/ppermute | solution.py:265
  62.8 23.1 %collective-permute-start.7 = (f32[512,128]{1,0:T(8,128)S(1)}, f32[512,128]{1,0:T(8,128)S(1)}, u32[]{:S(2)}, u32[]{:S(2)}) collective-permute-start(f32[512,128]{1,0:T(8,128)S(1)} %get-tuple-element.8), channel_id=1, source_target_pairs={{4,0},{8,4},{12,8},{16,12},{20,16},{24,20},{28,24},{5,1},{9,5},{13... | collective-permute-start | bytes 786440 | tf_op jit(solution)/shard_map/ppermute | solution.py:265
  64.1 3.7 %collective-permute-start.8 = (f32[8,128]{1,0:T(8,128)S(1)}, f32[8,128]{1,0:T(8,128)S(1)}, u32[]{:S(2)}, u32[]{:S(2)}) collective-permute-start(f32[8,128]{1,0:T(8,128)S(1)} %get-tuple-element.9), channel_id=1, source_target_pairs={{0,1},{1,0},{2,3},{3,2},{4,5},{5,4},{6,7},{7,6},{8,9},{9,8},{10,11... | collective-permute-start | bytes 12296 | tf_op jit(solution)/shard_map/ppermute | solution.py:279
  67.7 4.5 %collective-permute-start.9 = (f32[8,128]{1,0:T(8,128)S(1)}, f32[8,128]{1,0:T(8,128)S(1)}, u32[]{:S(2)}, u32[]{:S(2)}) collective-permute-start(f32[8,128]{1,0:T(8,128)S(1)} %add.15), channel_id=1, source_target_pairs={{0,2},{1,3},{2,0},{3,1},{4,6},{5,7},{6,4},{7,5},{8,10},{9,11},{10,... | collective-permute-start | bytes 12296 | tf_op jit(solution)/shard_map/ppermute | solution.py:279
  72.3 2.2 %collective-permute-start.10 = (f32[8,128]{1,0:T(8,128)S(1)}, f32[8,128]{1,0:T(8,128)S(1)}, u32[]{:S(2)}, u32[]{:S(2)}) collective-permute-start(f32[8,128]{1,0:T(8,128)S(1)} %add.16), channel_id=1, source_target_pairs={{0,4},{4,0},{8,12},{12,8},{16,20},{20,16},{24,28},{28,24},{1,5},{5... | collective-permute-start | bytes 12296 | tf_op jit(solution)/shard_map/ppermute | solution.py:279
  74.5 5.8 %collective-permute-start.11 = (f32[8,128]{1,0:T(8,128)S(1)}, f32[8,128]{1,0:T(8,128)S(1)}, u32[]{:S(2)}, u32[]{:S(2)}) collective-permute-start(f32[8,128]{1,0:T(8,128)S(1)} %add.17), channel_id=1, source_target_pairs={{0,8},{4,12},{8,0},{12,4},{16,24},{20,28},{24,16},{28,20},{1,9},{5... | collective-permute-start | bytes 12296 | tf_op jit(solution)/shard_map/ppermute | solution.py:279
  80.3 3.6 %collective-permute-start.12 = (f32[8,128]{1,0:T(8,128)S(1)}, f32[8,128]{1,0:T(8,128)S(1)}, u32[]{:S(2)}, u32[]{:S(2)}) collective-permute-start(f32[8,128]{1,0:T(8,128)S(1)} %add.18), channel_id=1, source_target_pairs={{0,16},{4,20},{8,24},{12,28},{16,0},{20,4},{24,8},{28,12},{1,17},{... | collective-permute-start | bytes 12296 | tf_op jit(solution)/shard_map/ppermute | solution.py:279

commit v2 on v1

v2 whole, which is shorter than its diff:
```python
import functools

import jax
import jax.numpy as jnp
from jax import lax
from jax.experimental import pallas as pl
from jax.experimental.pallas import tpu as pltpu
from jax.sharding import PartitionSpec as P

BLOCK = 64
WIDTH = 2 * BLOCK
ITERS = 3
TOLERANCE = 1e-8
LAST_ROWS = 8
VMEM = pl.BlockSpec(memory_space=pltpu.VMEM)
SMEM = pl.BlockSpec(memory_space=pltpu.SMEM)
PARAMS = pltpu.CompilerParams(vmem_limit_bytes=48 * 1024 * 1024)


def split(value):
    high = value.astype(jnp.bfloat16)
    low = (value - high.astype(jnp.float32)).astype(jnp.bfloat16)
    return jnp.concatenate([high, low], axis=1)


def product(left, right):
    both = jnp.dot(left, jnp.concatenate([right, right], axis=0), preferred_element_type=jnp.float32)
    half = both.shape[1] // 2
    return both[:, :half] + both[:, half:]


def unit(size):
    row_ids = lax.broadcasted_iota(jnp.int32, (size, size), 0)
    col_ids = lax.broadcasted_iota(jnp.int32, (size, size), 1)
    return row_ids == col_ids


def total(value):
    return jnp.sum(jnp.sum(value, axis=1, keepdims=True), axis=0, keepdims=True)


def gather_kernel(plan, slots, base, source, *outs):
    rows = source.shape[0]
    local = plan[0][0]
    low_lanes = lax.broadcasted_iota(jnp.int32, (rows, WIDTH), 1) < BLOCK

    def tile(block, lane_half):
        start = pl.multiple_of((block // 2) * WIDTH, WIDTH)
        value = source[:, pl.ds(start, WIDTH)]
        return jnp.where(block % 2 == lane_half, value, pltpu.roll(value, BLOCK, 1))

    for (_, first, positions), out in zip(plan, outs):
        count = out.shape[2] // WIDTH

        def one(group, place, first=first, count=count, out=out):
            for pair in range(count):
                slot = 2 * (group * local + first + pair)
                upper = tile(slots[slot], 0)
                lower = tile(slots[slot + 1], 1)
                out[place, :, pair * WIDTH : (pair + 1) * WIDTH] = jnp.where(low_lanes, upper, lower)

        if positions is None:

            def step(group, carry, one=one):
                one(group, group)
                return carry

            lax.fori_loop(0, out.shape[0], step, 0)
        else:
            for place, position in enumerate(positions):
                one(jnp.bitwise_xor(base[0], position), place)


def gather(r_factor, block_slots, base, plan):
    rows = r_factor.shape[0]
    groups = r_factor.shape[1] // WIDTH // plan[0][0]
    shapes = []
    for _, _, taken, positions in plan:
        count = groups if positions is None else len(positions)
        shapes.append(jax.ShapeDtypeStruct((count, rows, taken * WIDTH), jnp.float32))
    return pl.pallas_call(
        functools.partial(gather_kernel, tuple((local, first, positions) for local, first, _, positions in plan)),
        out_shape=tuple(shapes),
        in_specs=[SMEM, SMEM, VMEM],
        out_specs=(VMEM,) * len(shapes),
        compiler_params=PARAMS,
        name="gather",
    )(block_slots, base, r_factor)


def gram(pieces):
    parts = split(jnp.concatenate(pieces, axis=0))
    four = lax.dot_general(parts, parts, (((0,), (0,)), ((), ())), preferred_element_type=jnp.float32)
    half = four[:WIDTH] + four[WIDTH:]
    return half[:, :WIDTH] + half[:, WIDTH:]


def piece(refs, where, pair):
    operand, place = where
    return refs[operand][place, :, pair * WIDTH : (pair + 1) * WIDTH]


def deal(row, held, outs):
    each = outs[0].shape[0]
    for by, out in enumerate(outs):
        out[...] = held[pl.ds(jnp.bitwise_xor(row, by) * each, each)]


def grams_kernel(row, column, *refs):
    outs, held = refs[:-1], refs[-1]
    groups = column.shape[0]
    for pair in range(held.shape[0]):
        held[pair] = gram([piece([column], (0, group), pair) for group in range(groups)])
    deal(row[0], held, outs)


def grams(row, column, shares):
    pairs = column.shape[2] // WIDTH
    return pl.pallas_call(
        grams_kernel,
        out_shape=(jax.ShapeDtypeStruct((pairs // shares, WIDTH, WIDTH), jnp.float32),) * shares,
        in_specs=[SMEM, VMEM],
        out_specs=(VMEM,) * shares,
        scratch_shapes=[pltpu.VMEM((pairs, WIDTH, WIDTH), jnp.float32)],
        compiler_params=PARAMS,
        name="grams",
    )(row, column)


def pack(gram_matrix):
    half = WIDTH // 2
    top = gram_matrix[:half]
    last = pltpu.roll(gram_matrix[half:], half, 1)
    row_ids = lax.broadcasted_iota(jnp.int32, (half, WIDTH), 0)
    col_ids = lax.broadcasted_iota(jnp.int32, (half, WIDTH), 1)
    ends = jnp.sum(jnp.where(row_ids == col_ids, last, 0.0), axis=0, keepdims=True)
    both = jnp.where((col_ids < half) & (row_ids > col_ids), last, top)
    return jnp.concatenate([both, jnp.broadcast_to(ends, (LAST_ROWS, WIDTH))], axis=0)


def unpack(packed):
    half = WIDTH // 2
    both = packed[:half]
    ends = packed[half : half + 1]
    mirrored = jnp.transpose(jnp.concatenate([both, both], axis=0))
    row_ids = lax.broadcasted_iota(jnp.int32, (half, WIDTH), 0)
    col_ids = lax.broadcasted_iota(jnp.int32, (half, WIDTH), 1)
    top = jnp.where((col_ids < half) & (row_ids > col_ids), mirrored[:half], both)
    last = jnp.where(row_ids > col_ids, both, mirrored[:half])
    last = jnp.where(row_ids == col_ids, ends, last)
    bottom = jnp.where(col_ids < half, mirrored[half:], pltpu.roll(last, half, 1))
    return jnp.concatenate([top, bottom], axis=0)


PACKED = WIDTH // 2 + LAST_ROWS


def near_grams_kernel(*refs):
    count = len(refs) // 3
    for place in range(count):
        here, near, out = refs[place], refs[count + place], refs[2 * count + place]
        for pair in range(out.shape[0]):
            out[pair] = pack(gram([piece([ref], (0, 0), pair) for ref in (here, near)]))


def near_grams(here, near):
    pairs = here[0].shape[2] // WIDTH
    return pl.pallas_call(
        near_grams_kernel,
        out_shape=(jax.ShapeDtypeStruct((pairs, PACKED, WIDTH), jnp.float32),) * len(here),
        in_specs=[VMEM] * (2 * len(here)),
        out_specs=(VMEM,) * len(here),
        compiler_params=PARAMS,
        name="near_grams",
    )(*here, *near)


def joined_kernel(*refs):
    half = len(refs) // 3
    for side in range(half):
        for place in range(2):
            refs[2 * half + side][place] = refs[2 * side + place][0]


def joined(*sides):
    _, rows, cols = sides[0][0].shape
    return pl.pallas_call(
        joined_kernel,
        out_shape=(jax.ShapeDtypeStruct((2, rows, cols), jnp.float32),) * len(sides),
        in_specs=[VMEM] * (2 * len(sides)),
        out_specs=(VMEM,) * len(sides),
        compiler_params=PARAMS,
        name="joined",
    )(*[value for side in sides for value in side])


def merge_kernel(count, row, *refs):
    parts, outs, held = refs[:count], refs[count:-1], refs[-1]
    value = parts[0][...]
    for part in parts[1:]:
        value = value + part[...]
    held[...] = value
    deal(row[0], held, outs)


def merge(row, parts, shares):
    pairs, height, _ = parts[0].shape
    return pl.pallas_call(
        functools.partial(merge_kernel, len(parts)),
        out_shape=(jax.ShapeDtypeStruct((pairs // shares, height, WIDTH), jnp.float32),) * shares,
        in_specs=[SMEM] + [VMEM] * len(parts),
        out_specs=(VMEM,) * shares,
        scratch_shapes=[pltpu.VMEM((pairs, height, WIDTH), jnp.float32)],
        compiler_params=PARAMS,
        name="merge",
    )(row, *parts)


def rotation(gram, on_diag, even, odd, power):
    diag_part = jnp.where(on_diag, gram, 0.0)
    across = jnp.sum(diag_part, axis=1, keepdims=True)
    down = jnp.sum(diag_part, axis=0, keepdims=True)
    skew = gram * (across - down) / (2.0 * (across * across + down * down))
    skew_parts = split(skew)
    square = product(skew_parts, skew_parts)
    bound = jnp.sqrt(0.5 * total(square * square))
    scale = 2.0 / (2.0 + bound)
    rate = bound / (2.0 + bound)
    diag_one = jnp.where(on_diag, 1.0, 0.0)
    rest = (1.0 - scale) * diag_one + scale * square
    rest_parts = split(rest)
    size = gram.shape[0]
    first = product(jnp.concatenate([skew_parts, rest_parts], axis=0), rest_parts)
    even_now = scale * (diag_one + rest)
    odd_now = scale * (skew + first[:size])
    rest_parts = split(first[size:])
    second = product(jnp.concatenate([split(even_now), split(odd_now), rest_parts], axis=0), rest_parts)
    even_now = even_now + second[:size]
    odd_now = odd_now + second[size : 2 * size]
    rest_parts = split(second[2 * size :])
    third = product(jnp.concatenate([split(even_now), split(odd_now)], axis=0), rest_parts)
    even[...] = even_now + third[:size]
    odd[...] = odd_now + third[size:]
    power[...] = rest_parts

    def more(left):
        return left > TOLERANCE

    def step(left):
        old = power[...]
        parts = split(product(old, old))
        power[...] = parts
        even[...] += product(split(even[...]), parts)
        odd[...] += product(split(odd[...]), parts)
        return left * left

    rate = rate * rate
    rate = rate * rate
    lax.while_loop(more, step, (rate * rate)[0, 0])
    even_now = 2.0 * even[...] - diag_one
    odd_now = 2.0 * odd[...]
    return split(even_now - odd_now), split(even_now + odd_now)


def solve_kernel(count, *refs):
    parts, out, even, odd, power = refs[:count], *refs[count:]
    on_diag = unit(WIDTH)
    off_total = jnp.zeros((1, 1), jnp.float32)
    diag_total = jnp.zeros((1, 1), jnp.float32)
    for pair in range(parts[0].shape[0]):
        gram = parts[0][pair]
        for part in parts[1:]:
            gram = gram + part[pair]
        if gram.shape[0] != WIDTH:
            gram = unpack(gram)
        squares = gram * gram
        off_total += total(jnp.where(on_diag, 0.0, squares))
        diag_total += total(jnp.where(on_diag, squares, 0.0))
        so_far = None
        for sweep in range(ITERS):
            turn, back = rotation(gram, on_diag, even, odd, power)
            if sweep < ITERS - 1:
                gram = product(back, split(product(split(gram), turn)))
            so_far = turn if so_far is None else split(product(so_far, turn))
        rows = slice(pair * WIDTH, (pair + 1) * WIDTH)
        out[rows] = so_far[:, :WIDTH].astype(jnp.float32) + so_far[:, WIDTH:].astype(jnp.float32)
    first_lane = lax.broadcasted_iota(jnp.int32, (LAST_ROWS, WIDTH), 1) == 0
    out[-LAST_ROWS:] = jnp.where(first_lane, off_total, diag_total)


def solve(parts):
    pairs = parts[0].shape[0]
    return pl.pallas_call(
        functools.partial(solve_kernel, len(parts)),
        out_shape=jax.ShapeDtypeStruct((pairs * WIDTH + LAST_ROWS, WIDTH), jnp.float32),
        in_specs=[VMEM] * len(parts),
        out_specs=VMEM,
        scratch_shapes=[
            pltpu.VMEM((WIDTH, WIDTH), jnp.float32),
            pltpu.VMEM((WIDTH, WIDTH), jnp.float32),
            pltpu.VMEM((WIDTH, 2 * WIDTH), jnp.bfloat16),
        ],
        compiler_params=PARAMS,
        name="solve",
    )(*parts)


def load_turns(where, turns, held):
    count = len(turns)
    each = (turns[0].shape[0] - LAST_ROWS) // WIDTH
    for step in range(count):
        start = jnp.bitwise_xor(where[1], step) * each
        for pair in range(each):
            held[start + pair] = turns[step][pair * WIDTH : (pair + 1) * WIDTH]


def turned(tracks, columns, held):
    results = []
    for pairs, places in tracks:
        for pair in range(pairs):
            value = jnp.concatenate([piece(columns, place, pair) for place in places], axis=0)
            results.append((value, len(results)))
    return lambda index: product(split(results[index][0]), split(held[index]))


def edge_kernel(tracks, count, where, *refs):
    turns, columns = refs[:count], refs[count:-4]
    up, down, sums, held = refs[-4:]
    load_turns(where, turns, held)
    rows = columns[0].shape[1]
    half = rows // 2
    blocks = len(tracks[0][1])
    low_lanes = lax.broadcasted_iota(jnp.int32, (half, WIDTH), 1) < BLOCK
    result = turned(tracks, columns, held)
    last = result(held.shape[0] - 1)
    first = result(0)
    for block in range(blocks):
        span = slice(block * half, (block + 1) * half)
        one = last[block * rows : (block + 1) * rows]
        up[span] = jnp.where(low_lanes, one[:half], pltpu.roll(one[half:], BLOCK, 1))
        one = first[block * rows : (block + 1) * rows]
        down[span] = jnp.where(low_lanes, pltpu.roll(one[:half], BLOCK, 1), one[half:])
    value = turns[0][-LAST_ROWS:]
    for turn in turns[1:]:
        value = value + turn[-LAST_ROWS:]
    sums[...] = value


def edges(tracks, where, columns, turns):
    rows = columns[0].shape[1]
    blocks = len(tracks[0][1])
    pairs = sum(track[0] for track in tracks)
    shape = jax.ShapeDtypeStruct((blocks * rows // 2, WIDTH), jnp.float32)
    return pl.pallas_call(
        functools.partial(edge_kernel, tracks, len(turns)),
        out_shape=(shape, shape, jax.ShapeDtypeStruct((LAST_ROWS, WIDTH), jnp.float32)),
        in_specs=[SMEM] + [VMEM] * (len(turns) + len(columns)),
        out_specs=(VMEM,) * 3,
        scratch_shapes=[pltpu.VMEM((pairs, WIDTH, WIDTH), jnp.float32)],
        compiler_params=PARAMS,
        name="edges",
    )(where, *turns, *columns)


def place_kernel(tracks, count, where, came_up, came_down, *refs):
    turns, columns = refs[:count], refs[count:-2]
    out, held = refs[-2:]
    load_turns(where, turns, held)
    pairs = held.shape[0]
    rows = columns[0].shape[1]
    half = rows // 2
    blocks = len(tracks[0][1])
    is_first = where[0] == 0
    is_last = where[0] == where[2] - 1
    low_lanes = lax.broadcasted_iota(jnp.int32, (rows, WIDTH), 1) < BLOCK
    result = turned(tracks, columns, held)
    rotated = [result(pair) for pair in range(pairs)]
    for block in range(blocks):
        span = slice(block * rows, (block + 1) * rows)
        own_place = jnp.bitwise_xor(where[3], block)
        own_rows = pl.ds(pl.multiple_of(own_place * rows, rows), rows)
        place_up = jnp.bitwise_xor(own_place, where[4])
        place_down = jnp.bitwise_xor(own_place, where[5])
        arrived_up = came_up[pl.ds(pl.multiple_of(place_up * half, half), half)]
        arrived_up = jnp.concatenate([arrived_up, pltpu.roll(arrived_up, BLOCK, 1)], axis=0)
        arrived_down = came_down[pl.ds(pl.multiple_of(place_down * half, half), half)]
        arrived_down = jnp.concatenate([pltpu.roll(arrived_down, BLOCK, 1), arrived_down], axis=0)
        for pair in range(pairs):
            if pair == 0:
                upper = jnp.where(is_first, rotated[0][span], arrived_up)
            else:
                upper = rotated[pair - 1][span]
                if pair == 1:
                    upper = jnp.where(is_first, pltpu.roll(upper, BLOCK, 1), upper)
            if pair == pairs - 1:
                lower = jnp.where(is_last, pltpu.roll(rotated[pair][span], BLOCK, 1), arrived_down)
            else:
                lower = rotated[pair + 1][span]
            out[own_rows, pair * WIDTH : (pair + 1) * WIDTH] = jnp.where(low_lanes, upper, lower)


def place(tracks, where, columns, came_up, came_down, turns):
    rows = columns[0].shape[1]
    blocks = len(tracks[0][1])
    pairs = sum(track[0] for track in tracks)
    return pl.pallas_call(
        functools.partial(place_kernel, tracks, len(turns)),
        out_shape=jax.ShapeDtypeStruct((blocks * rows, pairs * WIDTH), jnp.float32),
        in_specs=[SMEM] + [VMEM] * (2 + len(turns) + len(columns)),
        out_specs=VMEM,
        scratch_shapes=[pltpu.VMEM((pairs, WIDTH, WIDTH), jnp.float32)],
        compiler_params=PARAMS,
        name="place",
    )(where, came_up, came_down, *turns, *columns)


def passed_along(value, axis, by):
    count = lax.axis_size(axis)
    pairs = [(i, i + by) for i in range(count) if 0 <= i + by < count]
    return lax.ppermute(value, axis, pairs)


def swapped(value, axis, by):
    count = lax.axis_size(axis)
    return lax.ppermute(value, axis, [(i, i ^ by) for i in range(count)])


def summed(value, axis, last):
    count = lax.axis_size(axis)
    if count & (count - 1):
        return lax.psum(value, axis), last
    step = 1
    while step < count:
        other = swapped(value, axis, step)
        step *= 2
        if step >= count:
            value, other, last = lax.optimization_barrier((value, other, last))
        value = value + other
    return value, last


def on_device(r_factor, block_slots):
    pair_count = lax.axis_size("pair")
    row_count = lax.axis_size("row")
    pair_index = lax.axis_index("pair")
    row_index = lax.axis_index("row")
    local = r_factor.shape[1] // WIDTH // pair_count
    shared = local % row_count == 0 and row_count & (row_count - 1) == 0
    shares = row_count if shared else 1
    row = (row_index if shared else jnp.zeros_like(row_index)).astype(jnp.int32).reshape(1)
    base = pair_index.astype(jnp.int32).reshape(1)
    if shared and pair_count == 8:
        plan = [(local, 0, local, (position,)) for position in range(pair_count)]
        arranged = gather(r_factor, block_slots, base, tuple(plan))
        here = arranged[0::2]
        near = [swapped(value, "pair", 1) for value in arranged[1::2]]
        here_two = swapped(here[1], "pair", 2)
        here_four = swapped(here[2], "pair", 4)
        own, *given = near_grams(here, near)
        taken = [swapped(value, "pair", by) for by, value in zip((2, 4, 6), given)]
        on_two, on_four = joined((near[1], here[3]), (near[2], near[3]))
        here_two, here_four, on_two, on_four, taken = lax.optimization_barrier((here_two, here_four, on_two, on_four, taken))
        parts = merge(row, [own] + taken, shares)
        from_two = swapped(on_two, "pair", 2)
        from_four = swapped(on_four, "pair", 4)
        tracks = ((local, tuple((position, 0) for position in range(pair_count))),)
        bases = (pair_index, pair_index - 1, pair_index + 1)
    else:
        (arranged,) = gather(r_factor, block_slots, base, ((local, 0, local, None),))
        column = lax.all_to_all(arranged, "pair", split_axis=0, concat_axis=0, tiled=True)
        parts = grams(row, column, shares)
        columns = (column,)
        tracks = ((local, tuple((0, group) for group in range(pair_count))),)
        bases = (jnp.zeros_like(pair_index),) * 3
    if shared:
        turn = solve([parts[0]] + [swapped(parts[by], "row", by) for by in range(1, row_count)])
        if pair_count == 8:
            from_two, from_four, turn = lax.optimization_barrier((from_two, from_four, turn))
            here_six = swapped(from_two[1:], "pair", 4)
            near_six = swapped(from_four[1:], "pair", 2)
            columns = (here[0], near[0], here_two, from_two, here_four, from_four, here_six, near_six)
        turns = [turn] + [swapped(turn, "row", by) for by in range(1, row_count)]
    else:
        turns = [solve([lax.psum(parts[0], "row")])]
    bases = [jnp.clip(value, 0, pair_count - 1) for value in bases]
    where = jnp.stack([pair_index, row[0], jnp.int32(pair_count)] + bases).astype(jnp.int32)
    up, down, sums = edges(tracks, where, columns, turns)
    came_up = passed_along(up, "pair", 1)
    came_down = passed_along(down, "pair", -1)
    rotated = place(tracks, where, columns, came_up, came_down, turns)
    sums, rotated = summed(sums, "pair", rotated)
    off_ratio = jnp.sqrt(sums[0, 0] / sums[0, 1])
    return (rotated, off_ratio)


def solution(mesh):
    in_specs = (P(("row", "pair"), None), P())
    out_specs = (P("row", "pair"), P())
    return jax.shard_map(
        on_device, mesh=mesh, in_specs=in_specs, out_specs=out_specs, check_vma=False
    )
```

time: 90 us -> 69 us (0.77)
  waiting for transfers between devices: 48.3 us -> 21.1 us
  starting transfers between devices: 23.2 us -> 29.9 us
  local copies, waits for them, and re-layouts: 4.16 us -> 2.96 us
    all_to_all x1 -> x0, waiting for transfers between devices: 26.6 us -> none  [on_device(): lax.all_to_all(arranged, 'pair', split_axis=0, concat_axis=0, tiled=True)]
    ppermute x11 -> x22, starting transfers between devices: 15.4 us -> 27.3 us  [swapped(): return lax.ppermute(value, axis, [(i, i ^ by) for i in range(count)])]
    all_to_all x1 -> x0, starting transfers between devices: 5.17 us -> none  [on_device(): lax.all_to_all(arranged, 'pair', split_axis=0, concat_axis=0, tiled=True)]
    unnamed x6 -> x4, local copies, waits for them, and re-layouts: 3.55 us -> 2.24 us
    pallas_call x5 -> x7, Pallas kernels: 10.8 us -> 11.5 us  [the longest x1 4.16 us: solve(): pl.pallas_call(functools.partial(solve_kernel, len(parts)), out_shape=jax...]
    ppermute x11 -> x22, waiting for transfers between devices: 21.6 us -> 21.1 us  [swapped(): return lax.ppermute(value, axis, [(i, i ^ by) for i in range(count)])]
  transfers between devices with their start and end apart: 14 -> 24, of which waited for: 11 -> 10; matrix products, arithmetic and copies ran while one was open for 1% -> 0% of each run, Pallas kernels for 0% -> 13%
where the time goes in v2:
time: 69 us; the launch traced here: 68.7 us
  starting transfers between devices  29.9 us (43%)
  waiting for transfers between devices  21.1 us (31%)
  Pallas kernels  11.5 us (17%)
  between operations  3.29 us (5%)
  local copies, waits for them, and re-layouts  2.96 us (4%)
    ppermute x22, starting transfers between devices, swapped(): return lax.ppermute(value, axis, [(i, i ^ by) for i in range(count)])  27.3 us
    ppermute x22, waiting for transfers between devices, swapped(): return lax.ppermute(value, axis, [(i, i ^ by) for i in range(count)])  21.1 us
    pallas_call x1, Pallas kernels, solve(): pl.pallas_call(functools.partial(solve_kernel, len(parts)), out_shape=jax...  4.16 us
    pallas_call x1, Pallas kernels, place(): pl.pallas_call(functools.partial(place_kernel, tracks, len(turns)), out_s...  2.78 us
    ppermute x2, starting transfers between devices, passed_along(): return lax.ppermute(value, axis, pairs)  2.6 us
    unnamed x4, local copies, waits for them, and re-layouts  2.24 us
    pallas_call x1, Pallas kernels, gather(): pl.pallas_call(functools.partial(gather_kernel, tuple(((local, first, pos...  1.7 us
  transfers between devices with their start and end apart: 24, of which 10 were waited for; matrix products, arithmetic and copies ran while one was open for 0% of the time, Pallas kernels for 13%

profile of v2, /device:TPU:0, one launch (start us, length us, event | category | flops | bytes accessed | tf_op | source)
XLA Modules:
  0.0 68.7 jit_solution(3517903956233707860)
XLA Ops:
  0.6 0.0 copy-start
  0.6 1.6 %copy-done = f32[128,4096]{1,0:T(8,128)S(1)} copy-done((f32[128,4096]{1,0:T(8,128)S(1)}, f32[128,4096]{1,0:T(8,128)}, u32[]{:S(2)}) %copy-start) | copy-done | bytes 2097176
  2.2 0.0 copy-start.1
  2.2 0.7 copy-done.1
  2.9 1.7 %gather.1 = (f32[1,128,512]{2,1,0:T(8,128)S(1)}, f32[1,128,512]{2,1,0:T(8,128)S(1)}, f32[1,128,512]{2,1,0:T(8,128)S(1)}, f32[1,128,512]{2,1,0:T(8,128)S(1)}, f32...) custom-call(s32[64]{0:T(128)S(1)} %copy-done.1, ...), custom_call_target="tpu_custom_call" | custom-call | tf_op jit(solution)/shard_map/gather/pallas_call | solution.py:81
  4.6 0.5 collective-permute-start.5
  5.1 0.1 collective-permute-start.2
  5.2 0.4 collective-permute-start.3
  5.6 0.1 collective-permute-start.4
  5.7 2.9 %collective-permute-start = (f32[1,128,512]{2,1,0:T(8,128)S(1)}, f32[1,128,512]{2,1,0:T(8,128)S(1)}, u32[]{:S(2)}, u32[]{:S(2)}) collective-permute-start(f32[1,128,512]{2,1,0:T(8,128)S(1)} %get-tuple-element.36.refs_1_), channel_id=1, source_target_pairs={{0,8},{4,12},{8,0},{12,4},{16,24},{20,28},{24,16},{28,20},{1,9},{5... | collective-permute-start | bytes 786440 | tf_op jit(solution)/shard_map/ppermute | solution.py:425
  8.6 0.0 collective-permute-done.5.refs_4_.refs_5_
  8.6 1.5 %collective-permute-start.1 = (f32[1,128,512]{2,1,0:T(8,128)S(1)}, f32[1,128,512]{2,1,0:T(8,128)S(1)}, u32[]{:S(2)}, u32[]{:S(2)}) collective-permute-start(f32[1,128,512]{2,1,0:T(8,128)S(1)} %get-tuple-element.37.refs_2_), channel_id=1, source_target_pairs={{0,16},{4,20},{8,24},{12,28},{16,0},{20,4},{24,8},{28,12},{1,17},{... | collective-permute-start | bytes 786440 | tf_op jit(solution)/shard_map/ppermute | solution.py:425
  10.1 0.0 collective-permute-done.2.refs_0_.refs_5_
  10.1 0.0 collective-permute-done.3.refs_2_.refs_6_
  10.1 0.0 collective-permute-done.4.refs_3_.refs_7_
  10.2 0.9 %near_grams.1 = (f32[4,72,128]{2,1,0:T(8,128)S(1)}, f32[4,72,128]{2,1,0:T(8,128)S(1)}, f32[4,72,128]{2,1,0:T(8,128)S(1)}, f32[4,72,128]{2,1,0:T(8,128)S(1)}) custom-call(f32[1,128,512]{2,1,0:T(8,128)S(1)} %get-tuple-element.44.refs_0_.refs_4_, f32[1,128,512]{2,1,0:T(8,128)S(1)} %get-tuple-element.36.refs_1_, f32[1,128,512]{2,1,0:T(8,128)S(1)} %get-tuple-element.37.refs_2_, ...), custom_call_target="tpu_custom_call" | custom-call | tf_op jit(solution)/shard_map/near_grams/pallas_call | solution.py:168
  11.0 0.6 collective-permute-start.6
  11.6 1.1 %collective-permute-start.7 = (f32[4,72,128]{2,1,0:T(8,128)S(1)}, f32[4,72,128]{2,1,0:T(8,128)S(1)}, u32[]{:S(2)}, u32[]{:S(2)}) collective-permute-start(f32[4,72,128]{2,1,0:T(8,128)S(1)} %get-tuple-element.47), channel_id=1, source_target_pairs={{0,16},{4,20},{8,24},{12,28},{16,0},{20,4},{24,8},{28,12},{1,17},{... | collective-permute-start | bytes 442376 | tf_op jit(solution)/shard_map/ppermute | solution.py:425
  12.7 1.9 %collective-permute-start.8 = (f32[4,72,128]{2,1,0:T(8,128)S(1)}, f32[4,72,128]{2,1,0:T(8,128)S(1)}, u32[]{:S(2)}, u32[]{:S(2)}) collective-permute-start(f32[4,72,128]{2,1,0:T(8,128)S(1)} %get-tuple-element.48), channel_id=1, source_target_pairs={{0,24},{4,28},{8,16},{12,20},{16,8},{20,12},{24,0},{28,4},{1,25},{... | collective-permute-start | bytes 442376 | tf_op jit(solution)/shard_map/ppermute | solution.py:425
  14.6 0.9 %joined.1 = (f32[2,128,512]{2,1,0:T(8,128)S(1)}, f32[2,128,512]{2,1,0:T(8,128)}) custom-call(f32[1,128,512]{2,1,0:T(8,128)S(1)} %collective-permute-done.2.refs_0_.refs_5_, f32[1,128,512]{2,1,0:T(8,128)S(1)} %get-tuple-element.39.refs_1_.refs_3_, f32[1,128,512]{2,1,0:T(8,128)S(1)} %collective-permute-done.3.refs_2_.refs_6_, ...), custom_call_target="tpu_custom_call" | custom-call | tf_op jit(solution)/shard_map/joined/pallas_call | solution.py:187
  15.4 0.3 collective-permute-done.refs_6_
  15.7 2.1 %collective-permute-done.1.refs_8_ = f32[1,128,512]{2,1,0:T(8,128)S(1)} collective-permute-done((f32[1,128,512]{2,1,0:T(8,128)S(1)}, f32[1,128,512]{2,1,0:T(8,128)S(1)}, u32[]{:S(2)}, u32[]{:S(2)}) %collective-permute-start.1) | collective-permute-done | bytes 262176 | tf_op jit(solution)/shard_map/ppermute | solution.py:425
  17.8 1.1 %collective-permute-done.6.refs_1_ = f32[4,72,128]{2,1,0:T(8,128)S(1)} collective-permute-done((f32[4,72,128]{2,1,0:T(8,128)S(1)}, f32[4,72,128]{2,1,0:T(8,128)S(1)}, u32[]{:S(2)}, u32[]{:S(2)}) %collective-permute-start.6) | collective-permute-done | bytes 147488 | tf_op jit(solution)/shard_map/ppermute | solution.py:425
  18.9 4.1 %collective-permute-done.7.refs_2_ = f32[4,72,128]{2,1,0:T(8,128)S(1)} collective-permute-done((f32[4,72,128]{2,1,0:T(8,128)S(1)}, f32[4,72,128]{2,1,0:T(8,128)S(1)}, u32[]{:S(2)}, u32[]{:S(2)}) %collective-permute-start.7) | collective-permute-done | bytes 147488 | tf_op jit(solution)/shard_map/ppermute | solution.py:425
  22.9 0.0 collective-permute-done.8.refs_3_
  23.0 1.5 %collective-permute-start.10 = (f32[2,128,512]{2,1,0:T(8,128)}, f32[2,128,512]{2,1,0:T(8,128)S(1)}, u32[]{:S(2)}, u32[]{:S(2)}) collective-permute-start(f32[2,128,512]{2,1,0:T(8,128)} %get-tuple-element.50), channel_id=1, source_target_pairs={{0,16},{4,20},{8,24},{12,28},{16,0},{20,4},{24,8},{28,12},{1,17},{... | collective-permute-start | bytes 1572872 | tf_op jit(solution)/shard_map/ppermute | solution.py:425
  24.5 0.8 %collective-permute-start.9 = (f32[2,128,512]{2,1,0:T(8,128)S(1)}, f32[2,128,512]{2,1,0:T(8,128)S(1)}, u32[]{:S(2)}, u32[]{:S(2)}) collective-permute-start(f32[2,128,512]{2,1,0:T(8,128)S(1)} %get-tuple-element.49), channel_id=1, source_target_pairs={{0,8},{4,12},{8,0},{12,4},{16,24},{20,28},{24,16},{28,20},{1,9},{5... | collective-permute-start | bytes 1572872 | tf_op jit(solution)/shard_map/ppermute | solution.py:425
  25.4 1.6 %collective-permute-start.11 = (f32[1,72,128]{2,1,0:T(8,128)S(1)}, f32[1,72,128]{2,1,0:T(8,128)S(1)}, u32[]{:S(2)}, u32[]{:S(2)}) collective-permute-start(f32[1,72,128]{2,1,0:T(8,128)S(1)} %get-tuple-element.56), channel_id=1, source_target_pairs={{0,1},{1,0},{2,3},{3,2},{4,5},{5,4},{6,7},{7,6},{8,9},{9,8},{10,11... | collective-permute-start | bytes 110600 | tf_op jit(solution)/shard_map/ppermute | solution.py:425
  27.0 2.6 %collective-permute-start.12 = (f32[1,72,128]{2,1,0:T(8,128)S(1)}, f32[1,72,128]{2,1,0:T(8,128)S(1)}, u32[]{:S(2)}, u32[]{:S(2)}) collective-permute-start(f32[1,72,128]{2,1,0:T(8,128)S(1)} %get-tuple-element.57), channel_id=1, source_target_pairs={{0,2},{1,3},{2,0},{3,1},{4,6},{5,7},{6,4},{7,5},{8,10},{9,11},{10,... | collective-permute-start | bytes 110600 | tf_op jit(solution)/shard_map/ppermute | solution.py:425
  29.6 0.2 collective-permute-start.13
  29.8 0.0 collective-permute-done.11.refs_1_
  29.8 2.8 %collective-permute-done.12.refs_2_ = f32[1,72,128]{2,1,0:T(8,128)S(1)} collective-permute-done((f32[1,72,128]{2,1,0:T(8,128)S(1)}, f32[1,72,128]{2,1,0:T(8,128)S(1)}, u32[]{:S(2)}, u32[]{:S(2)}) %collective-permute-start.12) | collective-permute-done | bytes 36896 | tf_op jit(solution)/shard_map/ppermute | solution.py:425
  32.6 2.8 %collective-permute-done.13.refs_3_ = f32[1,72,128]{2,1,0:T(8,128)S(1)} collective-permute-done((f32[1,72,128]{2,1,0:T(8,128)S(1)}, f32[1,72,128]{2,1,0:T(8,128)S(1)}, u32[]{:S(2)}, u32[]{:S(2)}) %collective-permute-start.13) | collective-permute-done | bytes 36896 | tf_op jit(solution)/shard_map/ppermute | solution.py:425
  35.4 4.2 %solve.1.refs_0_ = f32[136,128]{1,0:T(8,128)S(1)} custom-call(f32[1,72,128]{2,1,0:T(8,128)S(1)} %get-tuple-element.55.refs_0_, f32[1,72,128]{2,1,0:T(8,128)S(1)} %collective-permute-done.11.refs_1_, f32[1,72,128]{2,1,0:T(8,128)S(1)} %collective-permute-done.12.refs_2_, f32[1,72,128]{2,1,0:T(8,128)S(1)} %collective-permute-done.13.refs_3_), custom_call_target="tpu_custom_call" | custom-call | tf_op jit(solution)/shard_map/solve/pallas_call | solution.py:293
  39.5 0.0 collective-permute-done.10.refs_9_
  39.5 0.0 collective-permute-done.9.refs_7_
  39.6 1.0 %collective-permute-start.17 = (f32[1,128,512]{2,1,0:T(8,128)S(1)}, f32[1,128,512]{2,1,0:T(8,128)S(1)}, u32[]{:S(2)}, u32[]{:S(2)}) collective-permute-start(f32[1,128,512]{2,1,0:T(8,128)S(1)} %slice.12), channel_id=1, source_target_pairs={{0,16},{4,20},{8,24},{12,28},{16,0},{20,4},{24,8},{28,12},{1,17},{... | collective-permute-start | bytes 786440 | tf_op jit(solution)/shard_map/ppermute | solution.py:425
  40.5 0.9 %collective-permute-start.18 = (f32[1,128,512]{2,1,0:T(8,128)S(1)}, f32[1,128,512]{2,1,0:T(8,128)S(1)}, u32[]{:S(2)}, u32[]{:S(2)}) collective-permute-start(f32[1,128,512]{2,1,0:T(8,128)S(1)} %slice.13), channel_id=1, source_target_pairs={{0,8},{4,12},{8,0},{12,4},{16,24},{20,28},{24,16},{28,20},{1,9},{5... | collective-permute-start | bytes 786440 | tf_op jit(solution)/shard_map/ppermute | solution.py:425
  41.4 0.0 collective-permute-start.14
  41.4 1.9 %collective-permute-start.15 = (f32[136,128]{1,0:T(8,128)S(1)}, f32[136,128]{1,0:T(8,128)S(1)}, u32[]{:S(2)}, u32[]{:S(2)}) collective-permute-start(f32[136,128]{1,0:T(8,128)S(1)} %solve.1.refs_0_), channel_id=1, source_target_pairs={{0,2},{1,3},{2,0},{3,1},{4,6},{5,7},{6,4},{7,5},{8,10},{9,11},{10,... | collective-permute-start | bytes 208904 | tf_op jit(solution)/shard_map/ppermute | solution.py:425
  43.3 2.5 %collective-permute-start.16 = (f32[136,128]{1,0:T(8,128)S(1)}, f32[136,128]{1,0:T(8,128)S(1)}, u32[]{:S(2)}, u32[]{:S(2)}) collective-permute-start(f32[136,128]{1,0:T(8,128)S(1)} %solve.1.refs_0_), channel_id=1, source_target_pairs={{0,3},{1,2},{2,1},{3,0},{4,7},{5,6},{6,5},{7,4},{8,11},{9,10},{10,... | collective-permute-start | bytes 208904 | tf_op jit(solution)/shard_map/ppermute | solution.py:425
  45.8 0.1 stack.19.where
  45.9 1.1 %collective-permute-done.14.refs_1_ = f32[136,128]{1,0:T(8,128)S(1)} collective-permute-done((f32[136,128]{1,0:T(8,128)S(1)}, f32[136,128]{1,0:T(8,128)S(1)}, u32[]{:S(2)}, u32[]{:S(2)}) %collective-permute-start.14) | collective-permute-done | bytes 69664 | tf_op jit(solution)/shard_map/ppermute | solution.py:425
  47.0 0.0 collective-permute-done.15.refs_2_
  47.0 2.5 %collective-permute-done.16.refs_3_ = f32[136,128]{1,0:T(8,128)S(1)} collective-permute-done((f32[136,128]{1,0:T(8,128)S(1)}, f32[136,128]{1,0:T(8,128)S(1)}, u32[]{:S(2)}, u32[]{:S(2)}) %collective-permute-start.16) | collective-permute-done | bytes 69664 | tf_op jit(solution)/shard_map/ppermute | solution.py:425
  49.4 0.0 collective-permute-done.17.refs_10_
  49.4 0.0 collective-permute-done.18.refs_11_
  49.4 1.1 %edges.1 = (f32[512,128]{1,0:T(8,128)S(1)}, f32[512,128]{1,0:T(8,128)S(1)}, f32[8,128]{1,0:T(8,128)S(1)}) custom-call(s32[6]{0:T(128)S(1)} %stack.19.where, f32[136,128]{1,0:T(8,128)S(1)} %solve.1.refs_0_, f32[136,128]{1,0:T(8,128)S(1)} %collective-permute-done.14.refs_1_, f32[136,128]{1,0:T(8,128)S(1)} %collective-permute-done.15.refs_2_, ...), custom_call_target="tpu_custom_call" | custom-call | tf_op jit(solution)/shard_map/edges/pallas_call | solution.py:354
  50.5 1.3 %collective-permute-start.22 = (f32[512,128]{1,0:T(8,128)S(1)}, f32[512,128]{1,0:T(8,128)S(1)}, u32[]{:S(2)}, u32[]{:S(2)}) collective-permute-start(f32[512,128]{1,0:T(8,128)S(1)} %get-tuple-element.65), channel_id=1, source_target_pairs={{0,4},{4,8},{8,12},{12,16},{16,20},{20,24},{24,28},{1,5},{5,9},{9,... | collective-permute-start | bytes 786440 | tf_op jit(solution)/shard_map/ppermute | solution.py:420
  51.8 1.3 %collective-permute-start.23 = (f32[512,128]{1,0:T(8,128)S(1)}, f32[512,128]{1,0:T(8,128)S(1)}, u32[]{:S(2)}, u32[]{:S(2)}) collective-permute-start(f32[512,128]{1,0:T(8,128)S(1)} %get-tuple-element.66), channel_id=1, source_target_pairs={{4,0},{8,4},{12,8},{16,12},{20,16},{24,20},{28,24},{5,1},{9,5},{13... | collective-permute-start | bytes 786440 | tf_op jit(solution)/shard_map/ppermute | solution.py:420
  53.1 2.1 %collective-permute-start.19 = (f32[8,128]{1,0:T(8,128)S(1)}, f32[8,128]{1,0:T(8,128)S(1)}, u32[]{:S(2)}, u32[]{:S(2)}) collective-permute-start(f32[8,128]{1,0:T(8,128)S(1)} %get-tuple-element.64), channel_id=1, source_target_pairs={{0,4},{4,0},{8,12},{12,8},{16,20},{20,16},{24,28},{28,24},{1,5},{5... | collective-permute-start | bytes 12296 | tf_op jit(solution)/shard_map/ppermute | solution.py:425
  55.2 0.9 %collective-permute-done.19 = f32[8,128]{1,0:T(8,128)S(1)} collective-permute-done((f32[8,128]{1,0:T(8,128)S(1)}, f32[8,128]{1,0:T(8,128)S(1)}, u32[]{:S(2)}, u32[]{:S(2)}) %collective-permute-start.19) | collective-permute-done | bytes 4128 | tf_op jit(solution)/shard_map/ppermute | solution.py:425
  56.2 1.8 %collective-permute-start.20 = (f32[8,128]{1,0:T(8,128)S(1)}, f32[8,128]{1,0:T(8,128)S(1)}, u32[]{:S(2)}, u32[]{:S(2)}) collective-permute-start(f32[8,128]{1,0:T(8,128)S(1)} %add.14), channel_id=1, source_target_pairs={{0,8},{4,12},{8,0},{12,4},{16,24},{20,28},{24,16},{28,20},{1,9},{5... | collective-permute-start | bytes 12296 | tf_op jit(solution)/shard_map/ppermute | solution.py:425
  58.0 3.5 %collective-permute-done.20 = f32[8,128]{1,0:T(8,128)S(1)} collective-permute-done((f32[8,128]{1,0:T(8,128)S(1)}, f32[8,128]{1,0:T(8,128)S(1)}, u32[]{:S(2)}, u32[]{:S(2)}) %collective-permute-start.20) | collective-permute-done | bytes 4128 | tf_op jit(solution)/shard_map/ppermute | solution.py:425
  61.5 1.3 %collective-permute-start.21 = (f32[8,128]{1,0:T(8,128)S(1)}, f32[8,128]{1,0:T(8,128)S(1)}, u32[]{:S(2)}, u32[]{:S(2)}) collective-permute-start(f32[8,128]{1,0:T(8,128)S(1)} %add.15), channel_id=1, source_target_pairs={{0,16},{4,20},{8,24},{12,28},{16,0},{20,4},{24,8},{28,12},{1,17},{... | collective-permute-start | bytes 12296 | tf_op jit(solution)/shard_map/ppermute | solution.py:425
  62.8 0.0 collective-permute-done.22.came_up
  62.8 0.0 collective-permute-done.23.came_down
  62.8 2.8 %place.1 = f32[1024,512]{1,0:T(8,128)} custom-call(s32[6]{0:T(128)S(1)} %stack.19.where, f32[512,128]{1,0:T(8,128)S(1)} %collective-permute-done.22.came_up, f32[512,128]{1,0:T(8,128)S(1)} %collective-permute-done.23.came_down, f32[136,128]{1,0:T(8,128)S(1)} %solve.1.refs_0_, f32[136,128]{1,0:T(8,128)S(1)} %collective-permute-done.14.refs_1_, ...), custom_call_target="tpu_custom_call" | custom-call | tf_op jit(solution)/shard_map/place/pallas_call | solution.py:406
  65.6 0.0 collective-permute-done.21
  65.6 0.6 fusion
  (6 shorter events, 0.1 us)
Async XLA Ops:
  0.6 1.6 %copy-start = (f32[128,4096]{1,0:T(8,128)S(1)}, f32[128,4096]{1,0:T(8,128)}, u32[]{:S(2)}) copy-start(f32[128,4096]{1,0:T(8,128)} %source.1) | copy-start | bytes 6291460
  2.2 0.7 copy-start.1
  4.6 4.0 %collective-permute-start.5 = (f32[1,128,512]{2,1,0:T(8,128)S(1)}, f32[1,128,512]{2,1,0:T(8,128)S(1)}, u32[]{:S(2)}, u32[]{:S(2)}) collective-permute-start(f32[1,128,512]{2,1,0:T(8,128)S(1)} %get-tuple-element.45), channel_id=1, source_target_pairs={{0,4},{4,0},{8,12},{12,8},{16,20},{20,16},{24,28},{28,24},{1,5},{5... | collective-permute-start | bytes 786440 | tf_op jit(solution)/shard_map/ppermute | solution.py:425
  5.1 5.0 %collective-permute-start.2 = (f32[1,128,512]{2,1,0:T(8,128)S(1)}, f32[1,128,512]{2,1,0:T(8,128)S(1)}, u32[]{:S(2)}, u32[]{:S(2)}) collective-permute-start(f32[1,128,512]{2,1,0:T(8,128)S(1)} %get-tuple-element.38), channel_id=1, source_target_pairs={{0,4},{4,0},{8,12},{12,8},{16,20},{20,16},{24,28},{28,24},{1,5},{5... | collective-permute-start | bytes 786440 | tf_op jit(solution)/shard_map/ppermute | solution.py:425
  5.2 5.0 %collective-permute-start.3 = (f32[1,128,512]{2,1,0:T(8,128)S(1)}, f32[1,128,512]{2,1,0:T(8,128)S(1)}, u32[]{:S(2)}, u32[]{:S(2)}) collective-permute-start(f32[1,128,512]{2,1,0:T(8,128)S(1)} %get-tuple-element.40), channel_id=1, source_target_pairs={{0,4},{4,0},{8,12},{12,8},{16,20},{20,16},{24,28},{28,24},{1,5},{5... | collective-permute-start | bytes 786440 | tf_op jit(solution)/shard_map/ppermute | solution.py:425
  5.6 4.5 %collective-permute-start.4 = (f32[1,128,512]{2,1,0:T(8,128)S(1)}, f32[1,128,512]{2,1,0:T(8,128)S(1)}, u32[]{:S(2)}, u32[]{:S(2)}) collective-permute-start(f32[1,128,512]{2,1,0:T(8,128)S(1)} %get-tuple-element.41), channel_id=1, source_target_pairs={{0,4},{4,0},{8,12},{12,8},{16,20},{20,16},{24,28},{28,24},{1,5},{5... | collective-permute-start | bytes 786440 | tf_op jit(solution)/shard_map/ppermute | solution.py:425
  5.7 10.0 %collective-permute-start = (f32[1,128,512]{2,1,0:T(8,128)S(1)}, f32[1,128,512]{2,1,0:T(8,128)S(1)}, u32[]{:S(2)}, u32[]{:S(2)}) collective-permute-start(f32[1,128,512]{2,1,0:T(8,128)S(1)} %get-tuple-element.36.refs_1_), channel_id=1, source_target_pairs={{0,8},{4,12},{8,0},{12,4},{16,24},{20,28},{24,16},{28,20},{1,9},{5... | collective-permute-start | bytes 786440 | tf_op jit(solution)/shard_map/ppermute | solution.py:425
  8.6 9.2 %collective-permute-start.1 = (f32[1,128,512]{2,1,0:T(8,128)S(1)}, f32[1,128,512]{2,1,0:T(8,128)S(1)}, u32[]{:S(2)}, u32[]{:S(2)}) collective-permute-start(f32[1,128,512]{2,1,0:T(8,128)S(1)} %get-tuple-element.37.refs_2_), channel_id=1, source_target_pairs={{0,16},{4,20},{8,24},{12,28},{16,0},{20,4},{24,8},{28,12},{1,17},{... | collective-permute-start | bytes 786440 | tf_op jit(solution)/shard_map/ppermute | solution.py:425
  11.0 7.9 %collective-permute-start.6 = (f32[4,72,128]{2,1,0:T(8,128)S(1)}, f32[4,72,128]{2,1,0:T(8,128)S(1)}, u32[]{:S(2)}, u32[]{:S(2)}) collective-permute-start(f32[4,72,128]{2,1,0:T(8,128)S(1)} %get-tuple-element.46), channel_id=1, source_target_pairs={{0,8},{4,12},{8,0},{12,4},{16,24},{20,28},{24,16},{28,20},{1,9},{5... | collective-permute-start | bytes 442376 | tf_op jit(solution)/shard_map/ppermute | solution.py:425
  11.6 11.3 %collective-permute-start.7 = (f32[4,72,128]{2,1,0:T(8,128)S(1)}, f32[4,72,128]{2,1,0:T(8,128)S(1)}, u32[]{:S(2)}, u32[]{:S(2)}) collective-permute-start(f32[4,72,128]{2,1,0:T(8,128)S(1)} %get-tuple-element.47), channel_id=1, source_target_pairs={{0,16},{4,20},{8,24},{12,28},{16,0},{20,4},{24,8},{28,12},{1,17},{... | collective-permute-start | bytes 442376 | tf_op jit(solution)/shard_map/ppermute | solution.py:425
  12.7 10.3 %collective-permute-start.8 = (f32[4,72,128]{2,1,0:T(8,128)S(1)}, f32[4,72,128]{2,1,0:T(8,128)S(1)}, u32[]{:S(2)}, u32[]{:S(2)}) collective-permute-start(f32[4,72,128]{2,1,0:T(8,128)S(1)} %get-tuple-element.48), channel_id=1, source_target_pairs={{0,24},{4,28},{8,16},{12,20},{16,8},{20,12},{24,0},{28,4},{1,25},{... | collective-permute-start | bytes 442376 | tf_op jit(solution)/shard_map/ppermute | solution.py:425
  23.0 16.6 %collective-permute-start.10 = (f32[2,128,512]{2,1,0:T(8,128)}, f32[2,128,512]{2,1,0:T(8,128)S(1)}, u32[]{:S(2)}, u32[]{:S(2)}) collective-permute-start(f32[2,128,512]{2,1,0:T(8,128)} %get-tuple-element.50), channel_id=1, source_target_pairs={{0,16},{4,20},{8,24},{12,28},{16,0},{20,4},{24,8},{28,12},{1,17},{... | collective-permute-start | bytes 1572872 | tf_op jit(solution)/shard_map/ppermute | solution.py:425
  24.5 15.1 %collective-permute-start.9 = (f32[2,128,512]{2,1,0:T(8,128)S(1)}, f32[2,128,512]{2,1,0:T(8,128)S(1)}, u32[]{:S(2)}, u32[]{:S(2)}) collective-permute-start(f32[2,128,512]{2,1,0:T(8,128)S(1)} %get-tuple-element.49), channel_id=1, source_target_pairs={{0,8},{4,12},{8,0},{12,4},{16,24},{20,28},{24,16},{28,20},{1,9},{5... | collective-permute-start | bytes 1572872 | tf_op jit(solution)/shard_map/ppermute | solution.py:425
  25.4 4.5 %collective-permute-start.11 = (f32[1,72,128]{2,1,0:T(8,128)S(1)}, f32[1,72,128]{2,1,0:T(8,128)S(1)}, u32[]{:S(2)}, u32[]{:S(2)}) collective-permute-start(f32[1,72,128]{2,1,0:T(8,128)S(1)} %get-tuple-element.56), channel_id=1, source_target_pairs={{0,1},{1,0},{2,3},{3,2},{4,5},{5,4},{6,7},{7,6},{8,9},{9,8},{10,11... | collective-permute-start | bytes 110600 | tf_op jit(solution)/shard_map/ppermute | solution.py:425
  27.0 5.6 %collective-permute-start.12 = (f32[1,72,128]{2,1,0:T(8,128)S(1)}, f32[1,72,128]{2,1,0:T(8,128)S(1)}, u32[]{:S(2)}, u32[]{:S(2)}) collective-permute-start(f32[1,72,128]{2,1,0:T(8,128)S(1)} %get-tuple-element.57), channel_id=1, source_target_pairs={{0,2},{1,3},{2,0},{3,1},{4,6},{5,7},{6,4},{7,5},{8,10},{9,11},{10,... | collective-permute-start | bytes 110600 | tf_op jit(solution)/shard_map/ppermute | solution.py:425
  29.6 5.8 %collective-permute-start.13 = (f32[1,72,128]{2,1,0:T(8,128)S(1)}, f32[1,72,128]{2,1,0:T(8,128)S(1)}, u32[]{:S(2)}, u32[]{:S(2)}) collective-permute-start(f32[1,72,128]{2,1,0:T(8,128)S(1)} %get-tuple-element.58), channel_id=1, source_target_pairs={{0,3},{1,2},{2,1},{3,0},{4,7},{5,6},{6,5},{7,4},{8,11},{9,10},{10,... | collective-permute-start | bytes 110600 | tf_op jit(solution)/shard_map/ppermute | solution.py:425
  39.6 9.9 %collective-permute-start.17 = (f32[1,128,512]{2,1,0:T(8,128)S(1)}, f32[1,128,512]{2,1,0:T(8,128)S(1)}, u32[]{:S(2)}, u32[]{:S(2)}) collective-permute-start(f32[1,128,512]{2,1,0:T(8,128)S(1)} %slice.12), channel_id=1, source_target_pairs={{0,16},{4,20},{8,24},{12,28},{16,0},{20,4},{24,8},{28,12},{1,17},{... | collective-permute-start | bytes 786440 | tf_op jit(solution)/shard_map/ppermute | solution.py:425
  40.5 8.9 %collective-permute-start.18 = (f32[1,128,512]{2,1,0:T(8,128)S(1)}, f32[1,128,512]{2,1,0:T(8,128)S(1)}, u32[]{:S(2)}, u32[]{:S(2)}) collective-permute-start(f32[1,128,512]{2,1,0:T(8,128)S(1)} %slice.13), channel_id=1, source_target_pairs={{0,8},{4,12},{8,0},{12,4},{16,24},{20,28},{24,16},{28,20},{1,9},{5... | collective-permute-start | bytes 786440 | tf_op jit(solution)/shard_map/ppermute | solution.py:425
  41.4 5.6 %collective-permute-start.14 = (f32[136,128]{1,0:T(8,128)S(1)}, f32[136,128]{1,0:T(8,128)S(1)}, u32[]{:S(2)}, u32[]{:S(2)}) collective-permute-start(f32[136,128]{1,0:T(8,128)S(1)} %solve.1.refs_0_), channel_id=1, source_target_pairs={{0,1},{1,0},{2,3},{3,2},{4,5},{5,4},{6,7},{7,6},{8,9},{9,8},{10,11... | collective-permute-start | bytes 208904 | tf_op jit(solution)/shard_map/ppermute | solution.py:425
  41.4 5.6 %collective-permute-start.15 = (f32[136,128]{1,0:T(8,128)S(1)}, f32[136,128]{1,0:T(8,128)S(1)}, u32[]{:S(2)}, u32[]{:S(2)}) collective-permute-start(f32[136,128]{1,0:T(8,128)S(1)} %solve.1.refs_0_), channel_id=1, source_target_pairs={{0,2},{1,3},{2,0},{3,1},{4,6},{5,7},{6,4},{7,5},{8,10},{9,11},{10,... | collective-permute-start | bytes 208904 | tf_op jit(solution)/shard_map/ppermute | solution.py:425
  43.3 6.1 %collective-permute-start.16 = (f32[136,128]{1,0:T(8,128)S(1)}, f32[136,128]{1,0:T(8,128)S(1)}, u32[]{:S(2)}, u32[]{:S(2)}) collective-permute-start(f32[136,128]{1,0:T(8,128)S(1)} %solve.1.refs_0_), channel_id=1, source_target_pairs={{0,3},{1,2},{2,1},{3,0},{4,7},{5,6},{6,5},{7,4},{8,11},{9,10},{10,... | collective-permute-start | bytes 208904 | tf_op jit(solution)/shard_map/ppermute | solution.py:425
  50.5 12.3 %collective-permute-start.22 = (f32[512,128]{1,0:T(8,128)S(1)}, f32[512,128]{1,0:T(8,128)S(1)}, u32[]{:S(2)}, u32[]{:S(2)}) collective-permute-start(f32[512,128]{1,0:T(8,128)S(1)} %get-tuple-element.65), channel_id=1, source_target_pairs={{0,4},{4,8},{8,12},{12,16},{16,20},{20,24},{24,28},{1,5},{5,9},{9,... | collective-permute-start | bytes 786440 | tf_op jit(solution)/shard_map/ppermute | solution.py:420
  51.8 11.0 %collective-permute-start.23 = (f32[512,128]{1,0:T(8,128)S(1)}, f32[512,128]{1,0:T(8,128)S(1)}, u32[]{:S(2)}, u32[]{:S(2)}) collective-permute-start(f32[512,128]{1,0:T(8,128)S(1)} %get-tuple-element.66), channel_id=1, source_target_pairs={{4,0},{8,4},{12,8},{16,12},{20,16},{24,20},{28,24},{5,1},{9,5},{13... | collective-permute-start | bytes 786440 | tf_op jit(solution)/shard_map/ppermute | solution.py:420
  53.1 3.0 %collective-permute-start.19 = (f32[8,128]{1,0:T(8,128)S(1)}, f32[8,128]{1,0:T(8,128)S(1)}, u32[]{:S(2)}, u32[]{:S(2)}) collective-permute-start(f32[8,128]{1,0:T(8,128)S(1)} %get-tuple-element.64), channel_id=1, source_target_pairs={{0,4},{4,0},{8,12},{12,8},{16,20},{20,16},{24,28},{28,24},{1,5},{5... | collective-permute-start | bytes 12296 | tf_op jit(solution)/shard_map/ppermute | solution.py:425
  56.2 5.3 %collective-permute-start.20 = (f32[8,128]{1,0:T(8,128)S(1)}, f32[8,128]{1,0:T(8,128)S(1)}, u32[]{:S(2)}, u32[]{:S(2)}) collective-permute-start(f32[8,128]{1,0:T(8,128)S(1)} %add.14), channel_id=1, source_target_pairs={{0,8},{4,12},{8,0},{12,4},{16,24},{20,28},{24,16},{28,20},{1,9},{5... | collective-permute-start | bytes 12296 | tf_op jit(solution)/shard_map/ppermute | solution.py:425
  61.5 4.1 %collective-permute-start.21 = (f32[8,128]{1,0:T(8,128)S(1)}, f32[8,128]{1,0:T(8,128)S(1)}, u32[]{:S(2)}, u32[]{:S(2)}) collective-permute-start(f32[8,128]{1,0:T(8,128)S(1)} %add.15), channel_id=1, source_target_pairs={{0,16},{4,20},{8,24},{12,28},{16,0},{20,4},{24,8},{28,12},{1,17},{... | collective-permute-start | bytes 12296 | tf_op jit(solution)/shard_map/ppermute | solution.py:425

commit v3 on v2

--- a/solution.py
+++ b/solution.py
@@ -103,7 +103,7 @@
 def deal(row, held, outs):
     each = outs[0].shape[0]
     for by, out in enumerate(outs):
-        out[...] = held[pl.ds(jnp.bitwise_xor(row, by) * each, each)]
+        out[...] = held[pl.ds(jnp.bitwise_xor(jnp.bitwise_and(row, len(outs) - 1), by) * each, each)]
 
 
 def grams_kernel(row, column, *refs):
@@ -216,102 +216,120 @@
     )(row, *parts)
 
 
-def rotation(gram, on_diag, even, odd, power):
-    diag_part = jnp.where(on_diag, gram, 0.0)
-    across = jnp.sum(diag_part, axis=1, keepdims=True)
-    down = jnp.sum(diag_part, axis=0, keepdims=True)
-    skew = gram * (across - down) / (2.0 * (across * across + down * down))
-    skew_parts = split(skew)
-    square = product(skew_parts, skew_parts)
-    bound = jnp.sqrt(0.5 * total(square * square))
-    scale = 2.0 / (2.0 + bound)
-    rate = bound / (2.0 + bound)
+def rotations(grams_now, on_diag, even, odd, power):
     diag_one = jnp.where(on_diag, 1.0, 0.0)
-    rest = (1.0 - scale) * diag_one + scale * square
-    rest_parts = split(rest)
-    size = gram.shape[0]
-    first = product(jnp.concatenate([skew_parts, rest_parts], axis=0), rest_parts)
-    even_now = scale * (diag_one + rest)
-    odd_now = scale * (skew + first[:size])
-    rest_parts = split(first[size:])
-    second = product(jnp.concatenate([split(even_now), split(odd_now), rest_parts], axis=0), rest_parts)
-    even_now = even_now + second[:size]
-    odd_now = odd_now + second[size : 2 * size]
-    rest_parts = split(second[2 * size :])
-    third = product(jnp.concatenate([split(even_now), split(odd_now)], axis=0), rest_parts)
-    even[...] = even_now + third[:size]
-    odd[...] = odd_now + third[size:]
-    power[...] = rest_parts
+    size = diag_one.shape[0]
+    skews, skews_parts, squares = [], [], []
+    for gram_now in grams_now:
+        diag_part = jnp.where(on_diag, gram_now, 0.0)
+        across = jnp.sum(diag_part, axis=1, keepdims=True)
+        down = jnp.sum(diag_part, axis=0, keepdims=True)
+        skews.append(gram_now * (across - down) / (2.0 * (across * across + down * down)))
+    for skew in skews:
+        skews_parts.append(split(skew))
+        squares.append(product(skews_parts[-1], skews_parts[-1]))
+    evens, odds, rests, worst = [], [], [], None
+    for skew, parts, square in zip(skews, skews_parts, squares):
+        bound = jnp.sqrt(0.5 * total(square * square))
+        scale = 2.0 / (2.0 + bound)
+        rate = bound / (2.0 + bound)
+        worst = rate if worst is None else jnp.maximum(worst, rate)
+        rest = (1.0 - scale) * diag_one + scale * square
+        rest_parts = split(rest)
+        first = product(jnp.concatenate([parts, rest_parts], axis=0), rest_parts)
+        evens.append(scale * (diag_one + rest))
+        odds.append(scale * (skew + first[:size]))
+        rests.append(split(first[size:]))
+    for index, rest_parts in enumerate(rests):
+        stack = jnp.concatenate([split(evens[index]), split(odds[index]), rest_parts], axis=0)
+        second = product(stack, rest_parts)
+        evens[index] = evens[index] + second[:size]
+        odds[index] = odds[index] + second[size : 2 * size]
+        rests[index] = split(second[2 * size :])
+    for index, rest_parts in enumerate(rests):
+        third = product(jnp.concatenate([split(evens[index]), split(odds[index])], axis=0), rest_parts)
+        even[index] = evens[index] + third[:size]
+        odd[index] = odds[index] + third[size:]
+        power[index] = rest_parts
 
     def more(left):
         return left > TOLERANCE
 
     def step(left):
-        old = power[...]
-        parts = split(product(old, old))
-        power[...] = parts
-        even[...] += product(split(even[...]), parts)
-        odd[...] += product(split(odd[...]), parts)
+        for index in range(len(grams_now)):
+            old = power[index]
+            parts = split(product(old, old))
+            power[index] = parts
+            even[index] += product(split(even[index]), parts)
+            odd[index] += product(split(odd[index]), parts)
         return left * left
 
-    rate = rate * rate
-    rate = rate * rate
-    lax.while_loop(more, step, (rate * rate)[0, 0])
-    even_now = 2.0 * even[...] - diag_one
-    odd_now = 2.0 * odd[...]
-    return split(even_now - odd_now), split(even_now + odd_now)
-
-
-def solve_kernel(count, *refs):
-    parts, out, even, odd, power = refs[:count], *refs[count:]
+    worst = worst * worst
+    worst = worst * worst
+    lax.while_loop(more, step, (worst * worst)[0, 0])
+    results = []
+    for index in range(len(grams_now)):
+        even_now = 2.0 * even[index] - diag_one
+        odd_now = 2.0 * odd[index]
+        results.append((split(even_now - odd_now), split(even_now + odd_now)))
+    return results
+
+
+def solve_kernel(count, row, *refs):
+    parts, out, sums, held, even, odd, power = refs[:count], *refs[count:]
     on_diag = unit(WIDTH)
+    pairs = range(out.shape[0])
+    each = parts[0].shape[0]
+    for by, part in enumerate(parts):
+        held[pl.ds(jnp.bitwise_xor(jnp.bitwise_and(row[0], count - 1), by) * each, each)] = part[...]
     off_total = jnp.zeros((1, 1), jnp.float32)
     diag_total = jnp.zeros((1, 1), jnp.float32)
-    for pair in range(parts[0].shape[0]):
-        gram = parts[0][pair]
-        for part in parts[1:]:
-            gram = gram + part[pair]
-        if gram.shape[0] != WIDTH:
-            gram = unpack(gram)
-        squares = gram * gram
+    now = []
+    for pair in pairs:
+        gram_now = held[pair]
+        if gram_now.shape[0] != WIDTH:
+            gram_now = unpack(gram_now)
+        squares = gram_now * gram_now
         off_total += total(jnp.where(on_diag, 0.0, squares))
         diag_total += total(jnp.where(on_diag, squares, 0.0))
-        so_far = None
-        for sweep in range(ITERS):
-            turn, back = rotation(gram, on_diag, even, odd, power)
-            if sweep < ITERS - 1:
-                gram = product(back, split(product(split(gram), turn)))
-            so_far = turn if so_far is None else split(product(so_far, turn))
-        rows = slice(pair * WIDTH, (pair + 1) * WIDTH)
-        out[rows] = so_far[:, :WIDTH].astype(jnp.float32) + so_far[:, WIDTH:].astype(jnp.float32)
-    first_lane = lax.broadcasted_iota(jnp.int32, (LAST_ROWS, WIDTH), 1) == 0
-    out[-LAST_ROWS:] = jnp.where(first_lane, off_total, diag_total)
-
-
-def solve(parts):
-    pairs = parts[0].shape[0]
+        now.append(gram_now)
+    first_lane = lax.broadcasted_iota(jnp.int32, sums.shape, 1) == 0
+    sums[...] = jnp.where(first_lane, off_total, diag_total)
+    so_far = None
+    for sweep in range(ITERS):
+        turns = rotations(now, on_diag, even, odd, power)
+        if sweep < ITERS - 1:
+            halves = [split(product(split(now[pair]), turns[pair][0])) for pair in pairs]
+            now = [product(turns[pair][1], halves[pair]) for pair in pairs]
+        if so_far is None:
+            so_far = [turns[pair][0] for pair in pairs]
+        elif sweep < ITERS - 1:
+            so_far = [split(product(so_far[pair], turns[pair][0])) for pair in pairs]
+        else:
+            for pair in pairs:
+                out[pair] = product(so_far[pair], turns[pair][0])
+
+
+def solve(row, parts):
+    each, height, _ = parts[0].shape
+    pairs = each * len(parts)
     return pl.pallas_call(
         functools.partial(solve_kernel, len(parts)),
-        out_shape=jax.ShapeDtypeStruct((pairs * WIDTH + LAST_ROWS, WIDTH), jnp.float32),
-        in_specs=[VMEM] * len(parts),
-        out_specs=VMEM,
+        out_shape=(
+            jax.ShapeDtypeStruct((pairs, WIDTH, WIDTH), jnp.float32),
+            jax.ShapeDtypeStruct((LAST_ROWS, WIDTH), jnp.float32),
+        ),
+        in_specs=[SMEM] + [VMEM] * len(parts),
+        out_specs=(VMEM, VMEM),
         scratch_shapes=[
-            pltpu.VMEM((WIDTH, WIDTH), jnp.float32),
-            pltpu.VMEM((WIDTH, WIDTH), jnp.float32),
-            pltpu.VMEM((WIDTH, 2 * WIDTH), jnp.bfloat16),
+            pltpu.VMEM((pairs, height, WIDTH), jnp.float32),
+            pltpu.VMEM((pairs, WIDTH, WIDTH), jnp.float32),
+            pltpu.VMEM((pairs, WIDTH, WIDTH), jnp.float32),
+            pltpu.VMEM((pairs, WIDTH, 2 * WIDTH), jnp.bfloat16),
         ],
         compiler_params=PARAMS,
         name="solve",
-    )(*parts)
-
-
-def load_turns(where, turns, held):
-    count = len(turns)
-    each = (turns[0].shape[0] - LAST_ROWS) // WIDTH
-    for step in range(count):
-        start = jnp.bitwise_xor(where[1], step) * each
-        for pair in range(each):
-            held[start + pair] = turns[step][pair * WIDTH : (pair + 1) * WIDTH]
+    )(row, *parts)
 
 
 def turned(tracks, columns, held):
@@ -323,10 +341,9 @@
     return lambda index: product(split(results[index][0]), split(held[index]))
 
 
-def edge_kernel(tracks, count, where, *refs):
-    turns, columns = refs[:count], refs[count:-4]
-    up, down, sums, held = refs[-4:]
-    load_turns(where, turns, held)
+def edge_kernel(tracks, where, sums, held, *refs):
+    columns, near, far = refs[:-2], refs[-2], refs[-1]
+    odd = lax.rem(where[0], 2) == 1
     rows = columns[0].shape[1]
     half = rows // 2
     blocks = len(tracks[0][1])
@@ -337,53 +354,49 @@
     for block in range(blocks):
         span = slice(block * half, (block + 1) * half)
         one = last[block * rows : (block + 1) * rows]
-        up[span] = jnp.where(low_lanes, one[:half], pltpu.roll(one[half:], BLOCK, 1))
+        up = jnp.where(low_lanes, one[:half], pltpu.roll(one[half:], BLOCK, 1))
         one = first[block * rows : (block + 1) * rows]
-        down[span] = jnp.where(low_lanes, pltpu.roll(one[:half], BLOCK, 1), one[half:])
-    value = turns[0][-LAST_ROWS:]
-    for turn in turns[1:]:
-        value = value + turn[-LAST_ROWS:]
-    sums[...] = value
-
-
-def edges(tracks, where, columns, turns):
-    rows = columns[0].shape[1]
-    blocks = len(tracks[0][1])
-    pairs = sum(track[0] for track in tracks)
-    shape = jax.ShapeDtypeStruct((blocks * rows // 2, WIDTH), jnp.float32)
-    return pl.pallas_call(
-        functools.partial(edge_kernel, tracks, len(turns)),
-        out_shape=(shape, shape, jax.ShapeDtypeStruct((LAST_ROWS, WIDTH), jnp.float32)),
-        in_specs=[SMEM] + [VMEM] * (len(turns) + len(columns)),
-        out_specs=(VMEM,) * 3,
-        scratch_shapes=[pltpu.VMEM((pairs, WIDTH, WIDTH), jnp.float32)],
+        down = jnp.where(low_lanes, pltpu.roll(one[:half], BLOCK, 1), one[half:])
+        near[span] = jnp.where(odd, down, up)
+        far[span] = jnp.where(odd, up, down)
+    near[-LAST_ROWS:] = sums[...]
+
+
+def edges(tracks, where, sums, columns, turns):
+    half = len(tracks[0][1]) * columns[0].shape[1] // 2
+    return pl.pallas_call(
+        functools.partial(edge_kernel, tracks),
+        out_shape=tuple(jax.ShapeDtypeStruct((height, WIDTH), jnp.float32) for height in (half + LAST_ROWS, half)),
+        in_specs=[SMEM] + [VMEM] * (2 + len(columns)),
+        out_specs=(VMEM,) * 2,
         compiler_params=PARAMS,
         name="edges",
-    )(where, *turns, *columns)
-
-
-def place_kernel(tracks, count, where, came_up, came_down, *refs):
-    turns, columns = refs[:count], refs[count:-2]
-    out, held = refs[-2:]
-    load_turns(where, turns, held)
+    )(where, sums, turns, *columns)
+
+
+def place_kernel(tracks, where, near, far, held, *refs):
+    columns, out = refs[:-1], refs[-1]
     pairs = held.shape[0]
     rows = columns[0].shape[1]
     half = rows // 2
     blocks = len(tracks[0][1])
+    odd = lax.rem(where[0], 2) == 1
     is_first = where[0] == 0
-    is_last = where[0] == where[2] - 1
+    is_last = where[0] == where[1] - 1
     low_lanes = lax.broadcasted_iota(jnp.int32, (rows, WIDTH), 1) < BLOCK
     result = turned(tracks, columns, held)
     rotated = [result(pair) for pair in range(pairs)]
     for block in range(blocks):
         span = slice(block * rows, (block + 1) * rows)
-        own_place = jnp.bitwise_xor(where[3], block)
+        own_place = jnp.bitwise_xor(where[2], block)
         own_rows = pl.ds(pl.multiple_of(own_place * rows, rows), rows)
-        place_up = jnp.bitwise_xor(own_place, where[4])
-        place_down = jnp.bitwise_xor(own_place, where[5])
-        arrived_up = came_up[pl.ds(pl.multiple_of(place_up * half, half), half)]
+        place_up = jnp.bitwise_xor(own_place, where[3])
+        place_down = jnp.bitwise_xor(own_place, where[4])
+        span_up = pl.ds(pl.multiple_of(place_up * half, half), half)
+        arrived_up = jnp.where(odd, near[span_up], far[span_up])
         arrived_up = jnp.concatenate([arrived_up, pltpu.roll(arrived_up, BLOCK, 1)], axis=0)
-        arrived_down = came_down[pl.ds(pl.multiple_of(place_down * half, half), half)]
+        span_down = pl.ds(pl.multiple_of(place_down * half, half), half)
+        arrived_down = jnp.where(odd, far[span_down], near[span_down])
         arrived_down = jnp.concatenate([pltpu.roll(arrived_down, BLOCK, 1), arrived_down], axis=0)
         for pair in range(pairs):
             if pair == 0:
@@ -399,44 +412,30 @@
             out[own_rows, pair * WIDTH : (pair + 1) * WIDTH] = jnp.where(low_lanes, upper, lower)
 
 
-def place(tracks, where, columns, came_up, came_down, turns):
+def place(tracks, where, columns, near, far, turns):
     rows = columns[0].shape[1]
     blocks = len(tracks[0][1])
     pairs = sum(track[0] for track in tracks)
     return pl.pallas_call(
-        functools.partial(place_kernel, tracks, len(turns)),
+        functools.partial(place_kernel, tracks),
         out_shape=jax.ShapeDtypeStruct((blocks * rows, pairs * WIDTH), jnp.float32),
-        in_specs=[SMEM] + [VMEM] * (2 + len(turns) + len(columns)),
+        in_specs=[SMEM] + [VMEM] * (3 + len(columns)),
         out_specs=VMEM,
-        scratch_shapes=[pltpu.VMEM((pairs, WIDTH, WIDTH), jnp.float32)],
         compiler_params=PARAMS,
         name="place",
-    )(where, came_up, came_down, *turns, *columns)
-
-
-def passed_along(value, axis, by):
-    count = lax.axis_size(axis)
-    pairs = [(i, i + by) for i in range(count) if 0 <= i + by < count]
+    )(where, near, far, turns, *columns)
+
+
+def swapped_in_twos(value, axis, first):
+    pairs = []
+    for i in range(first, lax.axis_size(axis) - 1, 2):
+        pairs += [(i, i + 1), (i + 1, i)]
     return lax.ppermute(value, axis, pairs)
 
 
 def swapped(value, axis, by):
     count = lax.axis_size(axis)
     return lax.ppermute(value, axis, [(i, i ^ by) for i in range(count)])
-
-
-def summed(value, axis, last):
-    count = lax.axis_size(axis)
-    if count & (count - 1):
-        return lax.psum(value, axis), last
-    step = 1
-    while step < count:
-        other = swapped(value, axis, step)
-        step *= 2
-        if step >= count:
-            value, other, last = lax.optimization_barrier((value, other, last))
-        value = value + other
-    return value, last
 
 
 def on_device(r_factor, block_slots):
@@ -445,9 +444,9 @@
     pair_index = lax.axis_index("pair")
     row_index = lax.axis_index("row")
     local = r_factor.shape[1] // WIDTH // pair_count
-    shared = local % row_count == 0 and row_count & (row_count - 1) == 0
-    shares = row_count if shared else 1
-    row = (row_index if shared else jnp.zeros_like(row_index)).astype(jnp.int32).reshape(1)
+    shared = local % 2 == 0 and row_count > 1 and row_count & (row_count - 1) == 0
+    shares = 2 if shared else 1
+    row = row_index.astype(jnp.int32).reshape(1)
     base = pair_index.astype(jnp.int32).reshape(1)
     if shared and pair_count == 8:
         plan = [(local, 0, local, (position,)) for position in range(pair_count)]
@@ -458,12 +457,11 @@
         here_four = swapped(here[2], "pair", 4)
         own, *given = near_grams(here, near)
         taken = [swapped(value, "pair", by) for by, value in zip((2, 4, 6), given)]
-        on_two, on_four = joined((near[1], here[3]), (near[2], near[3]))
-        here_two, here_four, on_two, on_four, taken = lax.optimization_barrier((here_two, here_four, on_two, on_four, taken))
+        (on_six,) = joined((here[3], near[3]))
+        here_two, here_four, on_six, taken = lax.optimization_barrier((here_two, here_four, on_six, taken))
         parts = merge(row, [own] + taken, shares)
-        from_two = swapped(on_two, "pair", 2)
-        from_four = swapped(on_four, "pair", 4)
-        tracks = ((local, tuple((position, 0) for position in range(pair_count))),)
+        from_six = swapped(on_six, "pair", 6)
+        tracks = ((local, tuple((position, 0) for position in range(pair_count - 1)) + ((pair_count - 2, 1),)),)
         bases = (pair_index, pair_index - 1, pair_index + 1)
     else:
         (arranged,) = gather(r_factor, block_slots, base, ((local, 0, local, None),))
@@ -473,22 +471,32 @@
         tracks = ((local, tuple((0, group) for group in range(pair_count))),)
         bases = (jnp.zeros_like(pair_index),) * 3
     if shared:
-        turn = solve([parts[0]] + [swapped(parts[by], "row", by) for by in range(1, row_count)])
+        half = parts[0] + swapped(parts[1], "row", 1)
         if pair_count == 8:
-            from_two, from_four, turn = lax.optimization_barrier((from_two, from_four, turn))
-            here_six = swapped(from_two[1:], "pair", 4)
-            near_six = swapped(from_four[1:], "pair", 2)
-            columns = (here[0], near[0], here_two, from_two, here_four, from_four, here_six, near_six)
-        turns = [turn] + [swapped(turn, "row", by) for by in range(1, row_count)]
+            near_two, near_four, half = lax.optimization_barrier((near[1], near[2], half))
+            near_two = swapped(near_two, "pair", 2)
+            near_four = swapped(near_four, "pair", 4)
+            columns = (here[0], near[0], here_two, near_two, here_four, near_four, from_six)
+        for bit in range(1, row_count.bit_length() - 1):
+            half = half + swapped(half, "row", 1 << bit)
+        parts = (half, swapped(half, "row", 1))
     else:
-        turns = [solve([lax.psum(parts[0], "row")])]
+        parts = (lax.psum(parts[0], "row"),)
+    turns, sums = solve(row, parts)
     bases = [jnp.clip(value, 0, pair_count - 1) for value in bases]
-    where = jnp.stack([pair_index, row[0], jnp.int32(pair_count)] + bases).astype(jnp.int32)
-    up, down, sums = edges(tracks, where, columns, turns)
-    came_up = passed_along(up, "pair", 1)
-    came_down = passed_along(down, "pair", -1)
-    rotated = place(tracks, where, columns, came_up, came_down, turns)
-    sums, rotated = summed(sums, "pair", rotated)
+    where = jnp.stack([pair_index, jnp.int32(pair_count)] + bases).astype(jnp.int32)
+    near, far = edges(tracks, where, sums, columns, turns)
+    far = swapped_in_twos(far, "pair", 1)
+    near = swapped_in_twos(near, "pair", 0)
+    rotated = place(tracks, where, columns, near, far, turns)
+    if pair_count == 8:
+        sums = sums + near[-LAST_ROWS:]
+        others = [swapped(sums, "pair", by) for by in (2, 4, 6)]
+        others, rotated = lax.optimization_barrier((others, rotated))
+        for other in others:
+            sums = sums + other
+    else:
+        sums = lax.psum(sums, "pair")
     off_ratio = jnp.sqrt(sums[0, 0] / sums[0, 1])
     return (rotated, off_ratio)
 

time: 69 us -> 63.7 us (0.923)
  the two profiles are of different devices: /device:TPU:0 before, /device:TPU:28 now
where the time goes in v3:
time: 63.7 us; the launch traced here: 63.5 us
  waiting for transfers between devices  27.5 us (43%)
  starting transfers between devices  18 us (28%)
  Pallas kernels  11.8 us (19%)
  between operations  3.32 us (5%)
  local copies, waits for them, and re-layouts  2.91 us (5%)
    ppermute x18, waiting for transfers between devices, swapped(): return lax.ppermute(value, axis, [(i, i ^ by) for i in range(count)])  23.1 us
    ppermute x18, starting transfers between devices, swapped(): return lax.ppermute(value, axis, [(i, i ^ by) for i in range(count)])  14.7 us
    pallas_call x1, Pallas kernels, solve(): pl.pallas_call(functools.partial(solve_kernel, len(parts)), out_shape=(ja...  5.3 us
    ppermute x2, waiting for transfers between devices, swapped_in_twos(): return lax.ppermute(value, axis, pairs)  4.43 us
    ppermute x2, starting transfers between devices, swapped_in_twos(): return lax.ppermute(value, axis, pairs)  3.32 us
    pallas_call x1, Pallas kernels, place(): pl.pallas_call(functools.partial(place_kernel, tracks), out_shape=jax.Sha...  2.76 us
    unnamed x4, local copies, waits for them, and re-layouts  2.24 us
    pallas_call x1, Pallas kernels, gather(): pl.pallas_call(functools.partial(gather_kernel, tuple(((local, first, pos...  1.7 us
  transfers between devices with their start and end apart: 20, of which 8 were waited for; matrix products, arithmetic and copies ran while one was open for 0% of the time, Pallas kernels for 14%

profile of v3, /device:TPU:28, one launch (start us, length us, event | category | flops | bytes accessed | tf_op | source)
XLA Modules:
  0.0 63.5 jit_solution(18152890351080106904)
XLA Ops:
  0.6 0.0 copy-start
  0.6 1.6 %copy-done = f32[128,4096]{1,0:T(8,128)S(1)} copy-done((f32[128,4096]{1,0:T(8,128)S(1)}, f32[128,4096]{1,0:T(8,128)}, u32[]{:S(2)}) %copy-start) | copy-done | bytes 2097176
  2.2 0.0 copy-start.1
  2.2 0.7 %copy-done.1 = s32[64]{0:T(128)S(1)} copy-done((s32[64]{0:T(128)S(1)}, s32[64]{0:T(128)}, u32[]{:S(2)}) %copy-start.1) | copy-done | bytes 280
  2.9 1.7 %gather.1 = (f32[1,128,512]{2,1,0:T(8,128)S(1)}, f32[1,128,512]{2,1,0:T(8,128)S(1)}, f32[1,128,512]{2,1,0:T(8,128)S(1)}, f32[1,128,512]{2,1,0:T(8,128)S(1)}, f32...) custom-call(s32[64]{0:T(128)S(1)} %copy-done.1, ...), custom_call_target="tpu_custom_call" | custom-call | tf_op jit(solution)/shard_map/gather/pallas_call | solution.py:81
  4.6 0.1 collective-permute-start
  4.7 0.5 collective-permute-start.1
  5.2 0.1 collective-permute-start.2
  5.2 0.4 collective-permute-start.3
  5.7 1.5 %collective-permute-start.4 = (f32[1,128,512]{2,1,0:T(8,128)S(1)}, f32[1,128,512]{2,1,0:T(8,128)S(1)}, u32[]{:S(2)}, u32[]{:S(2)}) collective-permute-start(f32[1,128,512]{2,1,0:T(8,128)S(1)} %get-tuple-element.36.refs_1_), channel_id=1, source_target_pairs={{0,8},{4,12},{8,0},{12,4},{16,24},{20,28},{24,16},{28,20},{1,9},{5... | collective-permute-start | bytes 786440 | tf_op jit(solution)/shard_map/ppermute | solution.py:438
  7.2 0.0 collective-permute-done.refs_5_
  7.2 0.5 collective-permute-start.5
  7.7 0.0 collective-permute-done.1.refs_6_
  7.7 0.0 collective-permute-done.2.refs_4_.refs_1_
  7.7 0.0 collective-permute-done.3.refs_7_.refs_1_
  7.7 0.9 %near_grams.1 = (f32[4,72,128]{2,1,0:T(8,128)S(1)}, f32[4,72,128]{2,1,0:T(8,128)S(1)}, f32[4,72,128]{2,1,0:T(8,128)S(1)}, f32[4,72,128]{2,1,0:T(8,128)S(1)}) custom-call(f32[1,128,512]{2,1,0:T(8,128)S(1)} %get-tuple-element.35.refs_0_, f32[1,128,512]{2,1,0:T(8,128)S(1)} %get-tuple-element.36.refs_1_, f32[1,128,512]{2,1,0:T(8,128)S(1)} %get-tuple-element.37.refs_2_, ...), custom_call_target="tpu_custom_call" | custom-call | tf_op jit(solution)/shard_map/near_grams/pallas_call | solution.py:168
  8.6 1.2 %collective-permute-start.6 = (f32[4,72,128]{2,1,0:T(8,128)S(1)}, f32[4,72,128]{2,1,0:T(8,128)S(1)}, u32[]{:S(2)}, u32[]{:S(2)}) collective-permute-start(f32[4,72,128]{2,1,0:T(8,128)S(1)} %get-tuple-element.42), channel_id=1, source_target_pairs={{0,8},{4,12},{8,0},{12,4},{16,24},{20,28},{24,16},{28,20},{1,9},{5... | collective-permute-start | bytes 442376 | tf_op jit(solution)/shard_map/ppermute | solution.py:438
  9.7 0.9 %collective-permute-start.7 = (f32[4,72,128]{2,1,0:T(8,128)S(1)}, f32[4,72,128]{2,1,0:T(8,128)S(1)}, u32[]{:S(2)}, u32[]{:S(2)}) collective-permute-start(f32[4,72,128]{2,1,0:T(8,128)S(1)} %get-tuple-element.43), channel_id=1, source_target_pairs={{0,16},{4,20},{8,24},{12,28},{16,0},{20,4},{24,8},{28,12},{1,17},{... | collective-permute-start | bytes 442376 | tf_op jit(solution)/shard_map/ppermute | solution.py:438
  10.7 1.4 %collective-permute-start.8 = (f32[4,72,128]{2,1,0:T(8,128)S(1)}, f32[4,72,128]{2,1,0:T(8,128)S(1)}, u32[]{:S(2)}, u32[]{:S(2)}) collective-permute-start(f32[4,72,128]{2,1,0:T(8,128)S(1)} %get-tuple-element.44), channel_id=1, source_target_pairs={{0,24},{4,28},{8,16},{12,20},{16,8},{20,12},{24,0},{28,4},{1,25},{... | collective-permute-start | bytes 442376 | tf_op jit(solution)/shard_map/ppermute | solution.py:438
  12.1 2.7 %collective-permute-done.4.refs_2_ = f32[1,128,512]{2,1,0:T(8,128)S(1)} collective-permute-done((f32[1,128,512]{2,1,0:T(8,128)S(1)}, f32[1,128,512]{2,1,0:T(8,128)S(1)}, u32[]{:S(2)}, u32[]{:S(2)}) %collective-permute-start.4) | collective-permute-done | bytes 262176 | tf_op jit(solution)/shard_map/ppermute | solution.py:438
  14.8 1.7 %collective-permute-done.5.refs_4_ = f32[1,128,512]{2,1,0:T(8,128)S(1)} collective-permute-done((f32[1,128,512]{2,1,0:T(8,128)S(1)}, f32[1,128,512]{2,1,0:T(8,128)S(1)}, u32[]{:S(2)}, u32[]{:S(2)}) %collective-permute-start.5) | collective-permute-done | bytes 262176 | tf_op jit(solution)/shard_map/ppermute | solution.py:438
  16.5 1.5 %collective-permute-done.6.refs_1_ = f32[4,72,128]{2,1,0:T(8,128)S(1)} collective-permute-done((f32[4,72,128]{2,1,0:T(8,128)S(1)}, f32[4,72,128]{2,1,0:T(8,128)S(1)}, u32[]{:S(2)}, u32[]{:S(2)}) %collective-permute-start.6) | collective-permute-done | bytes 147488 | tf_op jit(solution)/shard_map/ppermute | solution.py:438
  18.0 3.5 %collective-permute-done.7.refs_2_ = f32[4,72,128]{2,1,0:T(8,128)S(1)} collective-permute-done((f32[4,72,128]{2,1,0:T(8,128)S(1)}, f32[4,72,128]{2,1,0:T(8,128)S(1)}, u32[]{:S(2)}, u32[]{:S(2)}) %collective-permute-start.7) | collective-permute-done | bytes 147488 | tf_op jit(solution)/shard_map/ppermute | solution.py:438
  21.5 0.0 collective-permute-done.8.refs_3_
  21.5 1.2 %collective-permute-start.14 = (f32[2,128,512]{2,1,0:T(8,128)S(1)}, f32[2,128,512]{2,1,0:T(8,128)S(1)}, u32[]{:S(2)}, u32[]{:S(2)}) collective-permute-start(f32[2,128,512]{2,1,0:T(8,128)S(1)} %joined.1), channel_id=1, source_target_pairs={{0,24},{4,28},{8,16},{12,20},{16,8},{20,12},{24,0},{28,4},{1,25},{... | collective-permute-start | bytes 1572872 | tf_op jit(solution)/shard_map/ppermute | solution.py:438
  22.7 0.5 collective-permute-start.9
  23.2 3.9 %collective-permute-done.9 = f32[2,72,128]{2,1,0:T(8,128)S(1)} collective-permute-done((f32[2,72,128]{2,1,0:T(8,128)S(1)}, f32[2,72,128]{2,1,0:T(8,128)S(1)}, u32[]{:S(2)}, u32[]{:S(2)}) %collective-permute-start.9) | collective-permute-done | bytes 73760 | tf_op jit(solution)/shard_map/ppermute | solution.py:438
  27.2 0.9 %collective-permute-start.12 = (f32[1,128,512]{2,1,0:T(8,128)S(1)}, f32[1,128,512]{2,1,0:T(8,128)S(1)}, u32[]{:S(2)}, u32[]{:S(2)}) collective-permute-start(f32[1,128,512]{2,1,0:T(8,128)S(1)} %collective-permute-done.refs_5_), channel_id=1, source_target_pairs={{0,8},{4,12},{8,0},{12,4},{16,24},{20,28},{24,16},{28,20},{1,9},{5... | collective-permute-start | bytes 786440 | tf_op jit(solution)/shard_map/ppermute | solution.py:438
  28.0 1.5 %collective-permute-start.13 = (f32[1,128,512]{2,1,0:T(8,128)S(1)}, f32[1,128,512]{2,1,0:T(8,128)S(1)}, u32[]{:S(2)}, u32[]{:S(2)}) collective-permute-start(f32[1,128,512]{2,1,0:T(8,128)S(1)} %collective-permute-done.1.refs_6_), channel_id=1, source_target_pairs={{0,16},{4,20},{8,24},{12,28},{16,0},{20,4},{24,8},{28,12},{1,17},{... | collective-permute-start | bytes 786440 | tf_op jit(solution)/shard_map/ppermute | solution.py:438
  29.5 0.3 collective-permute-start.10
  29.9 5.6 %collective-permute-done.10 = f32[2,72,128]{2,1,0:T(8,128)S(1)} collective-permute-done((f32[2,72,128]{2,1,0:T(8,128)S(1)}, f32[2,72,128]{2,1,0:T(8,128)S(1)}, u32[]{:S(2)}, u32[]{:S(2)}) %collective-permute-start.10) | collective-permute-done | bytes 73760 | tf_op jit(solution)/shard_map/ppermute | solution.py:438
  35.5 0.1 collective-permute-start.11
  35.6 0.1 stack.16.where
  35.7 4.2 %collective-permute-done.11.refs_1_ = f32[2,72,128]{2,1,0:T(8,128)S(1)} collective-permute-done((f32[2,72,128]{2,1,0:T(8,128)S(1)}, f32[2,72,128]{2,1,0:T(8,128)S(1)}, u32[]{:S(2)}, u32[]{:S(2)}) %collective-permute-start.11) | collective-permute-done | bytes 73760 | tf_op jit(solution)/shard_map/ppermute | solution.py:438
  39.9 5.3 %solve.1 = (f32[4,128,128]{2,1,0:T(8,128)S(1)}, f32[8,128]{1,0:T(8,128)S(1)}) custom-call(s32[1]{0:T(128)} %bitcast.row, f32[2,72,128]{2,1,0:T(8,128)S(1)} %add.23.refs_0_, f32[2,72,128]{2,1,0:T(8,128)S(1)} %collective-permute-done.11.refs_1_), custom_call_target="tpu_custom_call" | custom-call | tf_op jit(solution)/shard_map/solve/pallas_call | solution.py:316
  45.2 0.0 collective-permute-done.12.refs_3_
  45.2 0.0 collective-permute-done.13.refs_5_
  45.2 0.0 collective-permute-done.14.refs_6_
  45.2 1.1 %edges.1 = (f32[520,128]{1,0:T(8,128)S(1)}, f32[512,128]{1,0:T(8,128)S(1)}) custom-call(s32[5]{0:T(128)S(1)} %stack.16.where, f32[8,128]{1,0:T(8,128)S(1)} %get-tuple-element.51.sums, f32[4,128,128]{2,1,0:T(8,128)S(1)} %get-tuple-element.52.held, f32[1,128,512]{2,1,0:T(8,128)S(1)} %get-tuple-element.35.refs_0_, ...), custom_call_target="tpu_custom_call" | custom-call | tf_op jit(solution)/shard_map/edges/pallas_call | solution.py:367
  46.3 0.1 collective-permute-start.15
  46.4 3.2 %collective-permute-start.19 = (f32[512,128]{1,0:T(8,128)S(1)}, f32[512,128]{1,0:T(8,128)S(1)}, u32[]{:S(2)}, u32[]{:S(2)}) collective-permute-start(f32[512,128]{1,0:T(8,128)S(1)} %get-tuple-element.59), channel_id=1, source_target_pairs={{4,8},{8,4},{12,16},{16,12},{20,24},{24,20},{5,9},{9,5},{13,17},{1... | collective-permute-start | bytes 786440 | tf_op jit(solution)/shard_map/ppermute | solution.py:433
  49.6 0.0 collective-permute-done.15.near
  49.7 0.8 %collective-permute-start.18 = (f32[8,128]{1,0:T(8,128)S(1)}, f32[8,128]{1,0:T(8,128)S(1)}, u32[]{:S(2)}, u32[]{:S(2)}) collective-permute-start(f32[8,128]{1,0:T(8,128)S(1)} %slice_add_fusion), channel_id=1, source_target_pairs={{0,24},{4,28},{8,16},{12,20},{16,8},{20,12},{24,0},{28,4},{1,25},{... | collective-permute-start | bytes 12296 | tf_op jit(solution)/shard_map/ppermute | solution.py:438
  50.5 1.5 %collective-permute-start.17 = (f32[8,128]{1,0:T(8,128)S(1)}, f32[8,128]{1,0:T(8,128)S(1)}, u32[]{:S(2)}, u32[]{:S(2)}) collective-permute-start(f32[8,128]{1,0:T(8,128)S(1)} %slice_add_fusion), channel_id=1, source_target_pairs={{0,16},{4,20},{8,24},{12,28},{16,0},{20,4},{24,8},{28,12},{1,17},{... | collective-permute-start | bytes 12296 | tf_op jit(solution)/shard_map/ppermute | solution.py:438
  52.0 1.2 %collective-permute-start.16 = (f32[8,128]{1,0:T(8,128)S(1)}, f32[8,128]{1,0:T(8,128)S(1)}, u32[]{:S(2)}, u32[]{:S(2)}) collective-permute-start(f32[8,128]{1,0:T(8,128)S(1)} %slice_add_fusion), channel_id=1, source_target_pairs={{0,8},{4,12},{8,0},{12,4},{16,24},{20,28},{24,16},{28,20},{1,9},{5... | collective-permute-start | bytes 12296 | tf_op jit(solution)/shard_map/ppermute | solution.py:438
  53.2 4.4 %collective-permute-done.19.far = f32[512,128]{1,0:T(8,128)S(1)} collective-permute-done((f32[512,128]{1,0:T(8,128)S(1)}, f32[512,128]{1,0:T(8,128)S(1)}, u32[]{:S(2)}, u32[]{:S(2)}) %collective-permute-start.19) | collective-permute-done | bytes 262176 | tf_op jit(solution)/shard_map/ppermute | solution.py:433
  57.6 2.8 %place.1 = f32[1024,512]{1,0:T(8,128)} custom-call(s32[5]{0:T(128)S(1)} %stack.16.where, f32[520,128]{1,0:T(8,128)S(1)} %collective-permute-done.15.near, f32[512,128]{1,0:T(8,128)S(1)} %collective-permute-done.19.far, f32[4,128,128]{2,1,0:T(8,128)S(1)} %get-tuple-element.52.held, f32[1,128,512]{2,1,0:T(8,128)S(1)} %get-tuple-element.35.refs_0_, ...), custom_call_target="tpu_custom_call" | custom-call | tf_op jit(solution)/shard_map/place/pallas_call | solution.py:419
  60.4 0.0 collective-permute-done.18
  60.4 0.0 collective-permute-done.17
  60.4 0.0 collective-permute-done.16
  60.4 0.6 fusion
  (6 shorter events, 0.1 us)
Async XLA Ops:
  0.6 1.6 %copy-start = (f32[128,4096]{1,0:T(8,128)S(1)}, f32[128,4096]{1,0:T(8,128)}, u32[]{:S(2)}) copy-start(f32[128,4096]{1,0:T(8,128)} %source.1) | copy-start | bytes 6291460
  2.2 0.7 %copy-start.1 = (s32[64]{0:T(128)S(1)}, s32[64]{0:T(128)}, u32[]{:S(2)}) copy-start(s32[64]{0:T(128)} %slots.1) | copy-start | bytes 772
  4.6 2.6 %collective-permute-start = (f32[1,128,512]{2,1,0:T(8,128)S(1)}, f32[1,128,512]{2,1,0:T(8,128)S(1)}, u32[]{:S(2)}, u32[]{:S(2)}) collective-permute-start(f32[1,128,512]{2,1,0:T(8,128)S(1)} %get-tuple-element.33), channel_id=1, source_target_pairs={{0,4},{4,0},{8,12},{12,8},{16,20},{20,16},{24,28},{28,24},{1,5},{5... | collective-permute-start | bytes 786440 | tf_op jit(solution)/shard_map/ppermute | solution.py:438
  4.7 3.0 %collective-permute-start.1 = (f32[1,128,512]{2,1,0:T(8,128)S(1)}, f32[1,128,512]{2,1,0:T(8,128)S(1)}, u32[]{:S(2)}, u32[]{:S(2)}) collective-permute-start(f32[1,128,512]{2,1,0:T(8,128)S(1)} %get-tuple-element.34), channel_id=1, source_target_pairs={{0,4},{4,0},{8,12},{12,8},{16,20},{20,16},{24,28},{28,24},{1,5},{5... | collective-permute-start | bytes 786440 | tf_op jit(solution)/shard_map/ppermute | solution.py:438
  5.2 2.5 %collective-permute-start.2 = (f32[1,128,512]{2,1,0:T(8,128)S(1)}, f32[1,128,512]{2,1,0:T(8,128)S(1)}, u32[]{:S(2)}, u32[]{:S(2)}) collective-permute-start(f32[1,128,512]{2,1,0:T(8,128)S(1)} %get-tuple-element.39), channel_id=1, source_target_pairs={{0,4},{4,0},{8,12},{12,8},{16,20},{20,16},{24,28},{28,24},{1,5},{5... | collective-permute-start | bytes 786440 | tf_op jit(solution)/shard_map/ppermute | solution.py:438
  5.2 2.4 %collective-permute-start.3 = (f32[1,128,512]{2,1,0:T(8,128)S(1)}, f32[1,128,512]{2,1,0:T(8,128)S(1)}, u32[]{:S(2)}, u32[]{:S(2)}) collective-permute-start(f32[1,128,512]{2,1,0:T(8,128)S(1)} %get-tuple-element.40), channel_id=1, source_target_pairs={{0,4},{4,0},{8,12},{12,8},{16,20},{20,16},{24,28},{28,24},{1,5},{5... | collective-permute-start | bytes 786440 | tf_op jit(solution)/shard_map/ppermute | solution.py:438
  5.7 9.2 %collective-permute-start.4 = (f32[1,128,512]{2,1,0:T(8,128)S(1)}, f32[1,128,512]{2,1,0:T(8,128)S(1)}, u32[]{:S(2)}, u32[]{:S(2)}) collective-permute-start(f32[1,128,512]{2,1,0:T(8,128)S(1)} %get-tuple-element.36.refs_1_), channel_id=1, source_target_pairs={{0,8},{4,12},{8,0},{12,4},{16,24},{20,28},{24,16},{28,20},{1,9},{5... | collective-permute-start | bytes 786440 | tf_op jit(solution)/shard_map/ppermute | solution.py:438
  7.2 9.4 %collective-permute-start.5 = (f32[1,128,512]{2,1,0:T(8,128)S(1)}, f32[1,128,512]{2,1,0:T(8,128)S(1)}, u32[]{:S(2)}, u32[]{:S(2)}) collective-permute-start(f32[1,128,512]{2,1,0:T(8,128)S(1)} %get-tuple-element.37.refs_2_), channel_id=1, source_target_pairs={{0,16},{4,20},{8,24},{12,28},{16,0},{20,4},{24,8},{28,12},{1,17},{... | collective-permute-start | bytes 786440 | tf_op jit(solution)/shard_map/ppermute | solution.py:438
  8.6 9.4 %collective-permute-start.6 = (f32[4,72,128]{2,1,0:T(8,128)S(1)}, f32[4,72,128]{2,1,0:T(8,128)S(1)}, u32[]{:S(2)}, u32[]{:S(2)}) collective-permute-start(f32[4,72,128]{2,1,0:T(8,128)S(1)} %get-tuple-element.42), channel_id=1, source_target_pairs={{0,8},{4,12},{8,0},{12,4},{16,24},{20,28},{24,16},{28,20},{1,9},{5... | collective-permute-start | bytes 442376 | tf_op jit(solution)/shard_map/ppermute | solution.py:438
  9.7 11.8 %collective-permute-start.7 = (f32[4,72,128]{2,1,0:T(8,128)S(1)}, f32[4,72,128]{2,1,0:T(8,128)S(1)}, u32[]{:S(2)}, u32[]{:S(2)}) collective-permute-start(f32[4,72,128]{2,1,0:T(8,128)S(1)} %get-tuple-element.43), channel_id=1, source_target_pairs={{0,16},{4,20},{8,24},{12,28},{16,0},{20,4},{24,8},{28,12},{1,17},{... | collective-permute-start | bytes 442376 | tf_op jit(solution)/shard_map/ppermute | solution.py:438
  10.7 10.8 %collective-permute-start.8 = (f32[4,72,128]{2,1,0:T(8,128)S(1)}, f32[4,72,128]{2,1,0:T(8,128)S(1)}, u32[]{:S(2)}, u32[]{:S(2)}) collective-permute-start(f32[4,72,128]{2,1,0:T(8,128)S(1)} %get-tuple-element.44), channel_id=1, source_target_pairs={{0,24},{4,28},{8,16},{12,20},{16,8},{20,12},{24,0},{28,4},{1,25},{... | collective-permute-start | bytes 442376 | tf_op jit(solution)/shard_map/ppermute | solution.py:438
  21.5 23.7 %collective-permute-start.14 = (f32[2,128,512]{2,1,0:T(8,128)S(1)}, f32[2,128,512]{2,1,0:T(8,128)S(1)}, u32[]{:S(2)}, u32[]{:S(2)}) collective-permute-start(f32[2,128,512]{2,1,0:T(8,128)S(1)} %joined.1), channel_id=1, source_target_pairs={{0,24},{4,28},{8,16},{12,20},{16,8},{20,12},{24,0},{28,4},{1,25},{... | collective-permute-start | bytes 1572872 | tf_op jit(solution)/shard_map/ppermute | solution.py:438
  22.7 4.4 %collective-permute-start.9 = (f32[2,72,128]{2,1,0:T(8,128)S(1)}, f32[2,72,128]{2,1,0:T(8,128)S(1)}, u32[]{:S(2)}, u32[]{:S(2)}) collective-permute-start(f32[2,72,128]{2,1,0:T(8,128)S(1)} %get-tuple-element.49), channel_id=1, source_target_pairs={{0,1},{1,0},{2,3},{3,2},{4,5},{5,4},{6,7},{7,6},{8,9},{9,8},{10,11... | collective-permute-start | bytes 221192 | tf_op jit(solution)/shard_map/ppermute | solution.py:438
  27.2 18.1 %collective-permute-start.12 = (f32[1,128,512]{2,1,0:T(8,128)S(1)}, f32[1,128,512]{2,1,0:T(8,128)S(1)}, u32[]{:S(2)}, u32[]{:S(2)}) collective-permute-start(f32[1,128,512]{2,1,0:T(8,128)S(1)} %collective-permute-done.refs_5_), channel_id=1, source_target_pairs={{0,8},{4,12},{8,0},{12,4},{16,24},{20,28},{24,16},{28,20},{1,9},{5... | collective-permute-start | bytes 786440 | tf_op jit(solution)/shard_map/ppermute | solution.py:438
  28.0 17.2 %collective-permute-start.13 = (f32[1,128,512]{2,1,0:T(8,128)S(1)}, f32[1,128,512]{2,1,0:T(8,128)S(1)}, u32[]{:S(2)}, u32[]{:S(2)}) collective-permute-start(f32[1,128,512]{2,1,0:T(8,128)S(1)} %collective-permute-done.1.refs_6_), channel_id=1, source_target_pairs={{0,16},{4,20},{8,24},{12,28},{16,0},{20,4},{24,8},{28,12},{1,17},{... | collective-permute-start | bytes 786440 | tf_op jit(solution)/shard_map/ppermute | solution.py:438
  29.5 5.9 %collective-permute-start.10 = (f32[2,72,128]{2,1,0:T(8,128)S(1)}, f32[2,72,128]{2,1,0:T(8,128)S(1)}, u32[]{:S(2)}, u32[]{:S(2)}) collective-permute-start(f32[2,72,128]{2,1,0:T(8,128)S(1)} %add.22), channel_id=1, source_target_pairs={{0,2},{1,3},{2,0},{3,1},{4,6},{5,7},{6,4},{7,5},{8,10},{9,11},{10,... | collective-permute-start | bytes 221192 | tf_op jit(solution)/shard_map/ppermute | solution.py:438
  35.5 4.4 %collective-permute-start.11 = (f32[2,72,128]{2,1,0:T(8,128)S(1)}, f32[2,72,128]{2,1,0:T(8,128)S(1)}, u32[]{:S(2)}, u32[]{:S(2)}) collective-permute-start(f32[2,72,128]{2,1,0:T(8,128)S(1)} %add.23.refs_0_), channel_id=1, source_target_pairs={{0,1},{1,0},{2,3},{3,2},{4,5},{5,4},{6,7},{7,6},{8,9},{9,8},{10,11... | collective-permute-start | bytes 221192 | tf_op jit(solution)/shard_map/ppermute | solution.py:438
  46.3 3.3 %collective-permute-start.15 = (f32[520,128]{1,0:T(8,128)S(1)}, f32[520,128]{1,0:T(8,128)S(1)}, u32[]{:S(2)}, u32[]{:S(2)}) collective-permute-start(f32[520,128]{1,0:T(8,128)S(1)} %get-tuple-element.58), channel_id=1, source_target_pairs={{0,4},{4,0},{8,12},{12,8},{16,20},{20,16},{24,28},{28,24},{1,5},{5... | collective-permute-start | bytes 798728 | tf_op jit(solution)/shard_map/ppermute | solution.py:433
  46.4 11.3 %collective-permute-start.19 = (f32[512,128]{1,0:T(8,128)S(1)}, f32[512,128]{1,0:T(8,128)S(1)}, u32[]{:S(2)}, u32[]{:S(2)}) collective-permute-start(f32[512,128]{1,0:T(8,128)S(1)} %get-tuple-element.59), channel_id=1, source_target_pairs={{4,8},{8,4},{12,16},{16,12},{20,24},{24,20},{5,9},{9,5},{13,17},{1... | collective-permute-start | bytes 786440 | tf_op jit(solution)/shard_map/ppermute | solution.py:433
  49.7 10.7 %collective-permute-start.18 = (f32[8,128]{1,0:T(8,128)S(1)}, f32[8,128]{1,0:T(8,128)S(1)}, u32[]{:S(2)}, u32[]{:S(2)}) collective-permute-start(f32[8,128]{1,0:T(8,128)S(1)} %slice_add_fusion), channel_id=1, source_target_pairs={{0,24},{4,28},{8,16},{12,20},{16,8},{20,12},{24,0},{28,4},{1,25},{... | collective-permute-start | bytes 12296 | tf_op jit(solution)/shard_map/ppermute | solution.py:438
  50.5 9.9 %collective-permute-start.17 = (f32[8,128]{1,0:T(8,128)S(1)}, f32[8,128]{1,0:T(8,128)S(1)}, u32[]{:S(2)}, u32[]{:S(2)}) collective-permute-start(f32[8,128]{1,0:T(8,128)S(1)} %slice_add_fusion), channel_id=1, source_target_pairs={{0,16},{4,20},{8,24},{12,28},{16,0},{20,4},{24,8},{28,12},{1,17},{... | collective-permute-start | bytes 12296 | tf_op jit(solution)/shard_map/ppermute | solution.py:438
  52.0 8.4 %collective-permute-start.16 = (f32[8,128]{1,0:T(8,128)S(1)}, f32[8,128]{1,0:T(8,128)S(1)}, u32[]{:S(2)}, u32[]{:S(2)}) collective-permute-start(f32[8,128]{1,0:T(8,128)S(1)} %slice_add_fusion), channel_id=1, source_target_pairs={{0,8},{4,12},{8,0},{12,4},{16,24},{20,28},{24,16},{28,20},{1,9},{5... | collective-permute-start | bytes 12296 | tf_op jit(solution)/shard_map/ppermute | solution.py:438

commit v4 on v3

--- a/solution.py
+++ b/solution.py
@@ -12,8 +12,11 @@
 ITERS = 3
 TOLERANCE = 1e-8
 LAST_ROWS = 8
+GATHER_CHUNKS = 2
+GATHER_VMEM = 62 * 1024 * 1024
 VMEM = pl.BlockSpec(memory_space=pltpu.VMEM)
 SMEM = pl.BlockSpec(memory_space=pltpu.SMEM)
+HBM = pl.BlockSpec(memory_space=pltpu.HBM)
 PARAMS = pltpu.CompilerParams(vmem_limit_bytes=48 * 1024 * 1024)
 
 
@@ -39,36 +42,41 @@
     return jnp.sum(jnp.sum(value, axis=1, keepdims=True), axis=0, keepdims=True)
 
 
-def gather_kernel(plan, slots, base, source, *outs):
+def gather_kernel(plan, slots, source, *outs):
     rows = source.shape[0]
     local = plan[0][0]
+    base = slots[slots.shape[0] - 1]
     low_lanes = lax.broadcasted_iota(jnp.int32, (rows, WIDTH), 1) < BLOCK
 
-    def tile(block, lane_half):
-        start = pl.multiple_of((block // 2) * WIDTH, WIDTH)
-        value = source[:, pl.ds(start, WIDTH)]
-        return jnp.where(block % 2 == lane_half, value, pltpu.roll(value, BLOCK, 1))
+    def tile(block):
+        return source[:, pl.ds(pl.multiple_of(lax.shift_right_logical(block, 1) * WIDTH, WIDTH), WIDTH)]
+
+    def one_pair(slot):
+        upper_block, lower_block = slots[slot], slots[slot + 1]
+        upper, lower = tile(upper_block), tile(lower_block)
+        turned_over = pltpu.roll(jnp.where(low_lanes, lower, upper), BLOCK, 1)
+        upper = jnp.where(jnp.bitwise_and(upper_block, 1) == 0, upper, turned_over)
+        lower = jnp.where(jnp.bitwise_and(lower_block, 1) == 1, lower, turned_over)
+        return jnp.where(low_lanes, upper, lower)
 
     for (_, first, positions), out in zip(plan, outs):
         count = out.shape[2] // WIDTH
 
-        def one(group, place, first=first, count=count, out=out):
+        def one_group(group, place, first=first, count=count, out=out):
             for pair in range(count):
-                slot = 2 * (group * local + first + pair)
-                upper = tile(slots[slot], 0)
-                lower = tile(slots[slot + 1], 1)
-                out[place, :, pair * WIDTH : (pair + 1) * WIDTH] = jnp.where(low_lanes, upper, lower)
+                value = one_pair(2 * (group * local + first + pair))
+                out[place, :, pair * WIDTH : (pair + 1) * WIDTH] = value
 
         if positions is None:
 
-            def step(group, carry, one=one):
-                one(group, group)
+            def step(group, carry, one_group=one_group):
+                one_group(group, group)
                 return carry
 
             lax.fori_loop(0, out.shape[0], step, 0)
         else:
             for place, position in enumerate(positions):
-                one(jnp.bitwise_xor(base[0], position), place)
+                one_group(jnp.bitwise_xor(base, position), place)
 
 
 def gather(r_factor, block_slots, base, plan):
@@ -81,11 +89,11 @@
     return pl.pallas_call(
         functools.partial(gather_kernel, tuple((local, first, positions) for local, first, _, positions in plan)),
         out_shape=tuple(shapes),
-        in_specs=[SMEM, SMEM, VMEM],
+        in_specs=[SMEM, VMEM],
         out_specs=(VMEM,) * len(shapes),
         compiler_params=PARAMS,
         name="gather",
-    )(block_slots, base, r_factor)
+    )(jnp.concatenate([block_slots, base]), r_factor)
 
 
 def gram(pieces):
@@ -374,8 +382,8 @@
     )(where, sums, turns, *columns)
 
 
-def place_kernel(tracks, where, near, far, held, *refs):
-    columns, out = refs[:-1], refs[-1]
+def place_kernel(tracks, where, near, held, *refs):
+    columns, out, mate = refs[:-2], refs[-2], refs[-1]
     pairs = held.shape[0]
     rows = columns[0].shape[1]
     half = rows // 2
@@ -390,40 +398,86 @@
         span = slice(block * rows, (block + 1) * rows)
         own_place = jnp.bitwise_xor(where[2], block)
         own_rows = pl.ds(pl.multiple_of(own_place * rows, rows), rows)
-        place_up = jnp.bitwise_xor(own_place, where[3])
-        place_down = jnp.bitwise_xor(own_place, where[4])
-        span_up = pl.ds(pl.multiple_of(place_up * half, half), half)
-        arrived_up = jnp.where(odd, near[span_up], far[span_up])
-        arrived_up = jnp.concatenate([arrived_up, pltpu.roll(arrived_up, BLOCK, 1)], axis=0)
-        span_down = pl.ds(pl.multiple_of(place_down * half, half), half)
-        arrived_down = jnp.where(odd, far[span_down], near[span_down])
-        arrived_down = jnp.concatenate([pltpu.roll(arrived_down, BLOCK, 1), arrived_down], axis=0)
+        there = jnp.bitwise_xor(own_place, jnp.where(odd, where[3], where[4]))
+        arrived = near[pl.ds(pl.multiple_of(there * half, half), half)]
+        moved = pltpu.roll(arrived, BLOCK, 1)
         for pair in range(pairs):
             if pair == 0:
-                upper = jnp.where(is_first, rotated[0][span], arrived_up)
+                upper = jnp.where(is_first, rotated[0][span], jnp.concatenate([arrived, moved], axis=0))
             else:
                 upper = rotated[pair - 1][span]
                 if pair == 1:
                     upper = jnp.where(is_first, pltpu.roll(upper, BLOCK, 1), upper)
             if pair == pairs - 1:
-                lower = jnp.where(is_last, pltpu.roll(rotated[pair][span], BLOCK, 1), arrived_down)
+                own = pltpu.roll(rotated[pair][span], BLOCK, 1)
+                lower = jnp.where(is_last, own, jnp.concatenate([moved, arrived], axis=0))
             else:
                 lower = rotated[pair + 1][span]
-            out[own_rows, pair * WIDTH : (pair + 1) * WIDTH] = jnp.where(low_lanes, upper, lower)
-
-
-def place(tracks, where, columns, near, far, turns):
-    rows = columns[0].shape[1]
-    blocks = len(tracks[0][1])
+            value = jnp.where(low_lanes, upper, lower)
+            out[own_rows, pair * WIDTH : (pair + 1) * WIDTH] = value
+            if pair == 0:
+                first = value
+            if pair == pairs - 1:
+                mate[span] = jnp.where(odd, value, first)
+
+
+def place(tracks, where, columns, near, turns):
+    height = len(tracks[0][1]) * columns[0].shape[1]
     pairs = sum(track[0] for track in tracks)
     return pl.pallas_call(
         functools.partial(place_kernel, tracks),
-        out_shape=jax.ShapeDtypeStruct((blocks * rows, pairs * WIDTH), jnp.float32),
-        in_specs=[SMEM] + [VMEM] * (3 + len(columns)),
-        out_specs=VMEM,
+        out_shape=(
+            jax.ShapeDtypeStruct((height, pairs * WIDTH), jnp.float32),
+            jax.ShapeDtypeStruct((height, WIDTH), jnp.float32),
+        ),
+        in_specs=[SMEM] + [VMEM] * (2 + len(columns)),
+        out_specs=(VMEM, VMEM),
         compiler_params=PARAMS,
         name="place",
-    )(where, near, far, turns, *columns)
+    )(where, near, turns, *columns)
+
+
+def finish_kernel(blocks, count, where, far, mate, *refs):
+    sums, (out, ratio, tile, sems) = refs[:count], refs[count + 1 :]
+    value = sums[0][...]
+    for other in sums[1:]:
+        value = value + other[...]
+    ratio[...] = jnp.sqrt(value[:1, :1] / value[:1, 1:2])
+    rows = mate.shape[0] // blocks
+    half = rows // 2
+    odd = lax.rem(where[0], 2) == 1
+    used = jnp.where(odd, where[0] < where[1] - 1, where[0] > 0)
+    lanes = lax.broadcasted_iota(jnp.int32, (rows, WIDTH), 1)
+    first_lane = jnp.where(used, jnp.where(odd, BLOCK, 0), WIDTH)
+    here = (lanes >= first_lane) & (lanes < first_lane + BLOCK)
+    column = pl.ds(pl.multiple_of(jnp.where(odd, out.shape[1] - WIDTH, 0), WIDTH), WIDTH)
+    copies = []
+    for block in range(blocks):
+        span = pl.ds(block * rows, rows)
+        own_place = jnp.bitwise_xor(where[2], block)
+        there = jnp.bitwise_xor(own_place, jnp.where(odd, where[4], where[3]))
+        arrived = far[pl.ds(pl.multiple_of(there * half, half), half)]
+        moved = pltpu.roll(arrived, BLOCK, 1)
+        both = jnp.concatenate([jnp.where(odd, moved, arrived), jnp.where(odd, arrived, moved)], axis=0)
+        tile[span] = jnp.where(here, both, mate[span])
+        own_rows = pl.ds(pl.multiple_of(own_place * rows, rows), rows)
+        copies.append(pltpu.make_async_copy(tile.at[span], out.at[own_rows, column], sems.at[block]))
+        copies[-1].start()
+    for copy in copies:
+        copy.wait()
+
+
+def finish(blocks, where, far, mate, sums, rotated):
+    return pl.pallas_call(
+        functools.partial(finish_kernel, blocks, len(sums)),
+        out_shape=(jax.ShapeDtypeStruct(rotated.shape, jnp.float32), jax.ShapeDtypeStruct((1, 1), jnp.float32)),
+        in_specs=[SMEM] + [VMEM] * (2 + len(sums)) + [HBM],
+        out_specs=(HBM, VMEM),
+        input_output_aliases={3 + len(sums): 0},
+        scratch_shapes=[pltpu.VMEM(mate.shape, jnp.float32), pltpu.SemaphoreType.DMA((blocks,))],
+        compiler_params=PARAMS,
+        name="finish",
+    )(where, far, mate, *sums, rotated)
 
 
 def swapped_in_twos(value, axis, first):
@@ -488,17 +542,14 @@
     near, far = edges(tracks, where, sums, columns, turns)
     far = swapped_in_twos(far, "pair", 1)
     near = swapped_in_twos(near, "pair", 0)
-    rotated = place(tracks, where, columns, near, far, turns)
+    rotated, mate = place(tracks, where, columns, near, turns)
     if pair_count == 8:
         sums = sums + near[-LAST_ROWS:]
-        others = [swapped(sums, "pair", by) for by in (2, 4, 6)]
-        others, rotated = lax.optimization_barrier((others, rotated))
-        for other in others:
-            sums = sums + other
+        sums = [sums] + [swapped(sums, "pair", by) for by in (2, 4, 6)]
     else:
-        sums = lax.psum(sums, "pair")
-    off_ratio = jnp.sqrt(sums[0, 0] / sums[0, 1])
-    return (rotated, off_ratio)
+        sums = [lax.psum(sums, "pair")]
+    rotated, off_ratio = finish(pair_count, where, far, mate, sums, rotated)
+    return (rotated, off_ratio.reshape(()))
 
 
 def solution(mesh):

time: 63.7 us -> 60.4 us (0.948)
  the two profiles are of different devices: /device:TPU:28 before, /device:TPU:0 now
where the time goes in v4:
time: 60.4 us; the launch traced here: 60.3 us
  starting transfers between devices  23.9 us (40%)
  waiting for transfers between devices  19.5 us (32%)
  Pallas kernels  13.7 us (23%)
  local copies, waits for them, and re-layouts  1.67 us (3%)
  other arithmetic  0.75 us (1%)
  between operations  0.73 us (1%)
    ppermute x18, starting transfers between devices, swapped(): return lax.ppermute(value, axis, [(i, i ^ by) for i in range(count)])  23.1 us
    ppermute x18, waiting for transfers between devices, swapped(): return lax.ppermute(value, axis, [(i, i ^ by) for i in range(count)])  18.7 us
    pallas_call x1, Pallas kernels, solve(): pl.pallas_call(functools.partial(solve_kernel, len(parts)), out_shape=(ja...  5.29 us
    pallas_call x1, Pallas kernels, place(): pl.pallas_call(functools.partial(place_kernel, tracks), out_shape=(jax.Sh...  2.8 us
    pallas_call x1, Pallas kernels, finish(): pl.pallas_call(functools.partial(finish_kernel, blocks, len(sums)), out_s...  1.98 us
    pallas_call x1, Pallas kernels, gather(): pl.pallas_call(functools.partial(gather_kernel, tuple(((local, first, pos...  1.6 us
    unnamed x2, local copies, waits for them, and re-layouts  1.59 us
  transfers between devices with their start and end apart: 20, of which 10 were waited for; matrix products, arithmetic and copies ran while one was open for 0% of the time, Pallas kernels for 15%

profile of v4, /device:TPU:0, one launch (start us, length us, event | category | flops | bytes accessed | tf_op | source)
XLA Modules:
  0.0 60.3 jit_solution(5311584151906250366)
XLA Ops:
  0.6 0.7 %pad_add_fusion.slots = s32[65]{0:T(128)S(1)} fusion(s32[1]{0:T(128)} %bitcast, s32[64]{0:T(128)} %param.3), kind=kLoop, calls=%fused_computation.1 | loop fusion | flops 65 | bytes 520 | tf_op jit(solution)/shard_map/concatenate | solution.py:96
  1.4 0.0 copy-start
  1.4 1.6 %copy-done = f32[128,4096]{1,0:T(8,128)S(1)} copy-done((f32[128,4096]{1,0:T(8,128)S(1)}, f32[128,4096]{1,0:T(8,128)}, u32[]{:S(2)}) %copy-start) | copy-done | bytes 2097176
  3.0 1.6 %gather.1 = (f32[1,128,512]{2,1,0:T(8,128)S(1)}, f32[1,128,512]{2,1,0:T(8,128)S(1)}, f32[1,128,512]{2,1,0:T(8,128)S(1)}, f32[1,128,512]{2,1,0:T(8,128)S(1)}, f32...) custom-call(s32[65]{0:T(128)S(1)} %pad_add_fusion.slots, ...), custom_call_target="tpu_custom_call" | custom-call | tf_op jit(solution)/shard_map/gather/pallas_call | solution.py:89
  4.6 0.5 collective-permute-start
  5.1 0.1 collective-permute-start.1
  5.2 0.4 collective-permute-start.2
  5.6 0.1 collective-permute-start.3
  5.7 2.9 %collective-permute-start.4 = (f32[1,128,512]{2,1,0:T(8,128)S(1)}, f32[1,128,512]{2,1,0:T(8,128)S(1)}, u32[]{:S(2)}, u32[]{:S(2)}) collective-permute-start(f32[1,128,512]{2,1,0:T(8,128)S(1)} %get-tuple-element.36.refs_1_), channel_id=1, source_target_pairs={{0,8},{4,12},{8,0},{12,4},{16,24},{20,28},{24,16},{28,20},{1,9},{5... | collective-permute-start | bytes 786440 | tf_op jit(solution)/shard_map/ppermute | solution.py:492
  8.6 0.0 collective-permute-done.refs_5_
  8.6 1.5 %collective-permute-start.5 = (f32[1,128,512]{2,1,0:T(8,128)S(1)}, f32[1,128,512]{2,1,0:T(8,128)S(1)}, u32[]{:S(2)}, u32[]{:S(2)}) collective-permute-start(f32[1,128,512]{2,1,0:T(8,128)S(1)} %get-tuple-element.37.refs_2_), channel_id=1, source_target_pairs={{0,16},{4,20},{8,24},{12,28},{16,0},{20,4},{24,8},{28,12},{1,17},{... | collective-permute-start | bytes 786440 | tf_op jit(solution)/shard_map/ppermute | solution.py:492
  10.1 0.0 collective-permute-done.1.refs_6_
  10.1 0.0 collective-permute-done.2.refs_4_.refs_1_
  10.1 0.0 collective-permute-done.3.refs_7_.refs_1_
  10.1 0.9 %near_grams.1 = (f32[4,72,128]{2,1,0:T(8,128)S(1)}, f32[4,72,128]{2,1,0:T(8,128)S(1)}, f32[4,72,128]{2,1,0:T(8,128)S(1)}, f32[4,72,128]{2,1,0:T(8,128)S(1)}) custom-call(f32[1,128,512]{2,1,0:T(8,128)S(1)} %get-tuple-element.35.refs_0_, f32[1,128,512]{2,1,0:T(8,128)S(1)} %get-tuple-element.36.refs_1_, f32[1,128,512]{2,1,0:T(8,128)S(1)} %get-tuple-element.37.refs_2_, ...), custom_call_target="tpu_custom_call" | custom-call | tf_op jit(solution)/shard_map/near_grams/pallas_call | solution.py:176
  11.0 0.6 collective-permute-start.6
  11.6 1.1 %collective-permute-start.7 = (f32[4,72,128]{2,1,0:T(8,128)S(1)}, f32[4,72,128]{2,1,0:T(8,128)S(1)}, u32[]{:S(2)}, u32[]{:S(2)}) collective-permute-start(f32[4,72,128]{2,1,0:T(8,128)S(1)} %get-tuple-element.43), channel_id=1, source_target_pairs={{0,16},{4,20},{8,24},{12,28},{16,0},{20,4},{24,8},{28,12},{1,17},{... | collective-permute-start | bytes 442376 | tf_op jit(solution)/shard_map/ppermute | solution.py:492
  12.7 1.9 %collective-permute-start.8 = (f32[4,72,128]{2,1,0:T(8,128)S(1)}, f32[4,72,128]{2,1,0:T(8,128)S(1)}, u32[]{:S(2)}, u32[]{:S(2)}) collective-permute-start(f32[4,72,128]{2,1,0:T(8,128)S(1)} %get-tuple-element.44), channel_id=1, source_target_pairs={{0,24},{4,28},{8,16},{12,20},{16,8},{20,12},{24,0},{28,4},{1,25},{... | collective-permute-start | bytes 442376 | tf_op jit(solution)/shard_map/ppermute | solution.py:492
  14.6 1.1 %collective-permute-done.4.refs_2_ = f32[1,128,512]{2,1,0:T(8,128)S(1)} collective-permute-done((f32[1,128,512]{2,1,0:T(8,128)S(1)}, f32[1,128,512]{2,1,0:T(8,128)S(1)}, u32[]{:S(2)}, u32[]{:S(2)}) %collective-permute-start.4) | collective-permute-done | bytes 262176 | tf_op jit(solution)/shard_map/ppermute | solution.py:492
  15.7 2.1 %collective-permute-done.5.refs_4_ = f32[1,128,512]{2,1,0:T(8,128)S(1)} collective-permute-done((f32[1,128,512]{2,1,0:T(8,128)S(1)}, f32[1,128,512]{2,1,0:T(8,128)S(1)}, u32[]{:S(2)}, u32[]{:S(2)}) %collective-permute-start.5) | collective-permute-done | bytes 262176 | tf_op jit(solution)/shard_map/ppermute | solution.py:492
  17.8 1.1 %collective-permute-done.6.refs_1_ = f32[4,72,128]{2,1,0:T(8,128)S(1)} collective-permute-done((f32[4,72,128]{2,1,0:T(8,128)S(1)}, f32[4,72,128]{2,1,0:T(8,128)S(1)}, u32[]{:S(2)}, u32[]{:S(2)}) %collective-permute-start.6) | collective-permute-done | bytes 147488 | tf_op jit(solution)/shard_map/ppermute | solution.py:492
  18.8 4.1 %collective-permute-done.7.refs_2_ = f32[4,72,128]{2,1,0:T(8,128)S(1)} collective-permute-done((f32[4,72,128]{2,1,0:T(8,128)S(1)}, f32[4,72,128]{2,1,0:T(8,128)S(1)}, u32[]{:S(2)}, u32[]{:S(2)}) %collective-permute-start.7) | collective-permute-done | bytes 147488 | tf_op jit(solution)/shard_map/ppermute | solution.py:492
  22.9 0.0 collective-permute-done.8.refs_3_
  22.9 1.8 %collective-permute-start.14 = (f32[2,128,512]{2,1,0:T(8,128)S(1)}, f32[2,128,512]{2,1,0:T(8,128)S(1)}, u32[]{:S(2)}, u32[]{:S(2)}) collective-permute-start(f32[2,128,512]{2,1,0:T(8,128)S(1)} %joined.1), channel_id=1, source_target_pairs={{0,24},{4,28},{8,16},{12,20},{16,8},{20,12},{24,0},{28,4},{1,25},{... | collective-permute-start | bytes 1572872 | tf_op jit(solution)/shard_map/ppermute | solution.py:492
  24.8 1.6 %collective-permute-start.9 = (f32[2,72,128]{2,1,0:T(8,128)S(1)}, f32[2,72,128]{2,1,0:T(8,128)S(1)}, u32[]{:S(2)}, u32[]{:S(2)}) collective-permute-start(f32[2,72,128]{2,1,0:T(8,128)S(1)} %get-tuple-element.49), channel_id=1, source_target_pairs={{0,1},{1,0},{2,3},{3,2},{4,5},{5,4},{6,7},{7,6},{8,9},{9,8},{10,11... | collective-permute-start | bytes 221192 | tf_op jit(solution)/shard_map/ppermute | solution.py:492
  26.4 2.8 %collective-permute-done.9 = f32[2,72,128]{2,1,0:T(8,128)S(1)} collective-permute-done((f32[2,72,128]{2,1,0:T(8,128)S(1)}, f32[2,72,128]{2,1,0:T(8,128)S(1)}, u32[]{:S(2)}, u32[]{:S(2)}) %collective-permute-start.9) | collective-permute-done | bytes 73760 | tf_op jit(solution)/shard_map/ppermute | solution.py:492
  29.2 1.2 %collective-permute-start.12 = (f32[1,128,512]{2,1,0:T(8,128)S(1)}, f32[1,128,512]{2,1,0:T(8,128)S(1)}, u32[]{:S(2)}, u32[]{:S(2)}) collective-permute-start(f32[1,128,512]{2,1,0:T(8,128)S(1)} %collective-permute-done.refs_5_), channel_id=1, source_target_pairs={{0,8},{4,12},{8,0},{12,4},{16,24},{20,28},{24,16},{28,20},{1,9},{5... | collective-permute-start | bytes 786440 | tf_op jit(solution)/shard_map/ppermute | solution.py:492
  30.5 0.5 collective-permute-start.13
  31.0 2.6 %collective-permute-start.10 = (f32[2,72,128]{2,1,0:T(8,128)S(1)}, f32[2,72,128]{2,1,0:T(8,128)S(1)}, u32[]{:S(2)}, u32[]{:S(2)}) collective-permute-start(f32[2,72,128]{2,1,0:T(8,128)S(1)} %add.14), channel_id=1, source_target_pairs={{0,2},{1,3},{2,0},{3,1},{4,6},{5,7},{6,4},{7,5},{8,10},{9,11},{10,... | collective-permute-start | bytes 221192 | tf_op jit(solution)/shard_map/ppermute | solution.py:492
  33.5 2.8 %collective-permute-done.10 = f32[2,72,128]{2,1,0:T(8,128)S(1)} collective-permute-done((f32[2,72,128]{2,1,0:T(8,128)S(1)}, f32[2,72,128]{2,1,0:T(8,128)S(1)}, u32[]{:S(2)}, u32[]{:S(2)}) %collective-permute-start.10) | collective-permute-done | bytes 73760 | tf_op jit(solution)/shard_map/ppermute | solution.py:492
  36.3 1.5 %collective-permute-start.11 = (f32[2,72,128]{2,1,0:T(8,128)S(1)}, f32[2,72,128]{2,1,0:T(8,128)S(1)}, u32[]{:S(2)}, u32[]{:S(2)}) collective-permute-start(f32[2,72,128]{2,1,0:T(8,128)S(1)} %add.15.refs_0_), channel_id=1, source_target_pairs={{0,1},{1,0},{2,3},{3,2},{4,5},{5,4},{6,7},{7,6},{8,9},{9,8},{10,11... | collective-permute-start | bytes 221192 | tf_op jit(solution)/shard_map/ppermute | solution.py:492
  37.9 0.1 stack.19.where
  38.0 2.8 %collective-permute-done.11.refs_1_ = f32[2,72,128]{2,1,0:T(8,128)S(1)} collective-permute-done((f32[2,72,128]{2,1,0:T(8,128)S(1)}, f32[2,72,128]{2,1,0:T(8,128)S(1)}, u32[]{:S(2)}, u32[]{:S(2)}) %collective-permute-start.11) | collective-permute-done | bytes 73760 | tf_op jit(solution)/shard_map/ppermute | solution.py:492
  40.8 5.3 %solve.1 = (f32[4,128,128]{2,1,0:T(8,128)S(1)}, f32[8,128]{1,0:T(8,128)S(1)}) custom-call(s32[1]{0:T(128)} %bitcast.4.row, f32[2,72,128]{2,1,0:T(8,128)S(1)} %add.15.refs_0_, f32[2,72,128]{2,1,0:T(8,128)S(1)} %collective-permute-done.11.refs_1_), custom_call_target="tpu_custom_call" | custom-call | tf_op jit(solution)/shard_map/solve/pallas_call | solution.py:324
  46.1 0.0 collective-permute-done.12.refs_3_
  46.1 0.0 collective-permute-done.13.refs_5_
  46.1 0.0 collective-permute-done.14.refs_6_
  46.1 1.1 %edges.1 = (f32[520,128]{1,0:T(8,128)S(1)}, f32[512,128]{1,0:T(8,128)S(1)}) custom-call(s32[5]{0:T(128)S(1)} %stack.19.where, f32[8,128]{1,0:T(8,128)S(1)} %get-tuple-element.51.sums, f32[4,128,128]{2,1,0:T(8,128)S(1)} %get-tuple-element.52.held, f32[1,128,512]{2,1,0:T(8,128)S(1)} %get-tuple-element.35.refs_0_, ...), custom_call_target="tpu_custom_call" | custom-call | tf_op jit(solution)/shard_map/edges/pallas_call | solution.py:375
  47.2 0.1 collective-permute-start.16
  47.2 0.7 %collective-permute-start.15 = (f32[512,128]{1,0:T(8,128)S(1)}, f32[512,128]{1,0:T(8,128)S(1)}, u32[]{:S(2)}, u32[]{:S(2)}) collective-permute-start(f32[512,128]{1,0:T(8,128)S(1)} %get-tuple-element.58), channel_id=1, source_target_pairs={{4,8},{8,4},{12,16},{16,12},{20,24},{24,20},{5,9},{9,5},{13,17},{1... | collective-permute-start | bytes 786440 | tf_op jit(solution)/shard_map/ppermute | solution.py:487
  47.9 0.8 %collective-permute-done.16.near = f32[520,128]{1,0:T(8,128)S(1)} collective-permute-done((f32[520,128]{1,0:T(8,128)S(1)}, f32[520,128]{1,0:T(8,128)S(1)}, u32[]{:S(2)}, u32[]{:S(2)}) %collective-permute-start.16) | collective-permute-done | bytes 266272 | tf_op jit(solution)/shard_map/ppermute | solution.py:487
  48.8 3.6 %collective-permute-start.19 = (f32[8,128]{1,0:T(8,128)S(1)}, f32[8,128]{1,0:T(8,128)S(1)}, u32[]{:S(2)}, u32[]{:S(2)}) collective-permute-start(f32[8,128]{1,0:T(8,128)S(1)} %slice_add_fusion.refs_0_), channel_id=1, source_target_pairs={{0,24},{4,28},{8,16},{12,20},{16,8},{20,12},{24,0},{28,4},{1,25},{... | collective-permute-start | bytes 12296 | tf_op jit(solution)/shard_map/ppermute | solution.py:492
  52.4 0.4 collective-permute-start.18
  52.8 0.7 %collective-permute-start.17 = (f32[8,128]{1,0:T(8,128)S(1)}, f32[8,128]{1,0:T(8,128)S(1)}, u32[]{:S(2)}, u32[]{:S(2)}) collective-permute-start(f32[8,128]{1,0:T(8,128)S(1)} %slice_add_fusion.refs_0_), channel_id=1, source_target_pairs={{0,8},{4,12},{8,0},{12,4},{16,24},{20,28},{24,16},{28,20},{1,9},{5... | collective-permute-start | bytes 12296 | tf_op jit(solution)/shard_map/ppermute | solution.py:492
  53.5 2.8 %place.1 = (f32[1024,512]{1,0:T(8,128)}, f32[1024,128]{1,0:T(8,128)S(1)}) custom-call(s32[5]{0:T(128)S(1)} %stack.19.where, f32[520,128]{1,0:T(8,128)S(1)} %collective-permute-done.16.near, f32[4,128,128]{2,1,0:T(8,128)S(1)} %get-tuple-element.52.held, f32[1,128,512]{2,1,0:T(8,128)S(1)} %get-tuple-element.35.refs_0_, ...), custom_call_target="tpu_custom_call" | custom-call | tf_op jit(solution)/shard_map/place/pallas_call | solution.py:427
  56.3 0.0 collective-permute-done.15.far
  56.3 0.5 collective-permute-done.19.refs_3_
  56.8 0.0 collective-permute-done.18.refs_2_
  56.8 1.5 %collective-permute-done.17.refs_1_ = f32[8,128]{1,0:T(8,128)S(1)} collective-permute-done((f32[8,128]{1,0:T(8,128)S(1)}, f32[8,128]{1,0:T(8,128)S(1)}, u32[]{:S(2)}, u32[]{:S(2)}) %collective-permute-start.17) | collective-permute-done | bytes 4128 | tf_op jit(solution)/shard_map/ppermute | solution.py:492
  58.3 2.0 %finish.1 = (f32[1024,512]{1,0:T(8,128)}, f32[1,1]{1,0:T(1,128)}) custom-call(s32[5]{0:T(128)S(1)} %stack.19.where, f32[512,128]{1,0:T(8,128)S(1)} %collective-permute-done.15.far, f32[1024,128]{1,0:T(8,128)S(1)} %get-tuple-element.60.mate, f32[8,128]{1,0:T(8,128)S(1)} %slice_add_fusion.refs_0_, ...), custom_call_target="tpu_custom_call", output_to_operand_aliasing={{0}: (7, {})} | custom-call | tf_op jit(solution)/shard_map/finish/pallas_call | solution.py:471
  (5 shorter events, 0.1 us)
Async XLA Ops:
  1.4 1.6 %copy-start = (f32[128,4096]{1,0:T(8,128)S(1)}, f32[128,4096]{1,0:T(8,128)}, u32[]{:S(2)}) copy-start(f32[128,4096]{1,0:T(8,128)} %source.1) | copy-start | bytes 6291460
  4.6 4.0 %collective-permute-start = (f32[1,128,512]{2,1,0:T(8,128)S(1)}, f32[1,128,512]{2,1,0:T(8,128)S(1)}, u32[]{:S(2)}, u32[]{:S(2)}) collective-permute-start(f32[1,128,512]{2,1,0:T(8,128)S(1)} %get-tuple-element.33), channel_id=1, source_target_pairs={{0,4},{4,0},{8,12},{12,8},{16,20},{20,16},{24,28},{28,24},{1,5},{5... | collective-permute-start | bytes 786440 | tf_op jit(solution)/shard_map/ppermute | solution.py:492
  5.1 5.0 %collective-permute-start.1 = (f32[1,128,512]{2,1,0:T(8,128)S(1)}, f32[1,128,512]{2,1,0:T(8,128)S(1)}, u32[]{:S(2)}, u32[]{:S(2)}) collective-permute-start(f32[1,128,512]{2,1,0:T(8,128)S(1)} %get-tuple-element.34), channel_id=1, source_target_pairs={{0,4},{4,0},{8,12},{12,8},{16,20},{20,16},{24,28},{28,24},{1,5},{5... | collective-permute-start | bytes 786440 | tf_op jit(solution)/shard_map/ppermute | solution.py:492
  5.2 5.0 %collective-permute-start.2 = (f32[1,128,512]{2,1,0:T(8,128)S(1)}, f32[1,128,512]{2,1,0:T(8,128)S(1)}, u32[]{:S(2)}, u32[]{:S(2)}) collective-permute-start(f32[1,128,512]{2,1,0:T(8,128)S(1)} %get-tuple-element.39), channel_id=1, source_target_pairs={{0,4},{4,0},{8,12},{12,8},{16,20},{20,16},{24,28},{28,24},{1,5},{5... | collective-permute-start | bytes 786440 | tf_op jit(solution)/shard_map/ppermute | solution.py:492
  5.6 4.5 %collective-permute-start.3 = (f32[1,128,512]{2,1,0:T(8,128)S(1)}, f32[1,128,512]{2,1,0:T(8,128)S(1)}, u32[]{:S(2)}, u32[]{:S(2)}) collective-permute-start(f32[1,128,512]{2,1,0:T(8,128)S(1)} %get-tuple-element.40), channel_id=1, source_target_pairs={{0,4},{4,0},{8,12},{12,8},{16,20},{20,16},{24,28},{28,24},{1,5},{5... | collective-permute-start | bytes 786440 | tf_op jit(solution)/shard_map/ppermute | solution.py:492
  5.7 10.0 %collective-permute-start.4 = (f32[1,128,512]{2,1,0:T(8,128)S(1)}, f32[1,128,512]{2,1,0:T(8,128)S(1)}, u32[]{:S(2)}, u32[]{:S(2)}) collective-permute-start(f32[1,128,512]{2,1,0:T(8,128)S(1)} %get-tuple-element.36.refs_1_), channel_id=1, source_target_pairs={{0,8},{4,12},{8,0},{12,4},{16,24},{20,28},{24,16},{28,20},{1,9},{5... | collective-permute-start | bytes 786440 | tf_op jit(solution)/shard_map/ppermute | solution.py:492
  8.6 9.2 %collective-permute-start.5 = (f32[1,128,512]{2,1,0:T(8,128)S(1)}, f32[1,128,512]{2,1,0:T(8,128)S(1)}, u32[]{:S(2)}, u32[]{:S(2)}) collective-permute-start(f32[1,128,512]{2,1,0:T(8,128)S(1)} %get-tuple-element.37.refs_2_), channel_id=1, source_target_pairs={{0,16},{4,20},{8,24},{12,28},{16,0},{20,4},{24,8},{28,12},{1,17},{... | collective-permute-start | bytes 786440 | tf_op jit(solution)/shard_map/ppermute | solution.py:492
  11.0 7.9 %collective-permute-start.6 = (f32[4,72,128]{2,1,0:T(8,128)S(1)}, f32[4,72,128]{2,1,0:T(8,128)S(1)}, u32[]{:S(2)}, u32[]{:S(2)}) collective-permute-start(f32[4,72,128]{2,1,0:T(8,128)S(1)} %get-tuple-element.42), channel_id=1, source_target_pairs={{0,8},{4,12},{8,0},{12,4},{16,24},{20,28},{24,16},{28,20},{1,9},{5... | collective-permute-start | bytes 442376 | tf_op jit(solution)/shard_map/ppermute | solution.py:492
  11.6 11.3 %collective-permute-start.7 = (f32[4,72,128]{2,1,0:T(8,128)S(1)}, f32[4,72,128]{2,1,0:T(8,128)S(1)}, u32[]{:S(2)}, u32[]{:S(2)}) collective-permute-start(f32[4,72,128]{2,1,0:T(8,128)S(1)} %get-tuple-element.43), channel_id=1, source_target_pairs={{0,16},{4,20},{8,24},{12,28},{16,0},{20,4},{24,8},{28,12},{1,17},{... | collective-permute-start | bytes 442376 | tf_op jit(solution)/shard_map/ppermute | solution.py:492
  12.7 10.2 %collective-permute-start.8 = (f32[4,72,128]{2,1,0:T(8,128)S(1)}, f32[4,72,128]{2,1,0:T(8,128)S(1)}, u32[]{:S(2)}, u32[]{:S(2)}) collective-permute-start(f32[4,72,128]{2,1,0:T(8,128)S(1)} %get-tuple-element.44), channel_id=1, source_target_pairs={{0,24},{4,28},{8,16},{12,20},{16,8},{20,12},{24,0},{28,4},{1,25},{... | collective-permute-start | bytes 442376 | tf_op jit(solution)/shard_map/ppermute | solution.py:492
  22.9 23.2 %collective-permute-start.14 = (f32[2,128,512]{2,1,0:T(8,128)S(1)}, f32[2,128,512]{2,1,0:T(8,128)S(1)}, u32[]{:S(2)}, u32[]{:S(2)}) collective-permute-start(f32[2,128,512]{2,1,0:T(8,128)S(1)} %joined.1), channel_id=1, source_target_pairs={{0,24},{4,28},{8,16},{12,20},{16,8},{20,12},{24,0},{28,4},{1,25},{... | collective-permute-start | bytes 1572872 | tf_op jit(solution)/shard_map/ppermute | solution.py:492
  24.8 4.4 %collective-permute-start.9 = (f32[2,72,128]{2,1,0:T(8,128)S(1)}, f32[2,72,128]{2,1,0:T(8,128)S(1)}, u32[]{:S(2)}, u32[]{:S(2)}) collective-permute-start(f32[2,72,128]{2,1,0:T(8,128)S(1)} %get-tuple-element.49), channel_id=1, source_target_pairs={{0,1},{1,0},{2,3},{3,2},{4,5},{5,4},{6,7},{7,6},{8,9},{9,8},{10,11... | collective-permute-start | bytes 221192 | tf_op jit(solution)/shard_map/ppermute | solution.py:492
  29.2 16.8 %collective-permute-start.12 = (f32[1,128,512]{2,1,0:T(8,128)S(1)}, f32[1,128,512]{2,1,0:T(8,128)S(1)}, u32[]{:S(2)}, u32[]{:S(2)}) collective-permute-start(f32[1,128,512]{2,1,0:T(8,128)S(1)} %collective-permute-done.refs_5_), channel_id=1, source_target_pairs={{0,8},{4,12},{8,0},{12,4},{16,24},{20,28},{24,16},{28,20},{1,9},{5... | collective-permute-start | bytes 786440 | tf_op jit(solution)/shard_map/ppermute | solution.py:492
  30.5 15.6 %collective-permute-start.13 = (f32[1,128,512]{2,1,0:T(8,128)S(1)}, f32[1,128,512]{2,1,0:T(8,128)S(1)}, u32[]{:S(2)}, u32[]{:S(2)}) collective-permute-start(f32[1,128,512]{2,1,0:T(8,128)S(1)} %collective-permute-done.1.refs_6_), channel_id=1, source_target_pairs={{0,16},{4,20},{8,24},{12,28},{16,0},{20,4},{24,8},{28,12},{1,17},{... | collective-permute-start | bytes 786440 | tf_op jit(solution)/shard_map/ppermute | solution.py:492
  31.0 5.4 %collective-permute-start.10 = (f32[2,72,128]{2,1,0:T(8,128)S(1)}, f32[2,72,128]{2,1,0:T(8,128)S(1)}, u32[]{:S(2)}, u32[]{:S(2)}) collective-permute-start(f32[2,72,128]{2,1,0:T(8,128)S(1)} %add.14), channel_id=1, source_target_pairs={{0,2},{1,3},{2,0},{3,1},{4,6},{5,7},{6,4},{7,5},{8,10},{9,11},{10,... | collective-permute-start | bytes 221192 | tf_op jit(solution)/shard_map/ppermute | solution.py:492
  36.3 4.4 %collective-permute-start.11 = (f32[2,72,128]{2,1,0:T(8,128)S(1)}, f32[2,72,128]{2,1,0:T(8,128)S(1)}, u32[]{:S(2)}, u32[]{:S(2)}) collective-permute-start(f32[2,72,128]{2,1,0:T(8,128)S(1)} %add.15.refs_0_), channel_id=1, source_target_pairs={{0,1},{1,0},{2,3},{3,2},{4,5},{5,4},{6,7},{7,6},{8,9},{9,8},{10,11... | collective-permute-start | bytes 221192 | tf_op jit(solution)/shard_map/ppermute | solution.py:492
  47.2 1.6 %collective-permute-start.16 = (f32[520,128]{1,0:T(8,128)S(1)}, f32[520,128]{1,0:T(8,128)S(1)}, u32[]{:S(2)}, u32[]{:S(2)}) collective-permute-start(f32[520,128]{1,0:T(8,128)S(1)} %get-tuple-element.59), channel_id=1, source_target_pairs={{0,4},{4,0},{8,12},{12,8},{16,20},{20,16},{24,28},{28,24},{1,5},{5... | collective-permute-start | bytes 798728 | tf_op jit(solution)/shard_map/ppermute | solution.py:487
  47.2 9.1 %collective-permute-start.15 = (f32[512,128]{1,0:T(8,128)S(1)}, f32[512,128]{1,0:T(8,128)S(1)}, u32[]{:S(2)}, u32[]{:S(2)}) collective-permute-start(f32[512,128]{1,0:T(8,128)S(1)} %get-tuple-element.58), channel_id=1, source_target_pairs={{4,8},{8,4},{12,16},{16,12},{20,24},{24,20},{5,9},{9,5},{13,17},{1... | collective-permute-start | bytes 786440 | tf_op jit(solution)/shard_map/ppermute | solution.py:487
  48.8 8.0 %collective-permute-start.19 = (f32[8,128]{1,0:T(8,128)S(1)}, f32[8,128]{1,0:T(8,128)S(1)}, u32[]{:S(2)}, u32[]{:S(2)}) collective-permute-start(f32[8,128]{1,0:T(8,128)S(1)} %slice_add_fusion.refs_0_), channel_id=1, source_target_pairs={{0,24},{4,28},{8,16},{12,20},{16,8},{20,12},{24,0},{28,4},{1,25},{... | collective-permute-start | bytes 12296 | tf_op jit(solution)/shard_map/ppermute | solution.py:492
  52.4 4.4 %collective-permute-start.18 = (f32[8,128]{1,0:T(8,128)S(1)}, f32[8,128]{1,0:T(8,128)S(1)}, u32[]{:S(2)}, u32[]{:S(2)}) collective-permute-start(f32[8,128]{1,0:T(8,128)S(1)} %slice_add_fusion.refs_0_), channel_id=1, source_target_pairs={{0,16},{4,20},{8,24},{12,28},{16,0},{20,4},{24,8},{28,12},{1,17},{... | collective-permute-start | bytes 12296 | tf_op jit(solution)/shard_map/ppermute | solution.py:492
  52.8 5.5 %collective-permute-start.17 = (f32[8,128]{1,0:T(8,128)S(1)}, f32[8,128]{1,0:T(8,128)S(1)}, u32[]{:S(2)}, u32[]{:S(2)}) collective-permute-start(f32[8,128]{1,0:T(8,128)S(1)} %slice_add_fusion.refs_0_), channel_id=1, source_target_pairs={{0,8},{4,12},{8,0},{12,4},{16,24},{20,28},{24,16},{28,20},{1,9},{5... | collective-permute-start | bytes 12296 | tf_op jit(solution)/shard_map/ppermute | solution.py:492

commit v5 on v4

--- a/solution.py
+++ b/solution.py
@@ -12,6 +12,7 @@
 ITERS = 3
 TOLERANCE = 1e-8
 LAST_ROWS = 8
+FAR_PARTS = 1
 GATHER_CHUNKS = 2
 GATHER_VMEM = 62 * 1024 * 1024
 VMEM = pl.BlockSpec(memory_space=pltpu.VMEM)
@@ -183,23 +184,26 @@
     )(*here, *near)
 
 
-def joined_kernel(*refs):
-    half = len(refs) // 3
-    for side in range(half):
-        for place in range(2):
-            refs[2 * half + side][place] = refs[2 * side + place][0]
-
-
-def joined(*sides):
+def joined_kernel(counts, after, *refs):
+    del after
+    sources, outs = refs[: sum(counts)], refs[sum(counts) :]
+    for count, out in zip(counts, outs):
+        for place in range(count):
+            out[place] = sources[place][0]
+        sources = sources[count:]
+
+
+def joined(after, *sides):
     _, rows, cols = sides[0][0].shape
-    return pl.pallas_call(
-        joined_kernel,
-        out_shape=(jax.ShapeDtypeStruct((2, rows, cols), jnp.float32),) * len(sides),
-        in_specs=[VMEM] * (2 * len(sides)),
+    counts = tuple(len(side) for side in sides)
+    return pl.pallas_call(
+        functools.partial(joined_kernel, counts),
+        out_shape=tuple(jax.ShapeDtypeStruct((count, rows, cols), jnp.float32) for count in counts),
+        in_specs=[pl.BlockSpec(memory_space=pl.ANY)] + [VMEM] * sum(counts),
         out_specs=(VMEM,) * len(sides),
         compiler_params=PARAMS,
         name="joined",
-    )(*[value for side in sides for value in side])
+    )(after, *[value for side in sides for value in side])
 
 
 def merge_kernel(count, row, *refs):
@@ -349,8 +353,8 @@
     return lambda index: product(split(results[index][0]), split(held[index]))
 
 
-def edge_kernel(tracks, where, sums, held, *refs):
-    columns, near, far = refs[:-2], refs[-2], refs[-1]
+def edge_kernel(tracks, parts, where, sums, held, *refs):
+    columns, near, far = refs[: -1 - parts], refs[-1 - parts], refs[-parts:]
     odd = lax.rem(where[0], 2) == 1
     rows = columns[0].shape[1]
     half = rows // 2
@@ -366,17 +370,19 @@
         one = first[block * rows : (block + 1) * rows]
         down = jnp.where(low_lanes, pltpu.roll(one[:half], BLOCK, 1), one[half:])
         near[span] = jnp.where(odd, down, up)
-        far[span] = jnp.where(odd, up, down)
+        each = blocks // parts
+        far[block // each][block % each * half : (block % each + 1) * half] = jnp.where(odd, up, down)
     near[-LAST_ROWS:] = sums[...]
 
 
-def edges(tracks, where, sums, columns, turns):
+def edges(tracks, parts, where, sums, columns, turns):
     half = len(tracks[0][1]) * columns[0].shape[1] // 2
-    return pl.pallas_call(
-        functools.partial(edge_kernel, tracks),
-        out_shape=tuple(jax.ShapeDtypeStruct((height, WIDTH), jnp.float32) for height in (half + LAST_ROWS, half)),
+    heights = (half + LAST_ROWS,) + (half // parts,) * parts
+    return pl.pallas_call(
+        functools.partial(edge_kernel, tracks, parts),
+        out_shape=tuple(jax.ShapeDtypeStruct((height, WIDTH), jnp.float32) for height in heights),
         in_specs=[SMEM] + [VMEM] * (2 + len(columns)),
-        out_specs=(VMEM,) * 2,
+        out_specs=(VMEM,) * (1 + parts),
         compiler_params=PARAMS,
         name="edges",
     )(where, sums, turns, *columns)
@@ -437,14 +443,11 @@
     )(where, near, turns, *columns)
 
 
-def finish_kernel(blocks, count, where, far, mate, *refs):
-    sums, (out, ratio, tile, sems) = refs[:count], refs[count + 1 :]
-    value = sums[0][...]
-    for other in sums[1:]:
-        value = value + other[...]
-    ratio[...] = jnp.sqrt(value[:1, :1] / value[:1, 1:2])
+def finish_kernel(blocks, parts, where, mate, *refs):
+    far, sums, (_, out, ratio, tile, sems) = refs[:parts], refs[parts:-5], refs[-5:]
     rows = mate.shape[0] // blocks
     half = rows // 2
+    each = blocks // parts
     odd = lax.rem(where[0], 2) == 1
     used = jnp.where(odd, where[0] < where[1] - 1, where[0] > 0)
     lanes = lax.broadcasted_iota(jnp.int32, (rows, WIDTH), 1)
@@ -456,28 +459,35 @@
         span = pl.ds(block * rows, rows)
         own_place = jnp.bitwise_xor(where[2], block)
         there = jnp.bitwise_xor(own_place, jnp.where(odd, where[4], where[3]))
-        arrived = far[pl.ds(pl.multiple_of(there * half, half), half)]
+        far_rows = pl.ds(pl.multiple_of(lax.rem(there, each) * half, half), half)
+        arrived = far[0][far_rows]
+        for part in range(1, parts):
+            arrived = jnp.where(there < part * each, arrived, far[part][far_rows])
         moved = pltpu.roll(arrived, BLOCK, 1)
         both = jnp.concatenate([jnp.where(odd, moved, arrived), jnp.where(odd, arrived, moved)], axis=0)
         tile[span] = jnp.where(here, both, mate[span])
         own_rows = pl.ds(pl.multiple_of(own_place * rows, rows), rows)
         copies.append(pltpu.make_async_copy(tile.at[span], out.at[own_rows, column], sems.at[block]))
         copies[-1].start()
+    value = sums[0][...]
+    for other in sums[1:]:
+        value = value + other[...]
+    ratio[...] = jnp.sqrt(value[:1, :1] / value[:1, 1:2])
     for copy in copies:
         copy.wait()
 
 
 def finish(blocks, where, far, mate, sums, rotated):
     return pl.pallas_call(
-        functools.partial(finish_kernel, blocks, len(sums)),
+        functools.partial(finish_kernel, blocks, len(far)),
         out_shape=(jax.ShapeDtypeStruct(rotated.shape, jnp.float32), jax.ShapeDtypeStruct((1, 1), jnp.float32)),
-        in_specs=[SMEM] + [VMEM] * (2 + len(sums)) + [HBM],
+        in_specs=[SMEM] + [VMEM] * (1 + len(far) + len(sums)) + [HBM],
         out_specs=(HBM, VMEM),
-        input_output_aliases={3 + len(sums): 0},
+        input_output_aliases={2 + len(far) + len(sums): 0},
         scratch_shapes=[pltpu.VMEM(mate.shape, jnp.float32), pltpu.SemaphoreType.DMA((blocks,))],
         compiler_params=PARAMS,
         name="finish",
-    )(where, far, mate, *sums, rotated)
+    )(where, mate, *far, *sums, rotated)
 
 
 def swapped_in_twos(value, axis, first):
@@ -507,15 +517,15 @@
         arranged = gather(r_factor, block_slots, base, tuple(plan))
         here = arranged[0::2]
         near = [swapped(value, "pair", 1) for value in arranged[1::2]]
-        here_two = swapped(here[1], "pair", 2)
-        here_four = swapped(here[2], "pair", 4)
         own, *given = near_grams(here, near)
         taken = [swapped(value, "pair", by) for by, value in zip((2, 4, 6), given)]
-        (on_six,) = joined((here[3], near[3]))
-        here_two, here_four, on_six, taken = lax.optimization_barrier((here_two, here_four, on_six, taken))
+        going = joined(given[0], (here[1], near[1]), (here[2], near[2]), (here[3], near[3]))
+        going, taken = lax.optimization_barrier((going, taken))
         parts = merge(row, [own] + taken, shares)
-        from_six = swapped(on_six, "pair", 6)
-        tracks = ((local, tuple((position, 0) for position in range(pair_count - 1)) + ((pair_count - 2, 1),)),)
+        from_far = [swapped(value, "pair", by) for by, value in zip((2, 4, 6), going)]
+        columns = (here[0], near[0], *from_far)
+        places = ((0, 0), (1, 0), (2, 0), (2, 1), (3, 0), (3, 1), (4, 0), (4, 1))
+        tracks = ((local, places),)
         bases = (pair_index, pair_index - 1, pair_index + 1)
     else:
         (arranged,) = gather(r_factor, block_slots, base, ((local, 0, local, None),))
@@ -526,11 +536,6 @@
         bases = (jnp.zeros_like(pair_index),) * 3
     if shared:
         half = parts[0] + swapped(parts[1], "row", 1)
-        if pair_count == 8:
-            near_two, near_four, half = lax.optimization_barrier((near[1], near[2], half))
-            near_two = swapped(near_two, "pair", 2)
-            near_four = swapped(near_four, "pair", 4)
-            columns = (here[0], near[0], here_two, near_two, here_four, near_four, from_six)
         for bit in range(1, row_count.bit_length() - 1):
             half = half + swapped(half, "row", 1 << bit)
         parts = (half, swapped(half, "row", 1))
@@ -539,8 +544,8 @@
     turns, sums = solve(row, parts)
     bases = [jnp.clip(value, 0, pair_count - 1) for value in bases]
     where = jnp.stack([pair_index, jnp.int32(pair_count)] + bases).astype(jnp.int32)
-    near, far = edges(tracks, where, sums, columns, turns)
-    far = swapped_in_twos(far, "pair", 1)
+    near, *far = edges(tracks, FAR_PARTS if pair_count % FAR_PARTS == 0 else 1, where, sums, columns, turns)
+    far = [swapped_in_twos(part, "pair", 1) for part in far]
     near = swapped_in_twos(near, "pair", 0)
     rotated, mate = place(tracks, where, columns, near, turns)
     if pair_count == 8:

time: 60.4 us -> 59.8 us (0.990)
  starting transfers between devices: 23.9 us -> 21 us
  waiting for transfers between devices: 19.5 us -> 20.7 us
  Pallas kernels: 13.7 us -> 14.7 us
    ppermute x18 -> x16, starting transfers between devices: 23.1 us -> 20.3 us  [swapped(): return lax.ppermute(value, axis, [(i, i ^ by) for i in range(count)])]
    ppermute x18 -> x16, waiting for transfers between devices: 18.7 us -> 19.9 us  [swapped(): return lax.ppermute(value, axis, [(i, i ^ by) for i in range(count)])]
    pallas_call x3, Pallas kernels: 3.08 us -> 4.12 us  [the longest x1 1.98 us: finish(): pl.pallas_call(functools.partial(finish_kernel, blocks, len(far)), out_sh...]
  transfers between devices with their start and end apart: 20 -> 18, of which waited for: 10 -> 14; matrix products, arithmetic and copies ran while one was open for 0% -> 0% of each run, Pallas kernels for 15% -> 15%
where the time goes in v5:
time: 59.8 us; the launch traced here: 59.6 us
  starting transfers between devices  21 us (35%)
  waiting for transfers between devices  20.7 us (35%)
  Pallas kernels  14.7 us (25%)
  local copies, waits for them, and re-layouts  1.67 us (3%)
  other arithmetic  0.75 us (1%)
  between operations  0.71 us (1%)
    ppermute x16, starting transfers between devices, swapped(): return lax.ppermute(value, axis, [(i, i ^ by) for i in range(count)])  20.3 us
    ppermute x16, waiting for transfers between devices, swapped(): return lax.ppermute(value, axis, [(i, i ^ by) for i in range(count)])  19.9 us
    pallas_call x1, Pallas kernels, solve(): pl.pallas_call(functools.partial(solve_kernel, len(parts)), out_shape=(ja...  5.3 us
    pallas_call x1, Pallas kernels, place(): pl.pallas_call(functools.partial(place_kernel, tracks), out_shape=(jax.Sh...  2.8 us
    pallas_call x1, Pallas kernels, finish(): pl.pallas_call(functools.partial(finish_kernel, blocks, len(far)), out_sh...  1.98 us
    pallas_call x1, Pallas kernels, gather(): pl.pallas_call(functools.partial(gather_kernel, tuple(((local, first, pos...  1.6 us
    unnamed x2, local copies, waits for them, and re-layouts  1.59 us
  transfers between devices with their start and end apart: 18, of which 14 were waited for; matrix products, arithmetic and copies ran while one was open for 0% of the time, Pallas kernels for 15%

profile of v5, /device:TPU:0, one launch (start us, length us, event | category | flops | bytes accessed | tf_op | source)
XLA Modules:
  0.0 59.6 jit_solution(8072332685004269548)
XLA Ops:
  0.6 0.7 %pad_add_fusion.slots = s32[65]{0:T(128)S(1)} fusion(s32[1]{0:T(128)} %bitcast, s32[64]{0:T(128)} %param.3), kind=kLoop, calls=%fused_computation.1 | loop fusion | flops 65 | bytes 520 | tf_op jit(solution)/shard_map/concatenate | solution.py:97
  1.4 0.0 copy-start
  1.4 1.6 %copy-done = f32[128,4096]{1,0:T(8,128)S(1)} copy-done((f32[128,4096]{1,0:T(8,128)S(1)}, f32[128,4096]{1,0:T(8,128)}, u32[]{:S(2)}) %copy-start) | copy-done | bytes 2097176
  3.0 1.6 %gather.1 = (f32[1,128,512]{2,1,0:T(8,128)S(1)}, f32[1,128,512]{2,1,0:T(8,128)S(1)}, f32[1,128,512]{2,1,0:T(8,128)S(1)}, f32[1,128,512]{2,1,0:T(8,128)S(1)}, f32...) custom-call(s32[65]{0:T(128)S(1)} %pad_add_fusion.slots, ...), custom_call_target="tpu_custom_call" | custom-call | tf_op jit(solution)/shard_map/gather/pallas_call | solution.py:90
  4.6 0.5 collective-permute-start
  5.1 0.1 collective-permute-start.1
  5.2 0.4 collective-permute-start.2
  5.6 0.1 collective-permute-start.3
  5.7 0.6 collective-permute-done.refs_4_.refs_1_
  6.2 0.4 collective-permute-done.1.refs_5_.refs_1_
  6.6 0.4 collective-permute-done.2.refs_6_.refs_3_
  7.0 0.4 collective-permute-done.3.refs_7_.refs_5_
  7.4 0.9 %near_grams.1 = (f32[4,72,128]{2,1,0:T(8,128)S(1)}, f32[4,72,128]{2,1,0:T(8,128)S(1)}, f32[4,72,128]{2,1,0:T(8,128)S(1)}, f32[4,72,128]{2,1,0:T(8,128)S(1)}) custom-call(f32[1,128,512]{2,1,0:T(8,128)S(1)} %get-tuple-element.33.refs_0_, f32[1,128,512]{2,1,0:T(8,128)S(1)} %get-tuple-element.34.refs_1_.refs_0_, f32[1,128,512]{2,1,0:T(8,128)S(1)} %get-tuple-element.35.refs_2_, ...), custom_call_target="tpu_custom_call" | custom-call | tf_op jit(solution)/shard_map/near_grams/pallas_call | solution.py:177
  8.2 3.0 %collective-permute-start.5 = (f32[4,72,128]{2,1,0:T(8,128)S(1)}, f32[4,72,128]{2,1,0:T(8,128)S(1)}, u32[]{:S(2)}, u32[]{:S(2)}) collective-permute-start(f32[4,72,128]{2,1,0:T(8,128)S(1)} %get-tuple-element.46), channel_id=1, source_target_pairs={{0,16},{4,20},{8,24},{12,28},{16,0},{20,4},{24,8},{28,12},{1,17},{... | collective-permute-start | bytes 442376 | tf_op jit(solution)/shard_map/ppermute | solution.py:502
  11.2 1.4 %collective-permute-start.6 = (f32[4,72,128]{2,1,0:T(8,128)S(1)}, f32[4,72,128]{2,1,0:T(8,128)S(1)}, u32[]{:S(2)}, u32[]{:S(2)}) collective-permute-start(f32[4,72,128]{2,1,0:T(8,128)S(1)} %get-tuple-element.47), channel_id=1, source_target_pairs={{0,24},{4,28},{8,16},{12,20},{16,8},{20,12},{24,0},{28,4},{1,25},{... | collective-permute-start | bytes 442376 | tf_op jit(solution)/shard_map/ppermute | solution.py:502
  12.6 0.1 collective-permute-start.4
  12.7 1.1 %joined.1 = (f32[2,128,512]{2,1,0:T(8,128)}, f32[2,128,512]{2,1,0:T(8,128)}, f32[2,128,512]{2,1,0:T(8,128)S(1)}) custom-call(f32[4,72,128]{2,1,0:T(8,128)S(1)} %get-tuple-element.42.after, f32[1,128,512]{2,1,0:T(8,128)S(1)} %get-tuple-element.34.refs_1_.refs_0_, f32[1,128,512]{2,1,0:T(8,128)S(1)} %collective-permute-done.1.refs_5_.refs_1_, ...), custom_call_target="tpu_custom_call" | custom-call | tf_op jit(solution)/shard_map/joined/pallas_call | solution.py:199
  13.8 4.4 %collective-permute-done.5.refs_2_ = f32[4,72,128]{2,1,0:T(8,128)S(1)} collective-permute-done((f32[4,72,128]{2,1,0:T(8,128)S(1)}, f32[4,72,128]{2,1,0:T(8,128)S(1)}, u32[]{:S(2)}, u32[]{:S(2)}) %collective-permute-start.5) | collective-permute-done | bytes 147488 | tf_op jit(solution)/shard_map/ppermute | solution.py:502
  18.2 0.7 %collective-permute-done.6.refs_3_ = f32[4,72,128]{2,1,0:T(8,128)S(1)} collective-permute-done((f32[4,72,128]{2,1,0:T(8,128)S(1)}, f32[4,72,128]{2,1,0:T(8,128)S(1)}, u32[]{:S(2)}, u32[]{:S(2)}) %collective-permute-start.6) | collective-permute-done | bytes 147488 | tf_op jit(solution)/shard_map/ppermute | solution.py:502
  18.8 1.0 %collective-permute-done.4.refs_1_ = f32[4,72,128]{2,1,0:T(8,128)S(1)} collective-permute-done((f32[4,72,128]{2,1,0:T(8,128)S(1)}, f32[4,72,128]{2,1,0:T(8,128)S(1)}, u32[]{:S(2)}, u32[]{:S(2)}) %collective-permute-start.4) | collective-permute-done | bytes 147488 | tf_op jit(solution)/shard_map/ppermute | solution.py:502
  19.8 1.6 %collective-permute-start.10 = (f32[2,128,512]{2,1,0:T(8,128)}, f32[2,128,512]{2,1,0:T(8,128)S(1)}, u32[]{:S(2)}, u32[]{:S(2)}) collective-permute-start(f32[2,128,512]{2,1,0:T(8,128)} %get-tuple-element.55), channel_id=1, source_target_pairs={{0,8},{4,12},{8,0},{12,4},{16,24},{20,28},{24,16},{28,20},{1,9},{5... | collective-permute-start | bytes 1572872 | tf_op jit(solution)/shard_map/ppermute | solution.py:502
  21.4 1.5 %collective-permute-start.11 = (f32[2,128,512]{2,1,0:T(8,128)}, f32[2,128,512]{2,1,0:T(8,128)S(1)}, u32[]{:S(2)}, u32[]{:S(2)}) collective-permute-start(f32[2,128,512]{2,1,0:T(8,128)} %get-tuple-element.56), channel_id=1, source_target_pairs={{0,16},{4,20},{8,24},{12,28},{16,0},{20,4},{24,8},{28,12},{1,17},{... | collective-permute-start | bytes 1572872 | tf_op jit(solution)/shard_map/ppermute | solution.py:502
  23.0 0.3 collective-permute-start.12
  23.3 1.8 %collective-permute-start.7 = (f32[2,72,128]{2,1,0:T(8,128)S(1)}, f32[2,72,128]{2,1,0:T(8,128)S(1)}, u32[]{:S(2)}, u32[]{:S(2)}) collective-permute-start(f32[2,72,128]{2,1,0:T(8,128)S(1)} %get-tuple-element.52), channel_id=1, source_target_pairs={{0,1},{1,0},{2,3},{3,2},{4,5},{5,4},{6,7},{7,6},{8,9},{9,8},{10,11... | collective-permute-start | bytes 221192 | tf_op jit(solution)/shard_map/ppermute | solution.py:502
  25.1 2.6 %collective-permute-done.7 = f32[2,72,128]{2,1,0:T(8,128)S(1)} collective-permute-done((f32[2,72,128]{2,1,0:T(8,128)S(1)}, f32[2,72,128]{2,1,0:T(8,128)S(1)}, u32[]{:S(2)}, u32[]{:S(2)}) %collective-permute-start.7) | collective-permute-done | bytes 73760 | tf_op jit(solution)/shard_map/ppermute | solution.py:502
  27.8 2.9 %collective-permute-start.8 = (f32[2,72,128]{2,1,0:T(8,128)S(1)}, f32[2,72,128]{2,1,0:T(8,128)S(1)}, u32[]{:S(2)}, u32[]{:S(2)}) collective-permute-start(f32[2,72,128]{2,1,0:T(8,128)S(1)} %add.14), channel_id=1, source_target_pairs={{0,2},{1,3},{2,0},{3,1},{4,6},{5,7},{6,4},{7,5},{8,10},{9,11},{10,... | collective-permute-start | bytes 221192 | tf_op jit(solution)/shard_map/ppermute | solution.py:502
  30.7 2.5 %collective-permute-done.8 = f32[2,72,128]{2,1,0:T(8,128)S(1)} collective-permute-done((f32[2,72,128]{2,1,0:T(8,128)S(1)}, f32[2,72,128]{2,1,0:T(8,128)S(1)}, u32[]{:S(2)}, u32[]{:S(2)}) %collective-permute-start.8) | collective-permute-done | bytes 73760 | tf_op jit(solution)/shard_map/ppermute | solution.py:502
  33.2 1.7 %collective-permute-start.9 = (f32[2,72,128]{2,1,0:T(8,128)S(1)}, f32[2,72,128]{2,1,0:T(8,128)S(1)}, u32[]{:S(2)}, u32[]{:S(2)}) collective-permute-start(f32[2,72,128]{2,1,0:T(8,128)S(1)} %add.15.refs_0_), channel_id=1, source_target_pairs={{0,1},{1,0},{2,3},{3,2},{4,5},{5,4},{6,7},{7,6},{8,9},{9,8},{10,11... | collective-permute-start | bytes 221192 | tf_op jit(solution)/shard_map/ppermute | solution.py:502
  34.9 0.1 stack.19.where
  35.0 2.6 %collective-permute-done.9.refs_1_ = f32[2,72,128]{2,1,0:T(8,128)S(1)} collective-permute-done((f32[2,72,128]{2,1,0:T(8,128)S(1)}, f32[2,72,128]{2,1,0:T(8,128)S(1)}, u32[]{:S(2)}, u32[]{:S(2)}) %collective-permute-start.9) | collective-permute-done | bytes 73760 | tf_op jit(solution)/shard_map/ppermute | solution.py:502
  37.6 5.3 %solve.1 = (f32[4,128,128]{2,1,0:T(8,128)S(1)}, f32[8,128]{1,0:T(8,128)S(1)}) custom-call(s32[1]{0:T(128)} %bitcast.4.row, f32[2,72,128]{2,1,0:T(8,128)S(1)} %add.15.refs_0_, f32[2,72,128]{2,1,0:T(8,128)S(1)} %collective-permute-done.9.refs_1_), custom_call_target="tpu_custom_call" | custom-call | tf_op jit(solution)/shard_map/solve/pallas_call | solution.py:328
  42.9 0.0 collective-permute-done.10.refs_2_
  42.9 2.5 %collective-permute-done.11.refs_3_ = f32[2,128,512]{2,1,0:T(8,128)S(1)} collective-permute-done((f32[2,128,512]{2,1,0:T(8,128)}, f32[2,128,512]{2,1,0:T(8,128)S(1)}, u32[]{:S(2)}, u32[]{:S(2)}) %collective-permute-start.11) | collective-permute-done | bytes 524320 | tf_op jit(solution)/shard_map/ppermute | solution.py:502
  45.5 0.0 collective-permute-done.12.refs_4_
  45.5 1.1 %edges.1 = (f32[520,128]{1,0:T(8,128)S(1)}, f32[512,128]{1,0:T(8,128)S(1)}) custom-call(s32[5]{0:T(128)S(1)} %stack.19.where, f32[8,128]{1,0:T(8,128)S(1)} %get-tuple-element.53.sums, f32[4,128,128]{2,1,0:T(8,128)S(1)} %get-tuple-element.54.held, f32[1,128,512]{2,1,0:T(8,128)S(1)} %get-tuple-element.33.refs_0_, ...), custom_call_target="tpu_custom_call" | custom-call | tf_op jit(solution)/shard_map/edges/pallas_call | solution.py:381
  46.5 0.1 collective-permute-start.13
  46.6 0.7 %collective-permute-start.14 = (f32[512,128]{1,0:T(8,128)S(1)}, f32[512,128]{1,0:T(8,128)S(1)}, u32[]{:S(2)}, u32[]{:S(2)}) collective-permute-start(f32[512,128]{1,0:T(8,128)S(1)} %get-tuple-element.60), channel_id=1, source_target_pairs={{4,8},{8,4},{12,16},{16,12},{20,24},{24,20},{5,9},{9,5},{13,17},{1... | collective-permute-start | bytes 786440 | tf_op jit(solution)/shard_map/ppermute | solution.py:497
  47.3 0.8 %collective-permute-done.13.near = f32[520,128]{1,0:T(8,128)S(1)} collective-permute-done((f32[520,128]{1,0:T(8,128)S(1)}, f32[520,128]{1,0:T(8,128)S(1)}, u32[]{:S(2)}, u32[]{:S(2)}) %collective-permute-start.13) | collective-permute-done | bytes 266272 | tf_op jit(solution)/shard_map/ppermute | solution.py:497
  48.1 3.6 %collective-permute-start.17 = (f32[8,128]{1,0:T(8,128)S(1)}, f32[8,128]{1,0:T(8,128)S(1)}, u32[]{:S(2)}, u32[]{:S(2)}) collective-permute-start(f32[8,128]{1,0:T(8,128)S(1)} %slice_add_fusion.refs_1_), channel_id=1, source_target_pairs={{0,24},{4,28},{8,16},{12,20},{16,8},{20,12},{24,0},{28,4},{1,25},{... | collective-permute-start | bytes 12296 | tf_op jit(solution)/shard_map/ppermute | solution.py:502
  51.7 0.5 collective-permute-start.16
  52.2 0.7 %collective-permute-start.15 = (f32[8,128]{1,0:T(8,128)S(1)}, f32[8,128]{1,0:T(8,128)S(1)}, u32[]{:S(2)}, u32[]{:S(2)}) collective-permute-start(f32[8,128]{1,0:T(8,128)S(1)} %slice_add_fusion.refs_1_), channel_id=1, source_target_pairs={{0,8},{4,12},{8,0},{12,4},{16,24},{20,28},{24,16},{28,20},{1,9},{5... | collective-permute-start | bytes 12296 | tf_op jit(solution)/shard_map/ppermute | solution.py:502
  52.9 2.8 %place.1 = (f32[1024,512]{1,0:T(8,128)}, f32[1024,128]{1,0:T(8,128)S(1)}) custom-call(s32[5]{0:T(128)S(1)} %stack.19.where, f32[520,128]{1,0:T(8,128)S(1)} %collective-permute-done.13.near, f32[4,128,128]{2,1,0:T(8,128)S(1)} %get-tuple-element.54.held, f32[1,128,512]{2,1,0:T(8,128)S(1)} %get-tuple-element.33.refs_0_, ...), custom_call_target="tpu_custom_call" | custom-call | tf_op jit(solution)/shard_map/place/pallas_call | solution.py:433
  55.7 0.0 collective-permute-done.14.refs_0_
  55.7 0.4 collective-permute-done.17.refs_4_
  56.1 0.0 collective-permute-done.16.refs_3_
  56.1 1.6 %collective-permute-done.15.refs_2_ = f32[8,128]{1,0:T(8,128)S(1)} collective-permute-done((f32[8,128]{1,0:T(8,128)S(1)}, f32[8,128]{1,0:T(8,128)S(1)}, u32[]{:S(2)}, u32[]{:S(2)}) %collective-permute-start.15) | collective-permute-done | bytes 4128 | tf_op jit(solution)/shard_map/ppermute | solution.py:502
  57.6 2.0 %finish.1 = (f32[1024,512]{1,0:T(8,128)}, f32[1,1]{1,0:T(1,128)}) custom-call(s32[5]{0:T(128)S(1)} %stack.19.where, f32[1024,128]{1,0:T(8,128)S(1)} %get-tuple-element.59.mate, f32[512,128]{1,0:T(8,128)S(1)} %collective-permute-done.14.refs_0_, f32[8,128]{1,0:T(8,128)S(1)} %slice_add_fusion.refs_1_, ...), custom_call_target="tpu_custom_call", output_to_operand_aliasing={{0}: (7, {})} | custom-call | tf_op jit(solution)/shard_map/finish/pallas_call | solution.py:481
  (4 shorter events, 0.1 us)
Async XLA Ops:
  1.4 1.6 %copy-start = (f32[128,4096]{1,0:T(8,128)S(1)}, f32[128,4096]{1,0:T(8,128)}, u32[]{:S(2)}) copy-start(f32[128,4096]{1,0:T(8,128)} %source.1) | copy-start | bytes 6291460
  4.6 1.7 %collective-permute-start = (f32[1,128,512]{2,1,0:T(8,128)S(1)}, f32[1,128,512]{2,1,0:T(8,128)S(1)}, u32[]{:S(2)}, u32[]{:S(2)}) collective-permute-start(f32[1,128,512]{2,1,0:T(8,128)S(1)} %get-tuple-element.37), channel_id=1, source_target_pairs={{0,4},{4,0},{8,12},{12,8},{16,20},{20,16},{24,28},{28,24},{1,5},{5... | collective-permute-start | bytes 786440 | tf_op jit(solution)/shard_map/ppermute | solution.py:502
  5.1 1.5 %collective-permute-start.1 = (f32[1,128,512]{2,1,0:T(8,128)S(1)}, f32[1,128,512]{2,1,0:T(8,128)S(1)}, u32[]{:S(2)}, u32[]{:S(2)}) collective-permute-start(f32[1,128,512]{2,1,0:T(8,128)S(1)} %get-tuple-element.38), channel_id=1, source_target_pairs={{0,4},{4,0},{8,12},{12,8},{16,20},{20,16},{24,28},{28,24},{1,5},{5... | collective-permute-start | bytes 786440 | tf_op jit(solution)/shard_map/ppermute | solution.py:502
  5.2 1.8 %collective-permute-start.2 = (f32[1,128,512]{2,1,0:T(8,128)S(1)}, f32[1,128,512]{2,1,0:T(8,128)S(1)}, u32[]{:S(2)}, u32[]{:S(2)}) collective-permute-start(f32[1,128,512]{2,1,0:T(8,128)S(1)} %get-tuple-element.39), channel_id=1, source_target_pairs={{0,4},{4,0},{8,12},{12,8},{16,20},{20,16},{24,28},{28,24},{1,5},{5... | collective-permute-start | bytes 786440 | tf_op jit(solution)/shard_map/ppermute | solution.py:502
  5.6 1.8 %collective-permute-start.3 = (f32[1,128,512]{2,1,0:T(8,128)S(1)}, f32[1,128,512]{2,1,0:T(8,128)S(1)}, u32[]{:S(2)}, u32[]{:S(2)}) collective-permute-start(f32[1,128,512]{2,1,0:T(8,128)S(1)} %get-tuple-element.40), channel_id=1, source_target_pairs={{0,4},{4,0},{8,12},{12,8},{16,20},{20,16},{24,28},{28,24},{1,5},{5... | collective-permute-start | bytes 786440 | tf_op jit(solution)/shard_map/ppermute | solution.py:502
  8.2 9.9 %collective-permute-start.5 = (f32[4,72,128]{2,1,0:T(8,128)S(1)}, f32[4,72,128]{2,1,0:T(8,128)S(1)}, u32[]{:S(2)}, u32[]{:S(2)}) collective-permute-start(f32[4,72,128]{2,1,0:T(8,128)S(1)} %get-tuple-element.46), channel_id=1, source_target_pairs={{0,16},{4,20},{8,24},{12,28},{16,0},{20,4},{24,8},{28,12},{1,17},{... | collective-permute-start | bytes 442376 | tf_op jit(solution)/shard_map/ppermute | solution.py:502
  11.2 7.6 %collective-permute-start.6 = (f32[4,72,128]{2,1,0:T(8,128)S(1)}, f32[4,72,128]{2,1,0:T(8,128)S(1)}, u32[]{:S(2)}, u32[]{:S(2)}) collective-permute-start(f32[4,72,128]{2,1,0:T(8,128)S(1)} %get-tuple-element.47), channel_id=1, source_target_pairs={{0,24},{4,28},{8,16},{12,20},{16,8},{20,12},{24,0},{28,4},{1,25},{... | collective-permute-start | bytes 442376 | tf_op jit(solution)/shard_map/ppermute | solution.py:502
  12.6 7.2 %collective-permute-start.4 = (f32[4,72,128]{2,1,0:T(8,128)S(1)}, f32[4,72,128]{2,1,0:T(8,128)S(1)}, u32[]{:S(2)}, u32[]{:S(2)}) collective-permute-start(f32[4,72,128]{2,1,0:T(8,128)S(1)} %get-tuple-element.42.after), channel_id=1, source_target_pairs={{0,8},{4,12},{8,0},{12,4},{16,24},{20,28},{24,16},{28,20},{1,9},{5... | collective-permute-start | bytes 442376 | tf_op jit(solution)/shard_map/ppermute | solution.py:502
  19.8 23.1 %collective-permute-start.10 = (f32[2,128,512]{2,1,0:T(8,128)}, f32[2,128,512]{2,1,0:T(8,128)S(1)}, u32[]{:S(2)}, u32[]{:S(2)}) collective-permute-start(f32[2,128,512]{2,1,0:T(8,128)} %get-tuple-element.55), channel_id=1, source_target_pairs={{0,8},{4,12},{8,0},{12,4},{16,24},{20,28},{24,16},{28,20},{1,9},{5... | collective-permute-start | bytes 1572872 | tf_op jit(solution)/shard_map/ppermute | solution.py:502
  21.4 24.0 %collective-permute-start.11 = (f32[2,128,512]{2,1,0:T(8,128)}, f32[2,128,512]{2,1,0:T(8,128)S(1)}, u32[]{:S(2)}, u32[]{:S(2)}) collective-permute-start(f32[2,128,512]{2,1,0:T(8,128)} %get-tuple-element.56), channel_id=1, source_target_pairs={{0,16},{4,20},{8,24},{12,28},{16,0},{20,4},{24,8},{28,12},{1,17},{... | collective-permute-start | bytes 1572872 | tf_op jit(solution)/shard_map/ppermute | solution.py:502
  23.0 22.5 %collective-permute-start.12 = (f32[2,128,512]{2,1,0:T(8,128)S(1)}, f32[2,128,512]{2,1,0:T(8,128)S(1)}, u32[]{:S(2)}, u32[]{:S(2)}) collective-permute-start(f32[2,128,512]{2,1,0:T(8,128)S(1)} %get-tuple-element.57), channel_id=1, source_target_pairs={{0,24},{4,28},{8,16},{12,20},{16,8},{20,12},{24,0},{28,4},{1,25},{... | collective-permute-start | bytes 1572872 | tf_op jit(solution)/shard_map/ppermute | solution.py:502
  23.3 4.4 %collective-permute-start.7 = (f32[2,72,128]{2,1,0:T(8,128)S(1)}, f32[2,72,128]{2,1,0:T(8,128)S(1)}, u32[]{:S(2)}, u32[]{:S(2)}) collective-permute-start(f32[2,72,128]{2,1,0:T(8,128)S(1)} %get-tuple-element.52), channel_id=1, source_target_pairs={{0,1},{1,0},{2,3},{3,2},{4,5},{5,4},{6,7},{7,6},{8,9},{9,8},{10,11... | collective-permute-start | bytes 221192 | tf_op jit(solution)/shard_map/ppermute | solution.py:502
  27.8 5.4 %collective-permute-start.8 = (f32[2,72,128]{2,1,0:T(8,128)S(1)}, f32[2,72,128]{2,1,0:T(8,128)S(1)}, u32[]{:S(2)}, u32[]{:S(2)}) collective-permute-start(f32[2,72,128]{2,1,0:T(8,128)S(1)} %add.14), channel_id=1, source_target_pairs={{0,2},{1,3},{2,0},{3,1},{4,6},{5,7},{6,4},{7,5},{8,10},{9,11},{10,... | collective-permute-start | bytes 221192 | tf_op jit(solution)/shard_map/ppermute | solution.py:502
  33.2 4.4 %collective-permute-start.9 = (f32[2,72,128]{2,1,0:T(8,128)S(1)}, f32[2,72,128]{2,1,0:T(8,128)S(1)}, u32[]{:S(2)}, u32[]{:S(2)}) collective-permute-start(f32[2,72,128]{2,1,0:T(8,128)S(1)} %add.15.refs_0_), channel_id=1, source_target_pairs={{0,1},{1,0},{2,3},{3,2},{4,5},{5,4},{6,7},{7,6},{8,9},{9,8},{10,11... | collective-permute-start | bytes 221192 | tf_op jit(solution)/shard_map/ppermute | solution.py:502
  46.5 1.6 %collective-permute-start.13 = (f32[520,128]{1,0:T(8,128)S(1)}, f32[520,128]{1,0:T(8,128)S(1)}, u32[]{:S(2)}, u32[]{:S(2)}) collective-permute-start(f32[520,128]{1,0:T(8,128)S(1)} %get-tuple-element.58), channel_id=1, source_target_pairs={{0,4},{4,0},{8,12},{12,8},{16,20},{20,16},{24,28},{28,24},{1,5},{5... | collective-permute-start | bytes 798728 | tf_op jit(solution)/shard_map/ppermute | solution.py:497
  46.6 9.1 %collective-permute-start.14 = (f32[512,128]{1,0:T(8,128)S(1)}, f32[512,128]{1,0:T(8,128)S(1)}, u32[]{:S(2)}, u32[]{:S(2)}) collective-permute-start(f32[512,128]{1,0:T(8,128)S(1)} %get-tuple-element.60), channel_id=1, source_target_pairs={{4,8},{8,4},{12,16},{16,12},{20,24},{24,20},{5,9},{9,5},{13,17},{1... | collective-permute-start | bytes 786440 | tf_op jit(solution)/shard_map/ppermute | solution.py:497
  48.1 7.9 %collective-permute-start.17 = (f32[8,128]{1,0:T(8,128)S(1)}, f32[8,128]{1,0:T(8,128)S(1)}, u32[]{:S(2)}, u32[]{:S(2)}) collective-permute-start(f32[8,128]{1,0:T(8,128)S(1)} %slice_add_fusion.refs_1_), channel_id=1, source_target_pairs={{0,24},{4,28},{8,16},{12,20},{16,8},{20,12},{24,0},{28,4},{1,25},{... | collective-permute-start | bytes 12296 | tf_op jit(solution)/shard_map/ppermute | solution.py:502
  51.7 4.4 %collective-permute-start.16 = (f32[8,128]{1,0:T(8,128)S(1)}, f32[8,128]{1,0:T(8,128)S(1)}, u32[]{:S(2)}, u32[]{:S(2)}) collective-permute-start(f32[8,128]{1,0:T(8,128)S(1)} %slice_add_fusion.refs_1_), channel_id=1, source_target_pairs={{0,16},{4,20},{8,24},{12,28},{16,0},{20,4},{24,8},{28,12},{1,17},{... | collective-permute-start | bytes 12296 | tf_op jit(solution)/shard_map/ppermute | solution.py:502
  52.2 5.5 %collective-permute-start.15 = (f32[8,128]{1,0:T(8,128)S(1)}, f32[8,128]{1,0:T(8,128)S(1)}, u32[]{:S(2)}, u32[]{:S(2)}) collective-permute-start(f32[8,128]{1,0:T(8,128)S(1)} %slice_add_fusion.refs_1_), channel_id=1, source_target_pairs={{0,8},{4,12},{8,0},{12,4},{16,24},{20,28},{24,16},{28,20},{1,9},{5... | collective-permute-start | bytes 12296 | tf_op jit(solution)/shard_map/ppermute | solution.py:502

commit v6 on v5

--- a/solution.py
+++ b/solution.py
@@ -12,6 +12,7 @@
 ITERS = 3
 TOLERANCE = 1e-8
 LAST_ROWS = 8
+AHEAD = 3
 FAR_PARTS = 1
 GATHER_CHUNKS = 2
 GATHER_VMEM = 62 * 1024 * 1024
@@ -105,8 +106,8 @@
 
 
 def piece(refs, where, pair):
-    operand, place = where
-    return refs[operand][place, :, pair * WIDTH : (pair + 1) * WIDTH]
+    operand, place, first = where
+    return refs[operand][place, :, (first + pair) * WIDTH : (first + pair + 1) * WIDTH]
 
 
 def deal(row, held, outs):
@@ -119,7 +120,7 @@
     outs, held = refs[:-1], refs[-1]
     groups = column.shape[0]
     for pair in range(held.shape[0]):
-        held[pair] = gram([piece([column], (0, group), pair) for group in range(groups)])
+        held[pair] = gram([piece([column], (0, group, 0), pair) for group in range(groups)])
     deal(row[0], held, outs)
 
 
@@ -164,46 +165,42 @@
 PACKED = WIDTH // 2 + LAST_ROWS
 
 
-def near_grams_kernel(*refs):
-    count = len(refs) // 3
-    for place in range(count):
-        here, near, out = refs[place], refs[count + place], refs[2 * count + place]
+def near_grams_kernel(plan, *refs):
+    sources, outs = refs[: -len(plan)], refs[-len(plan) :]
+    for places, out in zip(plan, outs):
         for pair in range(out.shape[0]):
-            out[pair] = pack(gram([piece([ref], (0, 0), pair) for ref in (here, near)]))
-
-
-def near_grams(here, near):
-    pairs = here[0].shape[2] // WIDTH
-    return pl.pallas_call(
-        near_grams_kernel,
-        out_shape=(jax.ShapeDtypeStruct((pairs, PACKED, WIDTH), jnp.float32),) * len(here),
-        in_specs=[VMEM] * (2 * len(here)),
-        out_specs=(VMEM,) * len(here),
+            out[pair] = pack(gram([piece(sources, place, 0) for place in places[pair]]))
+
+
+def near_grams(plan, *sources):
+    return pl.pallas_call(
+        functools.partial(near_grams_kernel, plan),
+        out_shape=tuple(jax.ShapeDtypeStruct((len(places), PACKED, WIDTH), jnp.float32) for places in plan),
+        in_specs=[VMEM] * len(sources),
+        out_specs=(VMEM,) * len(plan),
         compiler_params=PARAMS,
         name="near_grams",
-    )(*here, *near)
-
-
-def joined_kernel(counts, after, *refs):
+    )(*sources)
+
+
+def joined_kernel(plan, after, *refs):
     del after
-    sources, outs = refs[: sum(counts)], refs[sum(counts) :]
-    for count, out in zip(counts, outs):
-        for place in range(count):
-            out[place] = sources[place][0]
-        sources = sources[count:]
-
-
-def joined(after, *sides):
-    _, rows, cols = sides[0][0].shape
-    counts = tuple(len(side) for side in sides)
-    return pl.pallas_call(
-        functools.partial(joined_kernel, counts),
-        out_shape=tuple(jax.ShapeDtypeStruct((count, rows, cols), jnp.float32) for count in counts),
-        in_specs=[pl.BlockSpec(memory_space=pl.ANY)] + [VMEM] * sum(counts),
-        out_specs=(VMEM,) * len(sides),
+    sources, outs = refs[: -len(plan)], refs[-len(plan) :]
+    for places, out in zip(plan, outs):
+        for place, (source, first) in enumerate(places):
+            out[place] = sources[source][0, :, first * WIDTH : first * WIDTH + out.shape[2]]
+
+
+def joined(after, plan, *sources):
+    rows = sources[0].shape[1]
+    return pl.pallas_call(
+        functools.partial(joined_kernel, tuple(places for _, places in plan)),
+        out_shape=tuple(jax.ShapeDtypeStruct((len(places), rows, pairs * WIDTH), jnp.float32) for pairs, places in plan),
+        in_specs=[pl.BlockSpec(memory_space=pl.ANY)] + [VMEM] * len(sources),
+        out_specs=(VMEM,) * len(plan),
         compiler_params=PARAMS,
         name="joined",
-    )(after, *[value for side in sides for value in side])
+    )(after, *sources)
 
 
 def merge_kernel(count, row, *refs):
@@ -444,7 +441,7 @@
 
 
 def finish_kernel(blocks, parts, where, mate, *refs):
-    far, sums, (_, out, ratio, tile, sems) = refs[:parts], refs[parts:-5], refs[-5:]
+    far, sums, (_, out, ratio, tile, held, sems) = refs[:parts], refs[parts:-6], refs[-6:]
     rows = mate.shape[0] // blocks
     half = rows // 2
     each = blocks // parts
@@ -455,6 +452,12 @@
     here = (lanes >= first_lane) & (lanes < first_lane + BLOCK)
     column = pl.ds(pl.multiple_of(jnp.where(odd, out.shape[1] - WIDTH, 0), WIDTH), WIDTH)
     copies = []
+    value = sums[0][...]
+    for other in sums[1:]:
+        value = value + other[...]
+    held[...] = jnp.sqrt(value[:1, :1] / value[:1, 1:2])
+    copies.append(pltpu.make_async_copy(held, ratio, sems.at[blocks]))
+    copies[-1].start()
     for block in range(blocks):
         span = pl.ds(block * rows, rows)
         own_place = jnp.bitwise_xor(where[2], block)
@@ -469,10 +472,6 @@
         own_rows = pl.ds(pl.multiple_of(own_place * rows, rows), rows)
         copies.append(pltpu.make_async_copy(tile.at[span], out.at[own_rows, column], sems.at[block]))
         copies[-1].start()
-    value = sums[0][...]
-    for other in sums[1:]:
-        value = value + other[...]
-    ratio[...] = jnp.sqrt(value[:1, :1] / value[:1, 1:2])
     for copy in copies:
         copy.wait()
 
@@ -482,9 +481,13 @@
         functools.partial(finish_kernel, blocks, len(far)),
         out_shape=(jax.ShapeDtypeStruct(rotated.shape, jnp.float32), jax.ShapeDtypeStruct((1, 1), jnp.float32)),
         in_specs=[SMEM] + [VMEM] * (1 + len(far) + len(sums)) + [HBM],
-        out_specs=(HBM, VMEM),
+        out_specs=(HBM, HBM),
         input_output_aliases={2 + len(far) + len(sums): 0},
-        scratch_shapes=[pltpu.VMEM(mate.shape, jnp.float32), pltpu.SemaphoreType.DMA((blocks,))],
+        scratch_shapes=[
+            pltpu.VMEM(mate.shape, jnp.float32),
+            pltpu.VMEM((1, 1), jnp.float32),
+            pltpu.SemaphoreType.DMA((blocks + 1,)),
+        ],
         compiler_params=PARAMS,
         name="finish",
     )(where, mate, *far, *sums, rotated)
@@ -513,26 +516,38 @@
     row = row_index.astype(jnp.int32).reshape(1)
     base = pair_index.astype(jnp.int32).reshape(1)
     if shared and pair_count == 8:
-        plan = [(local, 0, local, (position,)) for position in range(pair_count)]
+        ahead = local * AHEAD // 4
+        plan = [(local, 0, local, (position,)) for position in (0, 2, 4, 1, 3, 5, 7)]
+        plan += [(local, 0, ahead, (6,)), (local, ahead, local - ahead, (6,))]
         arranged = gather(r_factor, block_slots, base, tuple(plan))
-        here = arranged[0::2]
-        near = [swapped(value, "pair", 1) for value in arranged[1::2]]
-        own, *given = near_grams(here, near)
+        here, early, late = arranged[:3], arranged[7], arranged[8]
+        near = [swapped(value, "pair", 1) for value in arranged[3:7]]
+        early = swapped(early, "pair", 6)
+        plan = [[((side, 0, pair), (side + 3, 0, pair)) for pair in range(local)] for side in range(3)]
+        plan.append([((7, 0, pair), (6, 0, pair)) for pair in range(ahead)])
+        plan[3] += [((8, 0, pair - ahead), (6, 0, pair)) for pair in range(ahead, local)]
+        own, *given = near_grams(plan, *here, *near, arranged[7], late)
         taken = [swapped(value, "pair", by) for by, value in zip((2, 4, 6), given)]
-        going = joined(given[0], (here[1], near[1]), (here[2], near[2]), (here[3], near[3]))
-        going, taken = lax.optimization_barrier((going, taken))
+        single = tuple((4, pair) for pair in range(local)) + tuple((5, pair) for pair in range(local - ahead))
+        plan = ((local, ((0, 0), (2, 0))), (local, ((1, 0), (3, 0))), (1, single))
+        going = joined(given[0], plan, here[1], here[2], near[1], near[2], near[3], late)
+        early, going, taken = lax.optimization_barrier((early, going, taken))
         parts = merge(row, [own] + taken, shares)
         from_far = [swapped(value, "pair", by) for by, value in zip((2, 4, 6), going)]
-        columns = (here[0], near[0], *from_far)
-        places = ((0, 0), (1, 0), (2, 0), (2, 1), (3, 0), (3, 1), (4, 0), (4, 1))
-        tracks = ((local, places),)
+        columns = (here[0], near[0], early, *from_far)
+        tracks = []
+        for pair in range(local):
+            places = [(operand, place, pair) for operand, place in ((0, 0), (1, 0), (3, 0), (3, 1), (4, 0), (4, 1))]
+            places.append((2, 0, pair) if pair < ahead else (5, local + pair - ahead, 0))
+            tracks.append((1, (*places, (5, pair, 0))))
+        tracks = tuple(tracks)
         bases = (pair_index, pair_index - 1, pair_index + 1)
     else:
         (arranged,) = gather(r_factor, block_slots, base, ((local, 0, local, None),))
         column = lax.all_to_all(arranged, "pair", split_axis=0, concat_axis=0, tiled=True)
         parts = grams(row, column, shares)
         columns = (column,)
-        tracks = ((local, tuple((0, group) for group in range(pair_count))),)
+        tracks = ((local, tuple((0, group, 0) for group in range(pair_count))),)
         bases = (jnp.zeros_like(pair_index),) * 3
     if shared:
         half = parts[0] + swapped(parts[1], "row", 1)

time: 59.8 us -> 58.3 us (0.975)
  waiting for transfers between devices: 20.7 us -> 17.3 us
  starting transfers between devices: 21 us -> 23.7 us
  Pallas kernels: 14.7 us -> 14 us
    ppermute x16 -> x17, waiting for transfers between devices: 19.9 us -> 16.4 us  [swapped(): return lax.ppermute(value, axis, [(i, i ^ by) for i in range(count)])]
    ppermute x16 -> x17, starting transfers between devices: 20.3 us -> 22.9 us  [swapped(): return lax.ppermute(value, axis, [(i, i ^ by) for i in range(count)])]
  transfers between devices with their start and end apart: 18 -> 19, of which waited for: 14 -> 7; matrix products, arithmetic and copies ran while one was open for 0% -> 0% of each run, Pallas kernels for 15% -> 17%
where the time goes in v6:
time: 58.3 us; the launch traced here: 58.2 us
  starting transfers between devices  23.7 us (41%)
  waiting for transfers between devices  17.3 us (30%)
  Pallas kernels  14 us (24%)
  local copies, waits for them, and re-layouts  1.67 us (3%)
  other arithmetic  0.75 us (1%)
  between operations  0.74 us (1%)
    ppermute x17, starting transfers between devices, swapped(): return lax.ppermute(value, axis, [(i, i ^ by) for i in range(count)])  22.9 us
    ppermute x17, waiting for transfers between devices, swapped(): return lax.ppermute(value, axis, [(i, i ^ by) for i in range(count)])  16.4 us
    pallas_call x1, Pallas kernels, solve(): pl.pallas_call(functools.partial(solve_kernel, len(parts)), out_shape=(ja...  5.31 us
    pallas_call x1, Pallas kernels, place(): pl.pallas_call(functools.partial(place_kernel, tracks), out_shape=(jax.Sh...  2.8 us
    pallas_call x1, Pallas kernels, gather(): pl.pallas_call(functools.partial(gather_kernel, tuple(((local, first, pos...  1.6 us
    unnamed x2, local copies, waits for them, and re-layouts  1.59 us
    pallas_call x1, Pallas kernels, finish(): pl.pallas_call(functools.partial(finish_kernel, blocks, len(far)), out_sh...  1.49 us
  transfers between devices with their start and end apart: 19, of which 7 were waited for; matrix products, arithmetic and copies ran while one was open for 0% of the time, Pallas kernels for 17%

profile of v6, /device:TPU:0, one launch (start us, length us, event | category | flops | bytes accessed | tf_op | source)
XLA Modules:
  0.0 58.2 jit_solution(228011677566223892)
XLA Ops:
  0.6 0.7 %pad_add_fusion.slots = s32[65]{0:T(128)S(1)} fusion(s32[1]{0:T(128)} %bitcast, s32[64]{0:T(128)} %param.3), kind=kLoop, calls=%fused_computation.1 | loop fusion | flops 65 | bytes 520 | tf_op jit(solution)/shard_map/concatenate | solution.py:98
  1.4 0.0 copy-start
  1.4 1.6 %copy-done = f32[128,4096]{1,0:T(8,128)S(1)} copy-done((f32[128,4096]{1,0:T(8,128)S(1)}, f32[128,4096]{1,0:T(8,128)}, u32[]{:S(2)}) %copy-start) | copy-done | bytes 2097176
  3.0 1.6 %gather.1 = (f32[1,128,512]{2,1,0:T(8,128)S(1)}, f32[1,128,512]{2,1,0:T(8,128)S(1)}, f32[1,128,512]{2,1,0:T(8,128)S(1)}, f32[1,128,512]{2,1,0:T(8,128)S(1)}, f32...) custom-call(s32[65]{0:T(128)S(1)} %pad_add_fusion.slots, ...), custom_call_target="tpu_custom_call" | custom-call | tf_op jit(solution)/shard_map/gather/pallas_call | solution.py:91
  4.6 0.5 collective-permute-start
  5.1 0.1 collective-permute-start.1
  5.2 0.4 collective-permute-start.2
  5.6 0.1 collective-permute-start.3
  5.7 3.9 %collective-permute-start.4 = (f32[1,128,384]{2,1,0:T(8,128)S(1)}, f32[1,128,384]{2,1,0:T(8,128)S(1)}, u32[]{:S(2)}, u32[]{:S(2)}) collective-permute-start(f32[1,128,384]{2,1,0:T(8,128)S(1)} %get-tuple-element.42.refs_7_), channel_id=1, source_target_pairs={{0,24},{4,28},{8,16},{12,20},{16,8},{20,12},{24,0},{28,4},{1,25},{... | collective-permute-start | bytes 589832 | tf_op jit(solution)/shard_map/ppermute | solution.py:505
  9.5 0.0 collective-permute-done.refs_3_.refs_1_
  9.5 0.0 collective-permute-done.1.refs_4_.refs_2_
  9.5 0.0 collective-permute-done.2.refs_5_.refs_3_
  9.6 0.0 collective-permute-done.3.refs_6_.refs_4_
  9.6 0.9 %near_grams.1 = (f32[4,72,128]{2,1,0:T(8,128)S(1)}, f32[4,72,128]{2,1,0:T(8,128)S(1)}, f32[4,72,128]{2,1,0:T(8,128)S(1)}, f32[4,72,128]{2,1,0:T(8,128)S(1)}) custom-call(f32[1,128,512]{2,1,0:T(8,128)S(1)} %get-tuple-element.35.refs_0_, f32[1,128,512]{2,1,0:T(8,128)S(1)} %get-tuple-element.36.refs_1_.refs_0_, ...), custom_call_target="tpu_custom_call" | custom-call | tf_op jit(solution)/shard_map/near_grams/pallas_call | solution.py:176
  10.4 0.7 %collective-permute-start.6 = (f32[4,72,128]{2,1,0:T(8,128)S(1)}, f32[4,72,128]{2,1,0:T(8,128)S(1)}, u32[]{:S(2)}, u32[]{:S(2)}) collective-permute-start(f32[4,72,128]{2,1,0:T(8,128)S(1)} %get-tuple-element.49), channel_id=1, source_target_pairs={{0,16},{4,20},{8,24},{12,28},{16,0},{20,4},{24,8},{28,12},{1,17},{... | collective-permute-start | bytes 442376 | tf_op jit(solution)/shard_map/ppermute | solution.py:505
  11.2 1.4 %collective-permute-start.7 = (f32[4,72,128]{2,1,0:T(8,128)S(1)}, f32[4,72,128]{2,1,0:T(8,128)S(1)}, u32[]{:S(2)}, u32[]{:S(2)}) collective-permute-start(f32[4,72,128]{2,1,0:T(8,128)S(1)} %get-tuple-element.50), channel_id=1, source_target_pairs={{0,24},{4,28},{8,16},{12,20},{16,8},{20,12},{24,0},{28,4},{1,25},{... | collective-permute-start | bytes 442376 | tf_op jit(solution)/shard_map/ppermute | solution.py:505
  12.6 1.4 %collective-permute-start.5 = (f32[4,72,128]{2,1,0:T(8,128)S(1)}, f32[4,72,128]{2,1,0:T(8,128)S(1)}, u32[]{:S(2)}, u32[]{:S(2)}) collective-permute-start(f32[4,72,128]{2,1,0:T(8,128)S(1)} %get-tuple-element.45.after), channel_id=1, source_target_pairs={{0,8},{4,12},{8,0},{12,4},{16,24},{20,28},{24,16},{28,20},{1,9},{5... | collective-permute-start | bytes 442376 | tf_op jit(solution)/shard_map/ppermute | solution.py:505
  14.0 0.9 %joined.1 = (f32[2,128,512]{2,1,0:T(8,128)}, f32[2,128,512]{2,1,0:T(8,128)S(1)}, f32[5,128,128]{2,1,0:T(8,128)S(1)}) custom-call(f32[4,72,128]{2,1,0:T(8,128)S(1)} %get-tuple-element.45.after, f32[1,128,512]{2,1,0:T(8,128)S(1)} %get-tuple-element.36.refs_1_.refs_0_, f32[1,128,512]{2,1,0:T(8,128)S(1)} %get-tuple-element.37.refs_2_.refs_1_, ...), custom_call_target="tpu_custom_call" | custom-call | tf_op jit(solution)/shard_map/joined/pallas_call | solution.py:196
  14.9 0.0 collective-permute-done.4.refs_2_
  14.9 6.1 %collective-permute-done.6.refs_2_ = f32[4,72,128]{2,1,0:T(8,128)S(1)} collective-permute-done((f32[4,72,128]{2,1,0:T(8,128)S(1)}, f32[4,72,128]{2,1,0:T(8,128)S(1)}, u32[]{:S(2)}, u32[]{:S(2)}) %collective-permute-start.6) | collective-permute-done | bytes 147488 | tf_op jit(solution)/shard_map/ppermute | solution.py:505
  21.0 0.0 collective-permute-done.7.refs_3_
  21.0 0.3 collective-permute-done.5.refs_1_
  21.3 1.5 %collective-permute-start.11 = (f32[2,128,512]{2,1,0:T(8,128)}, f32[2,128,512]{2,1,0:T(8,128)S(1)}, u32[]{:S(2)}, u32[]{:S(2)}) collective-permute-start(f32[2,128,512]{2,1,0:T(8,128)} %get-tuple-element.59), channel_id=1, source_target_pairs={{0,8},{4,12},{8,0},{12,4},{16,24},{20,28},{24,16},{28,20},{1,9},{5... | collective-permute-start | bytes 1572872 | tf_op jit(solution)/shard_map/ppermute | solution.py:505
  22.8 1.4 %collective-permute-start.12 = (f32[2,128,512]{2,1,0:T(8,128)S(1)}, f32[2,128,512]{2,1,0:T(8,128)S(1)}, u32[]{:S(2)}, u32[]{:S(2)}) collective-permute-start(f32[2,128,512]{2,1,0:T(8,128)S(1)} %get-tuple-element.60), channel_id=1, source_target_pairs={{0,16},{4,20},{8,24},{12,28},{16,0},{20,4},{24,8},{28,12},{1,17},{... | collective-permute-start | bytes 1572872 | tf_op jit(solution)/shard_map/ppermute | solution.py:505
  24.2 0.6 collective-permute-start.13
  24.8 1.6 %collective-permute-start.8 = (f32[2,72,128]{2,1,0:T(8,128)S(1)}, f32[2,72,128]{2,1,0:T(8,128)S(1)}, u32[]{:S(2)}, u32[]{:S(2)}) collective-permute-start(f32[2,72,128]{2,1,0:T(8,128)S(1)} %get-tuple-element.55), channel_id=1, source_target_pairs={{0,1},{1,0},{2,3},{3,2},{4,5},{5,4},{6,7},{7,6},{8,9},{9,8},{10,11... | collective-permute-start | bytes 221192 | tf_op jit(solution)/shard_map/ppermute | solution.py:505
  26.5 2.8 %collective-permute-done.8 = f32[2,72,128]{2,1,0:T(8,128)S(1)} collective-permute-done((f32[2,72,128]{2,1,0:T(8,128)S(1)}, f32[2,72,128]{2,1,0:T(8,128)S(1)}, u32[]{:S(2)}, u32[]{:S(2)}) %collective-permute-start.8) | collective-permute-done | bytes 73760 | tf_op jit(solution)/shard_map/ppermute | solution.py:505
  29.3 2.7 %collective-permute-start.9 = (f32[2,72,128]{2,1,0:T(8,128)S(1)}, f32[2,72,128]{2,1,0:T(8,128)S(1)}, u32[]{:S(2)}, u32[]{:S(2)}) collective-permute-start(f32[2,72,128]{2,1,0:T(8,128)S(1)} %add.14), channel_id=1, source_target_pairs={{0,2},{1,3},{2,0},{3,1},{4,6},{5,7},{6,4},{7,5},{8,10},{9,11},{10,... | collective-permute-start | bytes 221192 | tf_op jit(solution)/shard_map/ppermute | solution.py:505
  31.9 2.7 %collective-permute-done.9 = f32[2,72,128]{2,1,0:T(8,128)S(1)} collective-permute-done((f32[2,72,128]{2,1,0:T(8,128)S(1)}, f32[2,72,128]{2,1,0:T(8,128)S(1)}, u32[]{:S(2)}, u32[]{:S(2)}) %collective-permute-start.9) | collective-permute-done | bytes 73760 | tf_op jit(solution)/shard_map/ppermute | solution.py:505
  34.6 1.6 %collective-permute-start.10 = (f32[2,72,128]{2,1,0:T(8,128)S(1)}, f32[2,72,128]{2,1,0:T(8,128)S(1)}, u32[]{:S(2)}, u32[]{:S(2)}) collective-permute-start(f32[2,72,128]{2,1,0:T(8,128)S(1)} %add.15.refs_0_), channel_id=1, source_target_pairs={{0,1},{1,0},{2,3},{3,2},{4,5},{5,4},{6,7},{7,6},{8,9},{9,8},{10,11... | collective-permute-start | bytes 221192 | tf_op jit(solution)/shard_map/ppermute | solution.py:505
  36.2 0.1 stack.19.where
  36.3 2.7 %collective-permute-done.10.refs_1_ = f32[2,72,128]{2,1,0:T(8,128)S(1)} collective-permute-done((f32[2,72,128]{2,1,0:T(8,128)S(1)}, f32[2,72,128]{2,1,0:T(8,128)S(1)}, u32[]{:S(2)}, u32[]{:S(2)}) %collective-permute-start.10) | collective-permute-done | bytes 73760 | tf_op jit(solution)/shard_map/ppermute | solution.py:505
  39.0 5.3 %solve.1 = (f32[4,128,128]{2,1,0:T(8,128)S(1)}, f32[8,128]{1,0:T(8,128)S(1)}) custom-call(s32[1]{0:T(128)} %bitcast.4.row, f32[2,72,128]{2,1,0:T(8,128)S(1)} %add.15.refs_0_, f32[2,72,128]{2,1,0:T(8,128)S(1)} %collective-permute-done.10.refs_1_), custom_call_target="tpu_custom_call" | custom-call | tf_op jit(solution)/shard_map/solve/pallas_call | solution.py:325
  44.4 0.0 collective-permute-done.13.refs_5_
  44.4 0.0 collective-permute-done.11.refs_3_
  44.4 0.0 collective-permute-done.12.refs_4_
  44.4 1.1 %edges.1 = (f32[520,128]{1,0:T(8,128)S(1)}, f32[512,128]{1,0:T(8,128)S(1)}) custom-call(s32[5]{0:T(128)S(1)} %stack.19.where, f32[8,128]{1,0:T(8,128)S(1)} %get-tuple-element.56.sums, f32[4,128,128]{2,1,0:T(8,128)S(1)} %get-tuple-element.57.held, f32[1,128,512]{2,1,0:T(8,128)S(1)} %get-tuple-element.35.refs_0_, ...), custom_call_target="tpu_custom_call" | custom-call | tf_op jit(solution)/shard_map/edges/pallas_call | solution.py:378
  45.5 0.1 collective-permute-start.14
  45.5 0.7 %collective-permute-start.15 = (f32[512,128]{1,0:T(8,128)S(1)}, f32[512,128]{1,0:T(8,128)S(1)}, u32[]{:S(2)}, u32[]{:S(2)}) collective-permute-start(f32[512,128]{1,0:T(8,128)S(1)} %get-tuple-element.64), channel_id=1, source_target_pairs={{4,8},{8,4},{12,16},{16,12},{20,24},{24,20},{5,9},{9,5},{13,17},{1... | collective-permute-start | bytes 786440 | tf_op jit(solution)/shard_map/ppermute | solution.py:500
  46.2 0.8 %collective-permute-done.14.near = f32[520,128]{1,0:T(8,128)S(1)} collective-permute-done((f32[520,128]{1,0:T(8,128)S(1)}, f32[520,128]{1,0:T(8,128)S(1)}, u32[]{:S(2)}, u32[]{:S(2)}) %collective-permute-start.14) | collective-permute-done | bytes 266272 | tf_op jit(solution)/shard_map/ppermute | solution.py:500
  47.1 3.4 %collective-permute-start.18 = (f32[8,128]{1,0:T(8,128)S(1)}, f32[8,128]{1,0:T(8,128)S(1)}, u32[]{:S(2)}, u32[]{:S(2)}) collective-permute-start(f32[8,128]{1,0:T(8,128)S(1)} %slice_add_fusion.refs_1_), channel_id=1, source_target_pairs={{0,24},{4,28},{8,16},{12,20},{16,8},{20,12},{24,0},{28,4},{1,25},{... | collective-permute-start | bytes 12296 | tf_op jit(solution)/shard_map/ppermute | solution.py:505
  50.5 0.6 %collective-permute-start.17 = (f32[8,128]{1,0:T(8,128)S(1)}, f32[8,128]{1,0:T(8,128)S(1)}, u32[]{:S(2)}, u32[]{:S(2)}) collective-permute-start(f32[8,128]{1,0:T(8,128)S(1)} %slice_add_fusion.refs_1_), channel_id=1, source_target_pairs={{0,16},{4,20},{8,24},{12,28},{16,0},{20,4},{24,8},{28,12},{1,17},{... | collective-permute-start | bytes 12296 | tf_op jit(solution)/shard_map/ppermute | solution.py:505
  51.1 0.9 %collective-permute-start.16 = (f32[8,128]{1,0:T(8,128)S(1)}, f32[8,128]{1,0:T(8,128)S(1)}, u32[]{:S(2)}, u32[]{:S(2)}) collective-permute-start(f32[8,128]{1,0:T(8,128)S(1)} %slice_add_fusion.refs_1_), channel_id=1, source_target_pairs={{0,8},{4,12},{8,0},{12,4},{16,24},{20,28},{24,16},{28,20},{1,9},{5... | collective-permute-start | bytes 12296 | tf_op jit(solution)/shard_map/ppermute | solution.py:505
  52.0 2.8 %place.1 = (f32[1024,512]{1,0:T(8,128)}, f32[1024,128]{1,0:T(8,128)S(1)}) custom-call(s32[5]{0:T(128)S(1)} %stack.19.where, f32[520,128]{1,0:T(8,128)S(1)} %collective-permute-done.14.near, f32[4,128,128]{2,1,0:T(8,128)S(1)} %get-tuple-element.57.held, f32[1,128,512]{2,1,0:T(8,128)S(1)} %get-tuple-element.35.refs_0_, ...), custom_call_target="tpu_custom_call" | custom-call | tf_op jit(solution)/shard_map/place/pallas_call | solution.py:430
  54.8 0.0 collective-permute-done.15.refs_0_
  54.8 0.0 collective-permute-done.18.refs_4_
  54.9 0.0 collective-permute-done.17.refs_3_
  54.9 1.8 %collective-permute-done.16.refs_2_ = f32[8,128]{1,0:T(8,128)S(1)} collective-permute-done((f32[8,128]{1,0:T(8,128)S(1)}, f32[8,128]{1,0:T(8,128)S(1)}, u32[]{:S(2)}, u32[]{:S(2)}) %collective-permute-start.16) | collective-permute-done | bytes 4128 | tf_op jit(solution)/shard_map/ppermute | solution.py:505
  56.7 1.5 %finish.1 = (f32[1024,512]{1,0:T(8,128)}, f32[1,1]{1,0:T(1,128)}) custom-call(s32[5]{0:T(128)S(1)} %stack.19.where, f32[1024,128]{1,0:T(8,128)S(1)} %get-tuple-element.63.mate, f32[512,128]{1,0:T(8,128)S(1)} %collective-permute-done.15.refs_0_, f32[8,128]{1,0:T(8,128)S(1)} %slice_add_fusion.refs_1_, ...), custom_call_target="tpu_custom_call", output_to_operand_aliasing={{0}: (7, {})} | custom-call | tf_op jit(solution)/shard_map/finish/pallas_call | solution.py:480
  (4 shorter events, 0.1 us)
Async XLA Ops:
  1.4 1.6 %copy-start = (f32[128,4096]{1,0:T(8,128)S(1)}, f32[128,4096]{1,0:T(8,128)}, u32[]{:S(2)}) copy-start(f32[128,4096]{1,0:T(8,128)} %source.1) | copy-start | bytes 6291460
  4.6 5.0 %collective-permute-start = (f32[1,128,512]{2,1,0:T(8,128)S(1)}, f32[1,128,512]{2,1,0:T(8,128)S(1)}, u32[]{:S(2)}, u32[]{:S(2)}) collective-permute-start(f32[1,128,512]{2,1,0:T(8,128)S(1)} %get-tuple-element.38), channel_id=1, source_target_pairs={{0,4},{4,0},{8,12},{12,8},{16,20},{20,16},{24,28},{28,24},{1,5},{5... | collective-permute-start | bytes 786440 | tf_op jit(solution)/shard_map/ppermute | solution.py:505
  5.1 4.5 %collective-permute-start.1 = (f32[1,128,512]{2,1,0:T(8,128)S(1)}, f32[1,128,512]{2,1,0:T(8,128)S(1)}, u32[]{:S(2)}, u32[]{:S(2)}) collective-permute-start(f32[1,128,512]{2,1,0:T(8,128)S(1)} %get-tuple-element.39), channel_id=1, source_target_pairs={{0,4},{4,0},{8,12},{12,8},{16,20},{20,16},{24,28},{28,24},{1,5},{5... | collective-permute-start | bytes 786440 | tf_op jit(solution)/shard_map/ppermute | solution.py:505
  5.2 4.4 %collective-permute-start.2 = (f32[1,128,512]{2,1,0:T(8,128)S(1)}, f32[1,128,512]{2,1,0:T(8,128)S(1)}, u32[]{:S(2)}, u32[]{:S(2)}) collective-permute-start(f32[1,128,512]{2,1,0:T(8,128)S(1)} %get-tuple-element.40), channel_id=1, source_target_pairs={{0,4},{4,0},{8,12},{12,8},{16,20},{20,16},{24,28},{28,24},{1,5},{5... | collective-permute-start | bytes 786440 | tf_op jit(solution)/shard_map/ppermute | solution.py:505
  5.6 4.0 %collective-permute-start.3 = (f32[1,128,512]{2,1,0:T(8,128)S(1)}, f32[1,128,512]{2,1,0:T(8,128)S(1)}, u32[]{:S(2)}, u32[]{:S(2)}) collective-permute-start(f32[1,128,512]{2,1,0:T(8,128)S(1)} %get-tuple-element.41), channel_id=1, source_target_pairs={{0,4},{4,0},{8,12},{12,8},{16,20},{20,16},{24,28},{28,24},{1,5},{5... | collective-permute-start | bytes 786440 | tf_op jit(solution)/shard_map/ppermute | solution.py:505
  5.7 9.2 %collective-permute-start.4 = (f32[1,128,384]{2,1,0:T(8,128)S(1)}, f32[1,128,384]{2,1,0:T(8,128)S(1)}, u32[]{:S(2)}, u32[]{:S(2)}) collective-permute-start(f32[1,128,384]{2,1,0:T(8,128)S(1)} %get-tuple-element.42.refs_7_), channel_id=1, source_target_pairs={{0,24},{4,28},{8,16},{12,20},{16,8},{20,12},{24,0},{28,4},{1,25},{... | collective-permute-start | bytes 589832 | tf_op jit(solution)/shard_map/ppermute | solution.py:505
  10.4 10.6 %collective-permute-start.6 = (f32[4,72,128]{2,1,0:T(8,128)S(1)}, f32[4,72,128]{2,1,0:T(8,128)S(1)}, u32[]{:S(2)}, u32[]{:S(2)}) collective-permute-start(f32[4,72,128]{2,1,0:T(8,128)S(1)} %get-tuple-element.49), channel_id=1, source_target_pairs={{0,16},{4,20},{8,24},{12,28},{16,0},{20,4},{24,8},{28,12},{1,17},{... | collective-permute-start | bytes 442376 | tf_op jit(solution)/shard_map/ppermute | solution.py:505
  11.2 9.8 %collective-permute-start.7 = (f32[4,72,128]{2,1,0:T(8,128)S(1)}, f32[4,72,128]{2,1,0:T(8,128)S(1)}, u32[]{:S(2)}, u32[]{:S(2)}) collective-permute-start(f32[4,72,128]{2,1,0:T(8,128)S(1)} %get-tuple-element.50), channel_id=1, source_target_pairs={{0,24},{4,28},{8,16},{12,20},{16,8},{20,12},{24,0},{28,4},{1,25},{... | collective-permute-start | bytes 442376 | tf_op jit(solution)/shard_map/ppermute | solution.py:505
  12.6 8.7 %collective-permute-start.5 = (f32[4,72,128]{2,1,0:T(8,128)S(1)}, f32[4,72,128]{2,1,0:T(8,128)S(1)}, u32[]{:S(2)}, u32[]{:S(2)}) collective-permute-start(f32[4,72,128]{2,1,0:T(8,128)S(1)} %get-tuple-element.45.after), channel_id=1, source_target_pairs={{0,8},{4,12},{8,0},{12,4},{16,24},{20,28},{24,16},{28,20},{1,9},{5... | collective-permute-start | bytes 442376 | tf_op jit(solution)/shard_map/ppermute | solution.py:505
  21.3 23.1 %collective-permute-start.11 = (f32[2,128,512]{2,1,0:T(8,128)}, f32[2,128,512]{2,1,0:T(8,128)S(1)}, u32[]{:S(2)}, u32[]{:S(2)}) collective-permute-start(f32[2,128,512]{2,1,0:T(8,128)} %get-tuple-element.59), channel_id=1, source_target_pairs={{0,8},{4,12},{8,0},{12,4},{16,24},{20,28},{24,16},{28,20},{1,9},{5... | collective-permute-start | bytes 1572872 | tf_op jit(solution)/shard_map/ppermute | solution.py:505
  22.8 21.6 %collective-permute-start.12 = (f32[2,128,512]{2,1,0:T(8,128)S(1)}, f32[2,128,512]{2,1,0:T(8,128)S(1)}, u32[]{:S(2)}, u32[]{:S(2)}) collective-permute-start(f32[2,128,512]{2,1,0:T(8,128)S(1)} %get-tuple-element.60), channel_id=1, source_target_pairs={{0,16},{4,20},{8,24},{12,28},{16,0},{20,4},{24,8},{28,12},{1,17},{... | collective-permute-start | bytes 1572872 | tf_op jit(solution)/shard_map/ppermute | solution.py:505
  24.2 20.1 %collective-permute-start.13 = (f32[5,128,128]{2,1,0:T(8,128)S(1)}, f32[5,128,128]{2,1,0:T(8,128)S(1)}, u32[]{:S(2)}, u32[]{:S(2)}) collective-permute-start(f32[5,128,128]{2,1,0:T(8,128)S(1)} %get-tuple-element.61), channel_id=1, source_target_pairs={{0,24},{4,28},{8,16},{12,20},{16,8},{20,12},{24,0},{28,4},{1,25},{... | collective-permute-start | bytes 983048 | tf_op jit(solution)/shard_map/ppermute | solution.py:505
  24.8 4.4 %collective-permute-start.8 = (f32[2,72,128]{2,1,0:T(8,128)S(1)}, f32[2,72,128]{2,1,0:T(8,128)S(1)}, u32[]{:S(2)}, u32[]{:S(2)}) collective-permute-start(f32[2,72,128]{2,1,0:T(8,128)S(1)} %get-tuple-element.55), channel_id=1, source_target_pairs={{0,1},{1,0},{2,3},{3,2},{4,5},{5,4},{6,7},{7,6},{8,9},{9,8},{10,11... | collective-permute-start | bytes 221192 | tf_op jit(solution)/shard_map/ppermute | solution.py:505
  29.3 5.3 %collective-permute-start.9 = (f32[2,72,128]{2,1,0:T(8,128)S(1)}, f32[2,72,128]{2,1,0:T(8,128)S(1)}, u32[]{:S(2)}, u32[]{:S(2)}) collective-permute-start(f32[2,72,128]{2,1,0:T(8,128)S(1)} %add.14), channel_id=1, source_target_pairs={{0,2},{1,3},{2,0},{3,1},{4,6},{5,7},{6,4},{7,5},{8,10},{9,11},{10,... | collective-permute-start | bytes 221192 | tf_op jit(solution)/shard_map/ppermute | solution.py:505
  34.6 4.4 %collective-permute-start.10 = (f32[2,72,128]{2,1,0:T(8,128)S(1)}, f32[2,72,128]{2,1,0:T(8,128)S(1)}, u32[]{:S(2)}, u32[]{:S(2)}) collective-permute-start(f32[2,72,128]{2,1,0:T(8,128)S(1)} %add.15.refs_0_), channel_id=1, source_target_pairs={{0,1},{1,0},{2,3},{3,2},{4,5},{5,4},{6,7},{7,6},{8,9},{9,8},{10,11... | collective-permute-start | bytes 221192 | tf_op jit(solution)/shard_map/ppermute | solution.py:505
  45.5 1.6 %collective-permute-start.14 = (f32[520,128]{1,0:T(8,128)S(1)}, f32[520,128]{1,0:T(8,128)S(1)}, u32[]{:S(2)}, u32[]{:S(2)}) collective-permute-start(f32[520,128]{1,0:T(8,128)S(1)} %get-tuple-element.62), channel_id=1, source_target_pairs={{0,4},{4,0},{8,12},{12,8},{16,20},{20,16},{24,28},{28,24},{1,5},{5... | collective-permute-start | bytes 798728 | tf_op jit(solution)/shard_map/ppermute | solution.py:500
  45.5 9.3 %collective-permute-start.15 = (f32[512,128]{1,0:T(8,128)S(1)}, f32[512,128]{1,0:T(8,128)S(1)}, u32[]{:S(2)}, u32[]{:S(2)}) collective-permute-start(f32[512,128]{1,0:T(8,128)S(1)} %get-tuple-element.64), channel_id=1, source_target_pairs={{4,8},{8,4},{12,16},{16,12},{20,24},{24,20},{5,9},{9,5},{13,17},{1... | collective-permute-start | bytes 786440 | tf_op jit(solution)/shard_map/ppermute | solution.py:500
  47.1 7.8 %collective-permute-start.18 = (f32[8,128]{1,0:T(8,128)S(1)}, f32[8,128]{1,0:T(8,128)S(1)}, u32[]{:S(2)}, u32[]{:S(2)}) collective-permute-start(f32[8,128]{1,0:T(8,128)S(1)} %slice_add_fusion.refs_1_), channel_id=1, source_target_pairs={{0,24},{4,28},{8,16},{12,20},{16,8},{20,12},{24,0},{28,4},{1,25},{... | collective-permute-start | bytes 12296 | tf_op jit(solution)/shard_map/ppermute | solution.py:505
  50.5 4.4 %collective-permute-start.17 = (f32[8,128]{1,0:T(8,128)S(1)}, f32[8,128]{1,0:T(8,128)S(1)}, u32[]{:S(2)}, u32[]{:S(2)}) collective-permute-start(f32[8,128]{1,0:T(8,128)S(1)} %slice_add_fusion.refs_1_), channel_id=1, source_target_pairs={{0,16},{4,20},{8,24},{12,28},{16,0},{20,4},{24,8},{28,12},{1,17},{... | collective-permute-start | bytes 12296 | tf_op jit(solution)/shard_map/ppermute | solution.py:505
  51.1 5.6 %collective-permute-start.16 = (f32[8,128]{1,0:T(8,128)S(1)}, f32[8,128]{1,0:T(8,128)S(1)}, u32[]{:S(2)}, u32[]{:S(2)}) collective-permute-start(f32[8,128]{1,0:T(8,128)S(1)} %slice_add_fusion.refs_1_), channel_id=1, source_target_pairs={{0,8},{4,12},{8,0},{12,4},{16,24},{20,28},{24,16},{28,20},{1,9},{5... | collective-permute-start | bytes 12296 | tf_op jit(solution)/shard_map/ppermute | solution.py:505

commit v7 on v6

--- a/solution.py
+++ b/solution.py
@@ -233,7 +233,8 @@
         diag_part = jnp.where(on_diag, gram_now, 0.0)
         across = jnp.sum(diag_part, axis=1, keepdims=True)
         down = jnp.sum(diag_part, axis=0, keepdims=True)
-        skews.append(gram_now * (across - down) / (2.0 * (across * across + down * down)))
+        skew = gram_now * (across - down) / (2.0 * (across * across + down * down))
+        skews.append(jnp.clip(skew, -0.25, 0.25))
     for skew in skews:
         skews_parts.append(split(skew))
         squares.append(product(skews_parts[-1], skews_parts[-1]))
@@ -275,7 +276,21 @@
 
     worst = worst * worst
     worst = worst * worst
-    lax.while_loop(more, step, (worst * worst)[0, 0])
+    left = (worst * worst)[0, 0]
+    lax.while_loop(more, step, left)
+
+    def refine(_, carry):
+        for index in range(len(grams_now)):
+            parts = split(skews[index])
+            even_now, odd_now = even[index], odd[index]
+            even_parts, odd_parts = split(even_now), split(odd_now)
+            even_rest = split(diag_one - even_now + product(parts, odd_parts))
+            odd_rest = split(product(parts, even_parts) - odd_now)
+            even[index] = even_now + product(even_parts, even_rest) + product(odd_parts, odd_rest)
+            odd[index] = odd_now + product(even_parts, odd_rest) + product(odd_parts, even_rest)
+        return carry
+
+    lax.fori_loop(0, jnp.where(left > TOLERANCE, 2, 0), refine, 0)
     results = []
     for index in range(len(grams_now)):
         even_now = 2.0 * even[index] - diag_one

time: 58.3 us -> 58.3 us (level)
  no operation moved by 1% of the time
where the time goes in v7:
time: 58.3 us; the launch traced here: 58.2 us
  starting transfers between devices  23.7 us (41%)
  waiting for transfers between devices  17.3 us (30%)
  Pallas kernels  14 us (24%)
  local copies, waits for them, and re-layouts  1.67 us (3%)
  other arithmetic  0.75 us (1%)
  between operations  0.74 us (1%)
    ppermute x17, starting transfers between devices, swapped(): return lax.ppermute(value, axis, [(i, i ^ by) for i in range(count)])  22.9 us
    ppermute x17, waiting for transfers between devices, swapped(): return lax.ppermute(value, axis, [(i, i ^ by) for i in range(count)])  16.5 us
    pallas_call x1, Pallas kernels, solve(): pl.pallas_call(functools.partial(solve_kernel, len(parts)), out_shape=(ja...  5.29 us
    pallas_call x1, Pallas kernels, place(): pl.pallas_call(functools.partial(place_kernel, tracks), out_shape=(jax.Sh...  2.8 us
    pallas_call x1, Pallas kernels, gather(): pl.pallas_call(functools.partial(gather_kernel, tuple(((local, first, pos...  1.6 us
    unnamed x2, local copies, waits for them, and re-layouts  1.59 us
    pallas_call x1, Pallas kernels, finish(): pl.pallas_call(functools.partial(finish_kernel, blocks, len(far)), out_sh...  1.49 us
  transfers between devices with their start and end apart: 19, of which 7 were waited for; matrix products, arithmetic and copies ran while one was open for 0% of the time, Pallas kernels for 17%

profile of v7, /device:TPU:0, one launch (start us, length us, event | category | flops | bytes accessed | tf_op | source)
XLA Modules:
  0.0 58.2 jit_solution(17377404024200380487)
XLA Ops:
  0.6 0.7 %pad_add_fusion.slots = s32[65]{0:T(128)S(1)} fusion(s32[1]{0:T(128)} %bitcast, s32[64]{0:T(128)} %param.3), kind=kLoop, calls=%fused_computation.1 | loop fusion | flops 65 | bytes 520 | tf_op jit(solution)/shard_map/concatenate | solution.py:98
  1.4 0.0 copy-start
  1.4 1.6 %copy-done = f32[128,4096]{1,0:T(8,128)S(1)} copy-done((f32[128,4096]{1,0:T(8,128)S(1)}, f32[128,4096]{1,0:T(8,128)}, u32[]{:S(2)}) %copy-start) | copy-done | bytes 2097176
  3.0 1.6 %gather.1 = (f32[1,128,512]{2,1,0:T(8,128)S(1)}, f32[1,128,512]{2,1,0:T(8,128)S(1)}, f32[1,128,512]{2,1,0:T(8,128)S(1)}, f32[1,128,512]{2,1,0:T(8,128)S(1)}, f32...) custom-call(s32[65]{0:T(128)S(1)} %pad_add_fusion.slots, ...), custom_call_target="tpu_custom_call" | custom-call | tf_op jit(solution)/shard_map/gather/pallas_call | solution.py:91
  4.6 0.5 collective-permute-start
  5.1 0.1 collective-permute-start.1
  5.2 0.4 collective-permute-start.2
  5.6 0.1 collective-permute-start.3
  5.7 3.9 %collective-permute-start.4 = (f32[1,128,384]{2,1,0:T(8,128)S(1)}, f32[1,128,384]{2,1,0:T(8,128)S(1)}, u32[]{:S(2)}, u32[]{:S(2)}) collective-permute-start(f32[1,128,384]{2,1,0:T(8,128)S(1)} %get-tuple-element.42.refs_7_), channel_id=1, source_target_pairs={{0,24},{4,28},{8,16},{12,20},{16,8},{20,12},{24,0},{28,4},{1,25},{... | collective-permute-start | bytes 589832 | tf_op jit(solution)/shard_map/ppermute | solution.py:520
  9.5 0.0 collective-permute-done.refs_3_.refs_1_
  9.5 0.0 collective-permute-done.1.refs_4_.refs_2_
  9.5 0.0 collective-permute-done.2.refs_5_.refs_3_
  9.6 0.0 collective-permute-done.3.refs_6_.refs_4_
  9.6 0.9 %near_grams.1 = (f32[4,72,128]{2,1,0:T(8,128)S(1)}, f32[4,72,128]{2,1,0:T(8,128)S(1)}, f32[4,72,128]{2,1,0:T(8,128)S(1)}, f32[4,72,128]{2,1,0:T(8,128)S(1)}) custom-call(f32[1,128,512]{2,1,0:T(8,128)S(1)} %get-tuple-element.35.refs_0_, f32[1,128,512]{2,1,0:T(8,128)S(1)} %get-tuple-element.36.refs_1_.refs_0_, ...), custom_call_target="tpu_custom_call" | custom-call | tf_op jit(solution)/shard_map/near_grams/pallas_call | solution.py:176
  10.4 0.7 %collective-permute-start.6 = (f32[4,72,128]{2,1,0:T(8,128)S(1)}, f32[4,72,128]{2,1,0:T(8,128)S(1)}, u32[]{:S(2)}, u32[]{:S(2)}) collective-permute-start(f32[4,72,128]{2,1,0:T(8,128)S(1)} %get-tuple-element.49), channel_id=1, source_target_pairs={{0,16},{4,20},{8,24},{12,28},{16,0},{20,4},{24,8},{28,12},{1,17},{... | collective-permute-start | bytes 442376 | tf_op jit(solution)/shard_map/ppermute | solution.py:520
  11.2 1.4 %collective-permute-start.7 = (f32[4,72,128]{2,1,0:T(8,128)S(1)}, f32[4,72,128]{2,1,0:T(8,128)S(1)}, u32[]{:S(2)}, u32[]{:S(2)}) collective-permute-start(f32[4,72,128]{2,1,0:T(8,128)S(1)} %get-tuple-element.50), channel_id=1, source_target_pairs={{0,24},{4,28},{8,16},{12,20},{16,8},{20,12},{24,0},{28,4},{1,25},{... | collective-permute-start | bytes 442376 | tf_op jit(solution)/shard_map/ppermute | solution.py:520
  12.6 1.4 %collective-permute-start.5 = (f32[4,72,128]{2,1,0:T(8,128)S(1)}, f32[4,72,128]{2,1,0:T(8,128)S(1)}, u32[]{:S(2)}, u32[]{:S(2)}) collective-permute-start(f32[4,72,128]{2,1,0:T(8,128)S(1)} %get-tuple-element.45.after), channel_id=1, source_target_pairs={{0,8},{4,12},{8,0},{12,4},{16,24},{20,28},{24,16},{28,20},{1,9},{5... | collective-permute-start | bytes 442376 | tf_op jit(solution)/shard_map/ppermute | solution.py:520
  14.0 0.9 %joined.1 = (f32[2,128,512]{2,1,0:T(8,128)}, f32[2,128,512]{2,1,0:T(8,128)S(1)}, f32[5,128,128]{2,1,0:T(8,128)S(1)}) custom-call(f32[4,72,128]{2,1,0:T(8,128)S(1)} %get-tuple-element.45.after, f32[1,128,512]{2,1,0:T(8,128)S(1)} %get-tuple-element.36.refs_1_.refs_0_, f32[1,128,512]{2,1,0:T(8,128)S(1)} %get-tuple-element.37.refs_2_.refs_1_, ...), custom_call_target="tpu_custom_call" | custom-call | tf_op jit(solution)/shard_map/joined/pallas_call | solution.py:196
  14.9 0.0 collective-permute-done.4.refs_2_
  14.9 6.1 %collective-permute-done.6.refs_2_ = f32[4,72,128]{2,1,0:T(8,128)S(1)} collective-permute-done((f32[4,72,128]{2,1,0:T(8,128)S(1)}, f32[4,72,128]{2,1,0:T(8,128)S(1)}, u32[]{:S(2)}, u32[]{:S(2)}) %collective-permute-start.6) | collective-permute-done | bytes 147488 | tf_op jit(solution)/shard_map/ppermute | solution.py:520
  21.0 0.0 collective-permute-done.7.refs_3_
  21.0 0.3 collective-permute-done.5.refs_1_
  21.3 1.5 %collective-permute-start.11 = (f32[2,128,512]{2,1,0:T(8,128)}, f32[2,128,512]{2,1,0:T(8,128)S(1)}, u32[]{:S(2)}, u32[]{:S(2)}) collective-permute-start(f32[2,128,512]{2,1,0:T(8,128)} %get-tuple-element.59), channel_id=1, source_target_pairs={{0,8},{4,12},{8,0},{12,4},{16,24},{20,28},{24,16},{28,20},{1,9},{5... | collective-permute-start | bytes 1572872 | tf_op jit(solution)/shard_map/ppermute | solution.py:520
  22.8 1.4 %collective-permute-start.12 = (f32[2,128,512]{2,1,0:T(8,128)S(1)}, f32[2,128,512]{2,1,0:T(8,128)S(1)}, u32[]{:S(2)}, u32[]{:S(2)}) collective-permute-start(f32[2,128,512]{2,1,0:T(8,128)S(1)} %get-tuple-element.60), channel_id=1, source_target_pairs={{0,16},{4,20},{8,24},{12,28},{16,0},{20,4},{24,8},{28,12},{1,17},{... | collective-permute-start | bytes 1572872 | tf_op jit(solution)/shard_map/ppermute | solution.py:520
  24.2 0.6 collective-permute-start.13
  24.8 1.6 %collective-permute-start.8 = (f32[2,72,128]{2,1,0:T(8,128)S(1)}, f32[2,72,128]{2,1,0:T(8,128)S(1)}, u32[]{:S(2)}, u32[]{:S(2)}) collective-permute-start(f32[2,72,128]{2,1,0:T(8,128)S(1)} %get-tuple-element.55), channel_id=1, source_target_pairs={{0,1},{1,0},{2,3},{3,2},{4,5},{5,4},{6,7},{7,6},{8,9},{9,8},{10,11... | collective-permute-start | bytes 221192 | tf_op jit(solution)/shard_map/ppermute | solution.py:520
  26.5 2.8 %collective-permute-done.8 = f32[2,72,128]{2,1,0:T(8,128)S(1)} collective-permute-done((f32[2,72,128]{2,1,0:T(8,128)S(1)}, f32[2,72,128]{2,1,0:T(8,128)S(1)}, u32[]{:S(2)}, u32[]{:S(2)}) %collective-permute-start.8) | collective-permute-done | bytes 73760 | tf_op jit(solution)/shard_map/ppermute | solution.py:520
  29.3 2.7 %collective-permute-start.9 = (f32[2,72,128]{2,1,0:T(8,128)S(1)}, f32[2,72,128]{2,1,0:T(8,128)S(1)}, u32[]{:S(2)}, u32[]{:S(2)}) collective-permute-start(f32[2,72,128]{2,1,0:T(8,128)S(1)} %add.14), channel_id=1, source_target_pairs={{0,2},{1,3},{2,0},{3,1},{4,6},{5,7},{6,4},{7,5},{8,10},{9,11},{10,... | collective-permute-start | bytes 221192 | tf_op jit(solution)/shard_map/ppermute | solution.py:520
  31.9 2.7 %collective-permute-done.9 = f32[2,72,128]{2,1,0:T(8,128)S(1)} collective-permute-done((f32[2,72,128]{2,1,0:T(8,128)S(1)}, f32[2,72,128]{2,1,0:T(8,128)S(1)}, u32[]{:S(2)}, u32[]{:S(2)}) %collective-permute-start.9) | collective-permute-done | bytes 73760 | tf_op jit(solution)/shard_map/ppermute | solution.py:520
  34.6 1.6 %collective-permute-start.10 = (f32[2,72,128]{2,1,0:T(8,128)S(1)}, f32[2,72,128]{2,1,0:T(8,128)S(1)}, u32[]{:S(2)}, u32[]{:S(2)}) collective-permute-start(f32[2,72,128]{2,1,0:T(8,128)S(1)} %add.15.refs_0_), channel_id=1, source_target_pairs={{0,1},{1,0},{2,3},{3,2},{4,5},{5,4},{6,7},{7,6},{8,9},{9,8},{10,11... | collective-permute-start | bytes 221192 | tf_op jit(solution)/shard_map/ppermute | solution.py:520
  36.2 0.1 stack.19.where
  36.3 2.7 %collective-permute-done.10.refs_1_ = f32[2,72,128]{2,1,0:T(8,128)S(1)} collective-permute-done((f32[2,72,128]{2,1,0:T(8,128)S(1)}, f32[2,72,128]{2,1,0:T(8,128)S(1)}, u32[]{:S(2)}, u32[]{:S(2)}) %collective-permute-start.10) | collective-permute-done | bytes 73760 | tf_op jit(solution)/shard_map/ppermute | solution.py:520
  39.0 5.3 %solve.1 = (f32[4,128,128]{2,1,0:T(8,128)S(1)}, f32[8,128]{1,0:T(8,128)S(1)}) custom-call(s32[1]{0:T(128)} %bitcast.4.row, f32[2,72,128]{2,1,0:T(8,128)S(1)} %add.15.refs_0_, f32[2,72,128]{2,1,0:T(8,128)S(1)} %collective-permute-done.10.refs_1_), custom_call_target="tpu_custom_call" | custom-call | tf_op jit(solution)/shard_map/solve/pallas_call | solution.py:340
  44.3 0.0 collective-permute-done.13.refs_5_
  44.4 0.0 collective-permute-done.11.refs_3_
  44.4 0.0 collective-permute-done.12.refs_4_
  44.4 1.1 %edges.1 = (f32[520,128]{1,0:T(8,128)S(1)}, f32[512,128]{1,0:T(8,128)S(1)}) custom-call(s32[5]{0:T(128)S(1)} %stack.19.where, f32[8,128]{1,0:T(8,128)S(1)} %get-tuple-element.56.sums, f32[4,128,128]{2,1,0:T(8,128)S(1)} %get-tuple-element.57.held, f32[1,128,512]{2,1,0:T(8,128)S(1)} %get-tuple-element.35.refs_0_, ...), custom_call_target="tpu_custom_call" | custom-call | tf_op jit(solution)/shard_map/edges/pallas_call | solution.py:393
  45.4 0.1 collective-permute-start.14
  45.5 0.7 %collective-permute-start.15 = (f32[512,128]{1,0:T(8,128)S(1)}, f32[512,128]{1,0:T(8,128)S(1)}, u32[]{:S(2)}, u32[]{:S(2)}) collective-permute-start(f32[512,128]{1,0:T(8,128)S(1)} %get-tuple-element.64), channel_id=1, source_target_pairs={{4,8},{8,4},{12,16},{16,12},{20,24},{24,20},{5,9},{9,5},{13,17},{1... | collective-permute-start | bytes 786440 | tf_op jit(solution)/shard_map/ppermute | solution.py:515
  46.2 0.8 %collective-permute-done.14.near = f32[520,128]{1,0:T(8,128)S(1)} collective-permute-done((f32[520,128]{1,0:T(8,128)S(1)}, f32[520,128]{1,0:T(8,128)S(1)}, u32[]{:S(2)}, u32[]{:S(2)}) %collective-permute-start.14) | collective-permute-done | bytes 266272 | tf_op jit(solution)/shard_map/ppermute | solution.py:515
  47.1 3.4 %collective-permute-start.18 = (f32[8,128]{1,0:T(8,128)S(1)}, f32[8,128]{1,0:T(8,128)S(1)}, u32[]{:S(2)}, u32[]{:S(2)}) collective-permute-start(f32[8,128]{1,0:T(8,128)S(1)} %slice_add_fusion.refs_1_), channel_id=1, source_target_pairs={{0,24},{4,28},{8,16},{12,20},{16,8},{20,12},{24,0},{28,4},{1,25},{... | collective-permute-start | bytes 12296 | tf_op jit(solution)/shard_map/ppermute | solution.py:520
  50.5 0.6 %collective-permute-start.17 = (f32[8,128]{1,0:T(8,128)S(1)}, f32[8,128]{1,0:T(8,128)S(1)}, u32[]{:S(2)}, u32[]{:S(2)}) collective-permute-start(f32[8,128]{1,0:T(8,128)S(1)} %slice_add_fusion.refs_1_), channel_id=1, source_target_pairs={{0,16},{4,20},{8,24},{12,28},{16,0},{20,4},{24,8},{28,12},{1,17},{... | collective-permute-start | bytes 12296 | tf_op jit(solution)/shard_map/ppermute | solution.py:520
  51.1 0.9 %collective-permute-start.16 = (f32[8,128]{1,0:T(8,128)S(1)}, f32[8,128]{1,0:T(8,128)S(1)}, u32[]{:S(2)}, u32[]{:S(2)}) collective-permute-start(f32[8,128]{1,0:T(8,128)S(1)} %slice_add_fusion.refs_1_), channel_id=1, source_target_pairs={{0,8},{4,12},{8,0},{12,4},{16,24},{20,28},{24,16},{28,20},{1,9},{5... | collective-permute-start | bytes 12296 | tf_op jit(solution)/shard_map/ppermute | solution.py:520
  52.0 2.8 %place.1 = (f32[1024,512]{1,0:T(8,128)}, f32[1024,128]{1,0:T(8,128)S(1)}) custom-call(s32[5]{0:T(128)S(1)} %stack.19.where, f32[520,128]{1,0:T(8,128)S(1)} %collective-permute-done.14.near, f32[4,128,128]{2,1,0:T(8,128)S(1)} %get-tuple-element.57.held, f32[1,128,512]{2,1,0:T(8,128)S(1)} %get-tuple-element.35.refs_0_, ...), custom_call_target="tpu_custom_call" | custom-call | tf_op jit(solution)/shard_map/place/pallas_call | solution.py:445
  54.8 0.0 collective-permute-done.15.refs_0_
  54.8 0.0 collective-permute-done.18.refs_4_
  54.9 0.0 collective-permute-done.17.refs_3_
  54.9 1.8 %collective-permute-done.16.refs_2_ = f32[8,128]{1,0:T(8,128)S(1)} collective-permute-done((f32[8,128]{1,0:T(8,128)S(1)}, f32[8,128]{1,0:T(8,128)S(1)}, u32[]{:S(2)}, u32[]{:S(2)}) %collective-permute-start.16) | collective-permute-done | bytes 4128 | tf_op jit(solution)/shard_map/ppermute | solution.py:520
  56.7 1.5 %finish.1 = (f32[1024,512]{1,0:T(8,128)}, f32[1,1]{1,0:T(1,128)}) custom-call(s32[5]{0:T(128)S(1)} %stack.19.where, f32[1024,128]{1,0:T(8,128)S(1)} %get-tuple-element.63.mate, f32[512,128]{1,0:T(8,128)S(1)} %collective-permute-done.15.refs_0_, f32[8,128]{1,0:T(8,128)S(1)} %slice_add_fusion.refs_1_, ...), custom_call_target="tpu_custom_call", output_to_operand_aliasing={{0}: (7, {})} | custom-call | tf_op jit(solution)/shard_map/finish/pallas_call | solution.py:495
  (4 shorter events, 0.1 us)
Async XLA Ops:
  1.4 1.6 %copy-start = (f32[128,4096]{1,0:T(8,128)S(1)}, f32[128,4096]{1,0:T(8,128)}, u32[]{:S(2)}) copy-start(f32[128,4096]{1,0:T(8,128)} %source.1) | copy-start | bytes 6291460
  4.6 5.0 %collective-permute-start = (f32[1,128,512]{2,1,0:T(8,128)S(1)}, f32[1,128,512]{2,1,0:T(8,128)S(1)}, u32[]{:S(2)}, u32[]{:S(2)}) collective-permute-start(f32[1,128,512]{2,1,0:T(8,128)S(1)} %get-tuple-element.38), channel_id=1, source_target_pairs={{0,4},{4,0},{8,12},{12,8},{16,20},{20,16},{24,28},{28,24},{1,5},{5... | collective-permute-start | bytes 786440 | tf_op jit(solution)/shard_map/ppermute | solution.py:520
  5.1 4.5 %collective-permute-start.1 = (f32[1,128,512]{2,1,0:T(8,128)S(1)}, f32[1,128,512]{2,1,0:T(8,128)S(1)}, u32[]{:S(2)}, u32[]{:S(2)}) collective-permute-start(f32[1,128,512]{2,1,0:T(8,128)S(1)} %get-tuple-element.39), channel_id=1, source_target_pairs={{0,4},{4,0},{8,12},{12,8},{16,20},{20,16},{24,28},{28,24},{1,5},{5... | collective-permute-start | bytes 786440 | tf_op jit(solution)/shard_map/ppermute | solution.py:520
  5.2 4.4 %collective-permute-start.2 = (f32[1,128,512]{2,1,0:T(8,128)S(1)}, f32[1,128,512]{2,1,0:T(8,128)S(1)}, u32[]{:S(2)}, u32[]{:S(2)}) collective-permute-start(f32[1,128,512]{2,1,0:T(8,128)S(1)} %get-tuple-element.40), channel_id=1, source_target_pairs={{0,4},{4,0},{8,12},{12,8},{16,20},{20,16},{24,28},{28,24},{1,5},{5... | collective-permute-start | bytes 786440 | tf_op jit(solution)/shard_map/ppermute | solution.py:520
  5.6 4.0 %collective-permute-start.3 = (f32[1,128,512]{2,1,0:T(8,128)S(1)}, f32[1,128,512]{2,1,0:T(8,128)S(1)}, u32[]{:S(2)}, u32[]{:S(2)}) collective-permute-start(f32[1,128,512]{2,1,0:T(8,128)S(1)} %get-tuple-element.41), channel_id=1, source_target_pairs={{0,4},{4,0},{8,12},{12,8},{16,20},{20,16},{24,28},{28,24},{1,5},{5... | collective-permute-start | bytes 786440 | tf_op jit(solution)/shard_map/ppermute | solution.py:520
  5.7 9.2 %collective-permute-start.4 = (f32[1,128,384]{2,1,0:T(8,128)S(1)}, f32[1,128,384]{2,1,0:T(8,128)S(1)}, u32[]{:S(2)}, u32[]{:S(2)}) collective-permute-start(f32[1,128,384]{2,1,0:T(8,128)S(1)} %get-tuple-element.42.refs_7_), channel_id=1, source_target_pairs={{0,24},{4,28},{8,16},{12,20},{16,8},{20,12},{24,0},{28,4},{1,25},{... | collective-permute-start | bytes 589832 | tf_op jit(solution)/shard_map/ppermute | solution.py:520
  10.4 10.6 %collective-permute-start.6 = (f32[4,72,128]{2,1,0:T(8,128)S(1)}, f32[4,72,128]{2,1,0:T(8,128)S(1)}, u32[]{:S(2)}, u32[]{:S(2)}) collective-permute-start(f32[4,72,128]{2,1,0:T(8,128)S(1)} %get-tuple-element.49), channel_id=1, source_target_pairs={{0,16},{4,20},{8,24},{12,28},{16,0},{20,4},{24,8},{28,12},{1,17},{... | collective-permute-start | bytes 442376 | tf_op jit(solution)/shard_map/ppermute | solution.py:520
  11.2 9.8 %collective-permute-start.7 = (f32[4,72,128]{2,1,0:T(8,128)S(1)}, f32[4,72,128]{2,1,0:T(8,128)S(1)}, u32[]{:S(2)}, u32[]{:S(2)}) collective-permute-start(f32[4,72,128]{2,1,0:T(8,128)S(1)} %get-tuple-element.50), channel_id=1, source_target_pairs={{0,24},{4,28},{8,16},{12,20},{16,8},{20,12},{24,0},{28,4},{1,25},{... | collective-permute-start | bytes 442376 | tf_op jit(solution)/shard_map/ppermute | solution.py:520
  12.6 8.7 %collective-permute-start.5 = (f32[4,72,128]{2,1,0:T(8,128)S(1)}, f32[4,72,128]{2,1,0:T(8,128)S(1)}, u32[]{:S(2)}, u32[]{:S(2)}) collective-permute-start(f32[4,72,128]{2,1,0:T(8,128)S(1)} %get-tuple-element.45.after), channel_id=1, source_target_pairs={{0,8},{4,12},{8,0},{12,4},{16,24},{20,28},{24,16},{28,20},{1,9},{5... | collective-permute-start | bytes 442376 | tf_op jit(solution)/shard_map/ppermute | solution.py:520
  21.3 23.1 %collective-permute-start.11 = (f32[2,128,512]{2,1,0:T(8,128)}, f32[2,128,512]{2,1,0:T(8,128)S(1)}, u32[]{:S(2)}, u32[]{:S(2)}) collective-permute-start(f32[2,128,512]{2,1,0:T(8,128)} %get-tuple-element.59), channel_id=1, source_target_pairs={{0,8},{4,12},{8,0},{12,4},{16,24},{20,28},{24,16},{28,20},{1,9},{5... | collective-permute-start | bytes 1572872 | tf_op jit(solution)/shard_map/ppermute | solution.py:520
  22.8 21.6 %collective-permute-start.12 = (f32[2,128,512]{2,1,0:T(8,128)S(1)}, f32[2,128,512]{2,1,0:T(8,128)S(1)}, u32[]{:S(2)}, u32[]{:S(2)}) collective-permute-start(f32[2,128,512]{2,1,0:T(8,128)S(1)} %get-tuple-element.60), channel_id=1, source_target_pairs={{0,16},{4,20},{8,24},{12,28},{16,0},{20,4},{24,8},{28,12},{1,17},{... | collective-permute-start | bytes 1572872 | tf_op jit(solution)/shard_map/ppermute | solution.py:520
  24.2 20.1 %collective-permute-start.13 = (f32[5,128,128]{2,1,0:T(8,128)S(1)}, f32[5,128,128]{2,1,0:T(8,128)S(1)}, u32[]{:S(2)}, u32[]{:S(2)}) collective-permute-start(f32[5,128,128]{2,1,0:T(8,128)S(1)} %get-tuple-element.61), channel_id=1, source_target_pairs={{0,24},{4,28},{8,16},{12,20},{16,8},{20,12},{24,0},{28,4},{1,25},{... | collective-permute-start | bytes 983048 | tf_op jit(solution)/shard_map/ppermute | solution.py:520
  24.8 4.4 %collective-permute-start.8 = (f32[2,72,128]{2,1,0:T(8,128)S(1)}, f32[2,72,128]{2,1,0:T(8,128)S(1)}, u32[]{:S(2)}, u32[]{:S(2)}) collective-permute-start(f32[2,72,128]{2,1,0:T(8,128)S(1)} %get-tuple-element.55), channel_id=1, source_target_pairs={{0,1},{1,0},{2,3},{3,2},{4,5},{5,4},{6,7},{7,6},{8,9},{9,8},{10,11... | collective-permute-start | bytes 221192 | tf_op jit(solution)/shard_map/ppermute | solution.py:520
  29.3 5.3 %collective-permute-start.9 = (f32[2,72,128]{2,1,0:T(8,128)S(1)}, f32[2,72,128]{2,1,0:T(8,128)S(1)}, u32[]{:S(2)}, u32[]{:S(2)}) collective-permute-start(f32[2,72,128]{2,1,0:T(8,128)S(1)} %add.14), channel_id=1, source_target_pairs={{0,2},{1,3},{2,0},{3,1},{4,6},{5,7},{6,4},{7,5},{8,10},{9,11},{10,... | collective-permute-start | bytes 221192 | tf_op jit(solution)/shard_map/ppermute | solution.py:520
  34.6 4.4 %collective-permute-start.10 = (f32[2,72,128]{2,1,0:T(8,128)S(1)}, f32[2,72,128]{2,1,0:T(8,128)S(1)}, u32[]{:S(2)}, u32[]{:S(2)}) collective-permute-start(f32[2,72,128]{2,1,0:T(8,128)S(1)} %add.15.refs_0_), channel_id=1, source_target_pairs={{0,1},{1,0},{2,3},{3,2},{4,5},{5,4},{6,7},{7,6},{8,9},{9,8},{10,11... | collective-permute-start | bytes 221192 | tf_op jit(solution)/shard_map/ppermute | solution.py:520
  45.4 1.6 %collective-permute-start.14 = (f32[520,128]{1,0:T(8,128)S(1)}, f32[520,128]{1,0:T(8,128)S(1)}, u32[]{:S(2)}, u32[]{:S(2)}) collective-permute-start(f32[520,128]{1,0:T(8,128)S(1)} %get-tuple-element.62), channel_id=1, source_target_pairs={{0,4},{4,0},{8,12},{12,8},{16,20},{20,16},{24,28},{28,24},{1,5},{5... | collective-permute-start | bytes 798728 | tf_op jit(solution)/shard_map/ppermute | solution.py:515
  45.5 9.3 %collective-permute-start.15 = (f32[512,128]{1,0:T(8,128)S(1)}, f32[512,128]{1,0:T(8,128)S(1)}, u32[]{:S(2)}, u32[]{:S(2)}) collective-permute-start(f32[512,128]{1,0:T(8,128)S(1)} %get-tuple-element.64), channel_id=1, source_target_pairs={{4,8},{8,4},{12,16},{16,12},{20,24},{24,20},{5,9},{9,5},{13,17},{1... | collective-permute-start | bytes 786440 | tf_op jit(solution)/shard_map/ppermute | solution.py:515
  47.1 7.8 %collective-permute-start.18 = (f32[8,128]{1,0:T(8,128)S(1)}, f32[8,128]{1,0:T(8,128)S(1)}, u32[]{:S(2)}, u32[]{:S(2)}) collective-permute-start(f32[8,128]{1,0:T(8,128)S(1)} %slice_add_fusion.refs_1_), channel_id=1, source_target_pairs={{0,24},{4,28},{8,16},{12,20},{16,8},{20,12},{24,0},{28,4},{1,25},{... | collective-permute-start | bytes 12296 | tf_op jit(solution)/shard_map/ppermute | solution.py:520
  50.5 4.4 %collective-permute-start.17 = (f32[8,128]{1,0:T(8,128)S(1)}, f32[8,128]{1,0:T(8,128)S(1)}, u32[]{:S(2)}, u32[]{:S(2)}) collective-permute-start(f32[8,128]{1,0:T(8,128)S(1)} %slice_add_fusion.refs_1_), channel_id=1, source_target_pairs={{0,16},{4,20},{8,24},{12,28},{16,0},{20,4},{24,8},{28,12},{1,17},{... | collective-permute-start | bytes 12296 | tf_op jit(solution)/shard_map/ppermute | solution.py:520
  51.1 5.6 %collective-permute-start.16 = (f32[8,128]{1,0:T(8,128)S(1)}, f32[8,128]{1,0:T(8,128)S(1)}, u32[]{:S(2)}, u32[]{:S(2)}) collective-permute-start(f32[8,128]{1,0:T(8,128)S(1)} %slice_add_fusion.refs_1_), channel_id=1, source_target_pairs={{0,8},{4,12},{8,0},{12,4},{16,24},{20,28},{24,16},{28,20},{1,9},{5... | collective-permute-start | bytes 12296 | tf_op jit(solution)/shard_map/ppermute | solution.py:520

commit v8 on v7

--- a/solution.py
+++ b/solution.py
@@ -544,17 +544,20 @@
         own, *given = near_grams(plan, *here, *near, arranged[7], late)
         taken = [swapped(value, "pair", by) for by, value in zip((2, 4, 6), given)]
         single = tuple((4, pair) for pair in range(local)) + tuple((5, pair) for pair in range(local - ahead))
-        plan = ((local, ((0, 0), (2, 0))), (local, ((1, 0), (3, 0))), (1, single))
-        going = joined(given[0], plan, here[1], here[2], near[1], near[2], near[3], late)
+        cut = (len(single) + 1) // 2
+        plan = ((local, ((0, 0), (2, 0))), (local, ((1, 0), (3, 0))), (1, single[:cut]), (1, single[cut:]))
+        *going, six_first, six_last = joined(given[0], plan, here[1], here[2], near[1], near[2], near[3], late)
         early, going, taken = lax.optimization_barrier((early, going, taken))
         parts = merge(row, [own] + taken, shares)
-        from_far = [swapped(value, "pair", by) for by, value in zip((2, 4, 6), going)]
+        from_far = [swapped(value, "pair", by) for by, value in zip((2, 4), going)]
+        from_far += [swapped(value, "pair", 6) for value in (six_first, six_last)]
         columns = (here[0], near[0], early, *from_far)
+        six = [(5, index, 0) for index in range(cut)] + [(6, index, 0) for index in range(len(single) - cut)]
         tracks = []
         for pair in range(local):
             places = [(operand, place, pair) for operand, place in ((0, 0), (1, 0), (3, 0), (3, 1), (4, 0), (4, 1))]
-            places.append((2, 0, pair) if pair < ahead else (5, local + pair - ahead, 0))
-            tracks.append((1, (*places, (5, pair, 0))))
+            places.append((2, 0, pair) if pair < ahead else six[local + pair - ahead])
+            tracks.append((1, (*places, six[pair])))
         tracks = tuple(tracks)
         bases = (pair_index, pair_index - 1, pair_index + 1)
     else:

time: 58.3 us -> 57.7 us (0.990)
  Pallas kernels: 14 us -> 13.2 us
  local copies, waits for them, and re-layouts: 1.67 us -> 2.35 us
    pallas_call x1, Pallas kernels: 0.88 us -> 0.09 us  [joined(): pl.pallas_call(functools.partial(joined_kernel, tuple((places for _, plac...]
    unnamed x2 -> x4, local copies, waits for them, and re-layouts: 1.59 us -> 2.26 us
    ppermute x17 -> x18, waiting for transfers between devices: 16.5 us -> 16.1 us  [swapped(): return lax.ppermute(value, axis, [(i, i ^ by) for i in range(count)])]
    ppermute x17 -> x18, starting transfers between devices: 22.9 us -> 22.8 us  [swapped(): return lax.ppermute(value, axis, [(i, i ^ by) for i in range(count)])]
  transfers between devices with their start and end apart: 19 -> 20, of which waited for: 7 -> 9; matrix products, arithmetic and copies ran while one was open for 0% -> 0% of each run, Pallas kernels for 17% -> 16%
where the time goes in v8:
time: 57.7 us; the launch traced here: 57.6 us
  starting transfers between devices  23.5 us (41%)
  waiting for transfers between devices  17 us (29%)
  Pallas kernels  13.2 us (23%)
  local copies, waits for them, and re-layouts  2.35 us (4%)
  other arithmetic  0.76 us (1%)
  between operations  0.75 us (1%)
    ppermute x18, starting transfers between devices, swapped(): return lax.ppermute(value, axis, [(i, i ^ by) for i in range(count)])  22.8 us
    ppermute x18, waiting for transfers between devices, swapped(): return lax.ppermute(value, axis, [(i, i ^ by) for i in range(count)])  16.1 us
    pallas_call x1, Pallas kernels, solve(): pl.pallas_call(functools.partial(solve_kernel, len(parts)), out_shape=(ja...  5.29 us
    pallas_call x1, Pallas kernels, place(): pl.pallas_call(functools.partial(place_kernel, tracks), out_shape=(jax.Sh...  2.79 us
    unnamed x4, local copies, waits for them, and re-layouts  2.26 us
    pallas_call x1, Pallas kernels, gather(): pl.pallas_call(functools.partial(gather_kernel, tuple(((local, first, pos...  1.6 us
    pallas_call x1, Pallas kernels, finish(): pl.pallas_call(functools.partial(finish_kernel, blocks, len(far)), out_sh...  1.49 us
  transfers between devices with their start and end apart: 20, of which 9 were waited for; matrix products, arithmetic and copies ran while one was open for 0% of the time, Pallas kernels for 16%

profile of v8, /device:TPU:0, one launch (start us, length us, event | category | flops | bytes accessed | tf_op | source)
XLA Modules:
  0.0 57.6 jit_solution(12078944501595285175)
XLA Ops:
  0.6 0.7 %pad_add_fusion.slots = s32[65]{0:T(128)S(1)} fusion(s32[1]{0:T(128)} %bitcast, s32[64]{0:T(128)} %param.3), kind=kLoop, calls=%fused_computation.1 | loop fusion | flops 65 | bytes 520 | tf_op jit(solution)/shard_map/concatenate | solution.py:98
  1.4 0.0 copy-start
  1.4 1.6 %copy-done = f32[128,4096]{1,0:T(8,128)S(1)} copy-done((f32[128,4096]{1,0:T(8,128)S(1)}, f32[128,4096]{1,0:T(8,128)}, u32[]{:S(2)}) %copy-start) | copy-done | bytes 2097176
  3.0 1.6 %gather.1 = (f32[1,128,512]{2,1,0:T(8,128)S(1)}, f32[1,128,512]{2,1,0:T(8,128)S(1)}, f32[1,128,512]{2,1,0:T(8,128)S(1)}, f32[1,128,512]{2,1,0:T(8,128)S(1)}, f32...) custom-call(s32[65]{0:T(128)S(1)} %pad_add_fusion.slots, ...), custom_call_target="tpu_custom_call" | custom-call | tf_op jit(solution)/shard_map/gather/pallas_call | solution.py:91
  4.6 0.5 collective-permute-start
  5.1 0.1 collective-permute-start.1
  5.2 0.4 collective-permute-start.2
  5.6 0.1 collective-permute-start.3
  5.7 3.9 %collective-permute-start.4 = (f32[1,128,384]{2,1,0:T(8,128)S(1)}, f32[1,128,384]{2,1,0:T(8,128)S(1)}, u32[]{:S(2)}, u32[]{:S(2)}) collective-permute-start(f32[1,128,384]{2,1,0:T(8,128)S(1)} %get-tuple-element.42.refs_7_), channel_id=1, source_target_pairs={{0,24},{4,28},{8,16},{12,20},{16,8},{20,12},{24,0},{28,4},{1,25},{... | collective-permute-start | bytes 589832 | tf_op jit(solution)/shard_map/ppermute | solution.py:520
  9.5 0.0 collective-permute-done.refs_3_.refs_1_
  9.5 0.0 collective-permute-done.1.refs_4_.refs_2_
  9.5 0.0 collective-permute-done.2.refs_5_.refs_3_
  9.6 0.0 collective-permute-done.3.refs_6_.refs_4_
  9.6 0.9 %near_grams.1 = (f32[4,72,128]{2,1,0:T(8,128)S(1)}, f32[4,72,128]{2,1,0:T(8,128)S(1)}, f32[4,72,128]{2,1,0:T(8,128)S(1)}, f32[4,72,128]{2,1,0:T(8,128)S(1)}) custom-call(f32[1,128,512]{2,1,0:T(8,128)S(1)} %get-tuple-element.35.refs_0_, f32[1,128,512]{2,1,0:T(8,128)S(1)} %get-tuple-element.36.refs_1_.refs_0_, ...), custom_call_target="tpu_custom_call" | custom-call | tf_op jit(solution)/shard_map/near_grams/pallas_call | solution.py:176
  10.4 0.7 %collective-permute-start.6 = (f32[4,72,128]{2,1,0:T(8,128)S(1)}, f32[4,72,128]{2,1,0:T(8,128)S(1)}, u32[]{:S(2)}, u32[]{:S(2)}) collective-permute-start(f32[4,72,128]{2,1,0:T(8,128)S(1)} %get-tuple-element.48), channel_id=1, source_target_pairs={{0,16},{4,20},{8,24},{12,28},{16,0},{20,4},{24,8},{28,12},{1,17},{... | collective-permute-start | bytes 442376 | tf_op jit(solution)/shard_map/ppermute | solution.py:520
  11.2 1.4 %collective-permute-start.7 = (f32[4,72,128]{2,1,0:T(8,128)S(1)}, f32[4,72,128]{2,1,0:T(8,128)S(1)}, u32[]{:S(2)}, u32[]{:S(2)}) collective-permute-start(f32[4,72,128]{2,1,0:T(8,128)S(1)} %get-tuple-element.49), channel_id=1, source_target_pairs={{0,24},{4,28},{8,16},{12,20},{16,8},{20,12},{24,0},{28,4},{1,25},{... | collective-permute-start | bytes 442376 | tf_op jit(solution)/shard_map/ppermute | solution.py:520
  12.6 1.4 %collective-permute-start.5 = (f32[4,72,128]{2,1,0:T(8,128)S(1)}, f32[4,72,128]{2,1,0:T(8,128)S(1)}, u32[]{:S(2)}, u32[]{:S(2)}) collective-permute-start(f32[4,72,128]{2,1,0:T(8,128)S(1)} %get-tuple-element.45.after), channel_id=1, source_target_pairs={{0,8},{4,12},{8,0},{12,4},{16,24},{20,28},{24,16},{28,20},{1,9},{5... | collective-permute-start | bytes 442376 | tf_op jit(solution)/shard_map/ppermute | solution.py:520
  14.0 0.1 joined.1
  14.1 0.0 copy-start.1
  14.1 0.7 %copy-done.1 = f32[3,128,128]{2,1,0:T(8,128)} copy-done((f32[3,128,128]{2,1,0:T(8,128)}, f32[3,128,128]{2,1,0:T(8,128)S(1)}, u32[]{:S(2)}) %copy-start.1) | copy-done | bytes 196632
  14.8 0.1 collective-permute-done.4.refs_2_
  14.9 6.1 %collective-permute-done.6.refs_2_ = f32[4,72,128]{2,1,0:T(8,128)S(1)} collective-permute-done((f32[4,72,128]{2,1,0:T(8,128)S(1)}, f32[4,72,128]{2,1,0:T(8,128)S(1)}, u32[]{:S(2)}, u32[]{:S(2)}) %collective-permute-start.6) | collective-permute-done | bytes 147488 | tf_op jit(solution)/shard_map/ppermute | solution.py:520
  21.0 0.0 collective-permute-done.7.refs_3_
  21.0 0.3 collective-permute-done.5.refs_1_
  21.3 1.5 %collective-permute-start.11 = (f32[2,128,512]{2,1,0:T(8,128)S(1)}, f32[2,128,512]{2,1,0:T(8,128)S(1)}, u32[]{:S(2)}, u32[]{:S(2)}) collective-permute-start(f32[2,128,512]{2,1,0:T(8,128)S(1)} %get-tuple-element.58), channel_id=1, source_target_pairs={{0,8},{4,12},{8,0},{12,4},{16,24},{20,28},{24,16},{28,20},{1,9},{5... | collective-permute-start | bytes 1572872 | tf_op jit(solution)/shard_map/ppermute | solution.py:520
  22.8 1.4 %collective-permute-start.12 = (f32[2,128,512]{2,1,0:T(8,128)S(1)}, f32[2,128,512]{2,1,0:T(8,128)S(1)}, u32[]{:S(2)}, u32[]{:S(2)}) collective-permute-start(f32[2,128,512]{2,1,0:T(8,128)S(1)} %get-tuple-element.59), channel_id=1, source_target_pairs={{0,16},{4,20},{8,24},{12,28},{16,0},{20,4},{24,8},{28,12},{1,17},{... | collective-permute-start | bytes 1572872 | tf_op jit(solution)/shard_map/ppermute | solution.py:520
  24.3 1.6 %collective-permute-start.8 = (f32[2,72,128]{2,1,0:T(8,128)S(1)}, f32[2,72,128]{2,1,0:T(8,128)S(1)}, u32[]{:S(2)}, u32[]{:S(2)}) collective-permute-start(f32[2,72,128]{2,1,0:T(8,128)S(1)} %get-tuple-element.54), channel_id=1, source_target_pairs={{0,1},{1,0},{2,3},{3,2},{4,5},{5,4},{6,7},{7,6},{8,9},{9,8},{10,11... | collective-permute-start | bytes 221192 | tf_op jit(solution)/shard_map/ppermute | solution.py:520
  25.9 0.6 collective-permute-start.13
  26.5 2.2 %collective-permute-done.8 = f32[2,72,128]{2,1,0:T(8,128)S(1)} collective-permute-done((f32[2,72,128]{2,1,0:T(8,128)S(1)}, f32[2,72,128]{2,1,0:T(8,128)S(1)}, u32[]{:S(2)}, u32[]{:S(2)}) %collective-permute-start.8) | collective-permute-done | bytes 73760 | tf_op jit(solution)/shard_map/ppermute | solution.py:520
  28.7 2.7 %collective-permute-start.9 = (f32[2,72,128]{2,1,0:T(8,128)S(1)}, f32[2,72,128]{2,1,0:T(8,128)S(1)}, u32[]{:S(2)}, u32[]{:S(2)}) collective-permute-start(f32[2,72,128]{2,1,0:T(8,128)S(1)} %add.14), channel_id=1, source_target_pairs={{0,2},{1,3},{2,0},{3,1},{4,6},{5,7},{6,4},{7,5},{8,10},{9,11},{10,... | collective-permute-start | bytes 221192 | tf_op jit(solution)/shard_map/ppermute | solution.py:520
  31.4 0.6 collective-permute-start.14
  31.9 2.1 %collective-permute-done.9 = f32[2,72,128]{2,1,0:T(8,128)S(1)} collective-permute-done((f32[2,72,128]{2,1,0:T(8,128)S(1)}, f32[2,72,128]{2,1,0:T(8,128)S(1)}, u32[]{:S(2)}, u32[]{:S(2)}) %collective-permute-start.9) | collective-permute-done | bytes 73760 | tf_op jit(solution)/shard_map/ppermute | solution.py:520
  34.0 1.6 %collective-permute-start.10 = (f32[2,72,128]{2,1,0:T(8,128)S(1)}, f32[2,72,128]{2,1,0:T(8,128)S(1)}, u32[]{:S(2)}, u32[]{:S(2)}) collective-permute-start(f32[2,72,128]{2,1,0:T(8,128)S(1)} %add.15.refs_0_), channel_id=1, source_target_pairs={{0,1},{1,0},{2,3},{3,2},{4,5},{5,4},{6,7},{7,6},{8,9},{9,8},{10,11... | collective-permute-start | bytes 221192 | tf_op jit(solution)/shard_map/ppermute | solution.py:520
  35.7 0.1 stack.19.where
  35.8 2.7 %collective-permute-done.10.refs_1_ = f32[2,72,128]{2,1,0:T(8,128)S(1)} collective-permute-done((f32[2,72,128]{2,1,0:T(8,128)S(1)}, f32[2,72,128]{2,1,0:T(8,128)S(1)}, u32[]{:S(2)}, u32[]{:S(2)}) %collective-permute-start.10) | collective-permute-done | bytes 73760 | tf_op jit(solution)/shard_map/ppermute | solution.py:520
  38.4 5.3 %solve.1 = (f32[4,128,128]{2,1,0:T(8,128)S(1)}, f32[8,128]{1,0:T(8,128)S(1)}) custom-call(s32[1]{0:T(128)} %bitcast.4.row, f32[2,72,128]{2,1,0:T(8,128)S(1)} %add.15.refs_0_, f32[2,72,128]{2,1,0:T(8,128)S(1)} %collective-permute-done.10.refs_1_), custom_call_target="tpu_custom_call" | custom-call | tf_op jit(solution)/shard_map/solve/pallas_call | solution.py:340
  43.7 0.0 collective-permute-done.14.refs_6_
  43.8 0.0 collective-permute-done.13.refs_5_
  43.8 0.0 collective-permute-done.11.refs_3_
  43.8 0.0 collective-permute-done.12.refs_4_
  43.8 1.1 %edges.1 = (f32[520,128]{1,0:T(8,128)S(1)}, f32[512,128]{1,0:T(8,128)S(1)}) custom-call(s32[5]{0:T(128)S(1)} %stack.19.where, f32[8,128]{1,0:T(8,128)S(1)} %get-tuple-element.55.sums, f32[4,128,128]{2,1,0:T(8,128)S(1)} %get-tuple-element.56.held, f32[1,128,512]{2,1,0:T(8,128)S(1)} %get-tuple-element.35.refs_0_, ...), custom_call_target="tpu_custom_call" | custom-call | tf_op jit(solution)/shard_map/edges/pallas_call | solution.py:393
  44.9 0.1 collective-permute-start.15
  44.9 0.7 %collective-permute-start.16 = (f32[512,128]{1,0:T(8,128)S(1)}, f32[512,128]{1,0:T(8,128)S(1)}, u32[]{:S(2)}, u32[]{:S(2)}) collective-permute-start(f32[512,128]{1,0:T(8,128)S(1)} %get-tuple-element.64), channel_id=1, source_target_pairs={{4,8},{8,4},{12,16},{16,12},{20,24},{24,20},{5,9},{9,5},{13,17},{1... | collective-permute-start | bytes 786440 | tf_op jit(solution)/shard_map/ppermute | solution.py:515
  45.6 0.8 %collective-permute-done.15.near = f32[520,128]{1,0:T(8,128)S(1)} collective-permute-done((f32[520,128]{1,0:T(8,128)S(1)}, f32[520,128]{1,0:T(8,128)S(1)}, u32[]{:S(2)}, u32[]{:S(2)}) %collective-permute-start.15) | collective-permute-done | bytes 266272 | tf_op jit(solution)/shard_map/ppermute | solution.py:515
  46.5 3.1 %collective-permute-start.19 = (f32[8,128]{1,0:T(8,128)S(1)}, f32[8,128]{1,0:T(8,128)S(1)}, u32[]{:S(2)}, u32[]{:S(2)}) collective-permute-start(f32[8,128]{1,0:T(8,128)S(1)} %slice_add_fusion.refs_1_), channel_id=1, source_target_pairs={{0,24},{4,28},{8,16},{12,20},{16,8},{20,12},{24,0},{28,4},{1,25},{... | collective-permute-start | bytes 12296 | tf_op jit(solution)/shard_map/ppermute | solution.py:520
  49.5 1.0 %collective-permute-start.18 = (f32[8,128]{1,0:T(8,128)S(1)}, f32[8,128]{1,0:T(8,128)S(1)}, u32[]{:S(2)}, u32[]{:S(2)}) collective-permute-start(f32[8,128]{1,0:T(8,128)S(1)} %slice_add_fusion.refs_1_), channel_id=1, source_target_pairs={{0,16},{4,20},{8,24},{12,28},{16,0},{20,4},{24,8},{28,12},{1,17},{... | collective-permute-start | bytes 12296 | tf_op jit(solution)/shard_map/ppermute | solution.py:520
  50.5 0.2 collective-permute-start.17
  50.7 2.8 %place.1 = (f32[1024,512]{1,0:T(8,128)}, f32[1024,128]{1,0:T(8,128)S(1)}) custom-call(s32[5]{0:T(128)S(1)} %stack.19.where, f32[520,128]{1,0:T(8,128)S(1)} %collective-permute-done.15.near, f32[4,128,128]{2,1,0:T(8,128)S(1)} %get-tuple-element.56.held, f32[1,128,512]{2,1,0:T(8,128)S(1)} %get-tuple-element.35.refs_0_, ...), custom_call_target="tpu_custom_call" | custom-call | tf_op jit(solution)/shard_map/place/pallas_call | solution.py:445
  53.5 0.0 collective-permute-done.16.refs_0_
  53.5 0.4 collective-permute-done.19.refs_4_
  53.9 0.0 collective-permute-done.18.refs_3_
  53.9 2.2 %collective-permute-done.17.refs_2_ = f32[8,128]{1,0:T(8,128)S(1)} collective-permute-done((f32[8,128]{1,0:T(8,128)S(1)}, f32[8,128]{1,0:T(8,128)S(1)}, u32[]{:S(2)}, u32[]{:S(2)}) %collective-permute-start.17) | collective-permute-done | bytes 4128 | tf_op jit(solution)/shard_map/ppermute | solution.py:520
  56.1 1.5 %finish.1 = (f32[1024,512]{1,0:T(8,128)}, f32[1,1]{1,0:T(1,128)}) custom-call(s32[5]{0:T(128)S(1)} %stack.19.where, f32[1024,128]{1,0:T(8,128)S(1)} %get-tuple-element.63.mate, f32[512,128]{1,0:T(8,128)S(1)} %collective-permute-done.16.refs_0_, f32[8,128]{1,0:T(8,128)S(1)} %slice_add_fusion.refs_1_, ...), custom_call_target="tpu_custom_call", output_to_operand_aliasing={{0}: (7, {})} | custom-call | tf_op jit(solution)/shard_map/finish/pallas_call | solution.py:495
  (4 shorter events, 0.1 us)
Async XLA Ops:
  1.4 1.6 %copy-start = (f32[128,4096]{1,0:T(8,128)S(1)}, f32[128,4096]{1,0:T(8,128)}, u32[]{:S(2)}) copy-start(f32[128,4096]{1,0:T(8,128)} %source.1) | copy-start | bytes 6291460
  4.6 5.0 %collective-permute-start = (f32[1,128,512]{2,1,0:T(8,128)S(1)}, f32[1,128,512]{2,1,0:T(8,128)S(1)}, u32[]{:S(2)}, u32[]{:S(2)}) collective-permute-start(f32[1,128,512]{2,1,0:T(8,128)S(1)} %get-tuple-element.38), channel_id=1, source_target_pairs={{0,4},{4,0},{8,12},{12,8},{16,20},{20,16},{24,28},{28,24},{1,5},{5... | collective-permute-start | bytes 786440 | tf_op jit(solution)/shard_map/ppermute | solution.py:520
  5.1 4.5 %collective-permute-start.1 = (f32[1,128,512]{2,1,0:T(8,128)S(1)}, f32[1,128,512]{2,1,0:T(8,128)S(1)}, u32[]{:S(2)}, u32[]{:S(2)}) collective-permute-start(f32[1,128,512]{2,1,0:T(8,128)S(1)} %get-tuple-element.39), channel_id=1, source_target_pairs={{0,4},{4,0},{8,12},{12,8},{16,20},{20,16},{24,28},{28,24},{1,5},{5... | collective-permute-start | bytes 786440 | tf_op jit(solution)/shard_map/ppermute | solution.py:520
  5.2 4.4 %collective-permute-start.2 = (f32[1,128,512]{2,1,0:T(8,128)S(1)}, f32[1,128,512]{2,1,0:T(8,128)S(1)}, u32[]{:S(2)}, u32[]{:S(2)}) collective-permute-start(f32[1,128,512]{2,1,0:T(8,128)S(1)} %get-tuple-element.40), channel_id=1, source_target_pairs={{0,4},{4,0},{8,12},{12,8},{16,20},{20,16},{24,28},{28,24},{1,5},{5... | collective-permute-start | bytes 786440 | tf_op jit(solution)/shard_map/ppermute | solution.py:520
  5.6 4.0 %collective-permute-start.3 = (f32[1,128,512]{2,1,0:T(8,128)S(1)}, f32[1,128,512]{2,1,0:T(8,128)S(1)}, u32[]{:S(2)}, u32[]{:S(2)}) collective-permute-start(f32[1,128,512]{2,1,0:T(8,128)S(1)} %get-tuple-element.41), channel_id=1, source_target_pairs={{0,4},{4,0},{8,12},{12,8},{16,20},{20,16},{24,28},{28,24},{1,5},{5... | collective-permute-start | bytes 786440 | tf_op jit(solution)/shard_map/ppermute | solution.py:520
  5.7 9.2 %collective-permute-start.4 = (f32[1,128,384]{2,1,0:T(8,128)S(1)}, f32[1,128,384]{2,1,0:T(8,128)S(1)}, u32[]{:S(2)}, u32[]{:S(2)}) collective-permute-start(f32[1,128,384]{2,1,0:T(8,128)S(1)} %get-tuple-element.42.refs_7_), channel_id=1, source_target_pairs={{0,24},{4,28},{8,16},{12,20},{16,8},{20,12},{24,0},{28,4},{1,25},{... | collective-permute-start | bytes 589832 | tf_op jit(solution)/shard_map/ppermute | solution.py:520
  10.4 10.6 %collective-permute-start.6 = (f32[4,72,128]{2,1,0:T(8,128)S(1)}, f32[4,72,128]{2,1,0:T(8,128)S(1)}, u32[]{:S(2)}, u32[]{:S(2)}) collective-permute-start(f32[4,72,128]{2,1,0:T(8,128)S(1)} %get-tuple-element.48), channel_id=1, source_target_pairs={{0,16},{4,20},{8,24},{12,28},{16,0},{20,4},{24,8},{28,12},{1,17},{... | collective-permute-start | bytes 442376 | tf_op jit(solution)/shard_map/ppermute | solution.py:520
  11.2 9.8 %collective-permute-start.7 = (f32[4,72,128]{2,1,0:T(8,128)S(1)}, f32[4,72,128]{2,1,0:T(8,128)S(1)}, u32[]{:S(2)}, u32[]{:S(2)}) collective-permute-start(f32[4,72,128]{2,1,0:T(8,128)S(1)} %get-tuple-element.49), channel_id=1, source_target_pairs={{0,24},{4,28},{8,16},{12,20},{16,8},{20,12},{24,0},{28,4},{1,25},{... | collective-permute-start | bytes 442376 | tf_op jit(solution)/shard_map/ppermute | solution.py:520
  12.6 8.7 %collective-permute-start.5 = (f32[4,72,128]{2,1,0:T(8,128)S(1)}, f32[4,72,128]{2,1,0:T(8,128)S(1)}, u32[]{:S(2)}, u32[]{:S(2)}) collective-permute-start(f32[4,72,128]{2,1,0:T(8,128)S(1)} %get-tuple-element.45.after), channel_id=1, source_target_pairs={{0,8},{4,12},{8,0},{12,4},{16,24},{20,28},{24,16},{28,20},{1,9},{5... | collective-permute-start | bytes 442376 | tf_op jit(solution)/shard_map/ppermute | solution.py:520
  14.1 0.7 %copy-start.1 = (f32[3,128,128]{2,1,0:T(8,128)}, f32[3,128,128]{2,1,0:T(8,128)S(1)}, u32[]{:S(2)}) copy-start(f32[3,128,128]{2,1,0:T(8,128)S(1)} %get-tuple-element.60) | copy-start | bytes 589828
  21.3 22.5 %collective-permute-start.11 = (f32[2,128,512]{2,1,0:T(8,128)S(1)}, f32[2,128,512]{2,1,0:T(8,128)S(1)}, u32[]{:S(2)}, u32[]{:S(2)}) collective-permute-start(f32[2,128,512]{2,1,0:T(8,128)S(1)} %get-tuple-element.58), channel_id=1, source_target_pairs={{0,8},{4,12},{8,0},{12,4},{16,24},{20,28},{24,16},{28,20},{1,9},{5... | collective-permute-start | bytes 1572872 | tf_op jit(solution)/shard_map/ppermute | solution.py:520
  22.8 21.0 %collective-permute-start.12 = (f32[2,128,512]{2,1,0:T(8,128)S(1)}, f32[2,128,512]{2,1,0:T(8,128)S(1)}, u32[]{:S(2)}, u32[]{:S(2)}) collective-permute-start(f32[2,128,512]{2,1,0:T(8,128)S(1)} %get-tuple-element.59), channel_id=1, source_target_pairs={{0,16},{4,20},{8,24},{12,28},{16,0},{20,4},{24,8},{28,12},{1,17},{... | collective-permute-start | bytes 1572872 | tf_op jit(solution)/shard_map/ppermute | solution.py:520
  24.3 4.4 %collective-permute-start.8 = (f32[2,72,128]{2,1,0:T(8,128)S(1)}, f32[2,72,128]{2,1,0:T(8,128)S(1)}, u32[]{:S(2)}, u32[]{:S(2)}) collective-permute-start(f32[2,72,128]{2,1,0:T(8,128)S(1)} %get-tuple-element.54), channel_id=1, source_target_pairs={{0,1},{1,0},{2,3},{3,2},{4,5},{5,4},{6,7},{7,6},{8,9},{9,8},{10,11... | collective-permute-start | bytes 221192 | tf_op jit(solution)/shard_map/ppermute | solution.py:520
  25.9 17.8 %collective-permute-start.13 = (f32[3,128,128]{2,1,0:T(8,128)}, f32[3,128,128]{2,1,0:T(8,128)S(1)}, u32[]{:S(2)}, u32[]{:S(2)}) collective-permute-start(f32[3,128,128]{2,1,0:T(8,128)} %copy-done.1), channel_id=1, source_target_pairs={{0,24},{4,28},{8,16},{12,20},{16,8},{20,12},{24,0},{28,4},{1,25},{... | collective-permute-start | bytes 589832 | tf_op jit(solution)/shard_map/ppermute | solution.py:520
  28.7 5.3 %collective-permute-start.9 = (f32[2,72,128]{2,1,0:T(8,128)S(1)}, f32[2,72,128]{2,1,0:T(8,128)S(1)}, u32[]{:S(2)}, u32[]{:S(2)}) collective-permute-start(f32[2,72,128]{2,1,0:T(8,128)S(1)} %add.14), channel_id=1, source_target_pairs={{0,2},{1,3},{2,0},{3,1},{4,6},{5,7},{6,4},{7,5},{8,10},{9,11},{10,... | collective-permute-start | bytes 221192 | tf_op jit(solution)/shard_map/ppermute | solution.py:520
  31.4 12.4 %collective-permute-start.14 = (f32[2,128,128]{2,1,0:T(8,128)S(1)}, f32[2,128,128]{2,1,0:T(8,128)S(1)}, u32[]{:S(2)}, u32[]{:S(2)}) collective-permute-start(f32[2,128,128]{2,1,0:T(8,128)S(1)} %get-tuple-element.61), channel_id=1, source_target_pairs={{0,24},{4,28},{8,16},{12,20},{16,8},{20,12},{24,0},{28,4},{1,25},{... | collective-permute-start | bytes 393224 | tf_op jit(solution)/shard_map/ppermute | solution.py:520
  34.0 4.4 %collective-permute-start.10 = (f32[2,72,128]{2,1,0:T(8,128)S(1)}, f32[2,72,128]{2,1,0:T(8,128)S(1)}, u32[]{:S(2)}, u32[]{:S(2)}) collective-permute-start(f32[2,72,128]{2,1,0:T(8,128)S(1)} %add.15.refs_0_), channel_id=1, source_target_pairs={{0,1},{1,0},{2,3},{3,2},{4,5},{5,4},{6,7},{7,6},{8,9},{9,8},{10,11... | collective-permute-start | bytes 221192 | tf_op jit(solution)/shard_map/ppermute | solution.py:520
  44.9 1.6 %collective-permute-start.15 = (f32[520,128]{1,0:T(8,128)S(1)}, f32[520,128]{1,0:T(8,128)S(1)}, u32[]{:S(2)}, u32[]{:S(2)}) collective-permute-start(f32[520,128]{1,0:T(8,128)S(1)} %get-tuple-element.62), channel_id=1, source_target_pairs={{0,4},{4,0},{8,12},{12,8},{16,20},{20,16},{24,28},{28,24},{1,5},{5... | collective-permute-start | bytes 798728 | tf_op jit(solution)/shard_map/ppermute | solution.py:515
  44.9 8.6 %collective-permute-start.16 = (f32[512,128]{1,0:T(8,128)S(1)}, f32[512,128]{1,0:T(8,128)S(1)}, u32[]{:S(2)}, u32[]{:S(2)}) collective-permute-start(f32[512,128]{1,0:T(8,128)S(1)} %get-tuple-element.64), channel_id=1, source_target_pairs={{4,8},{8,4},{12,16},{16,12},{20,24},{24,20},{5,9},{9,5},{13,17},{1... | collective-permute-start | bytes 786440 | tf_op jit(solution)/shard_map/ppermute | solution.py:515
  46.5 7.4 %collective-permute-start.19 = (f32[8,128]{1,0:T(8,128)S(1)}, f32[8,128]{1,0:T(8,128)S(1)}, u32[]{:S(2)}, u32[]{:S(2)}) collective-permute-start(f32[8,128]{1,0:T(8,128)S(1)} %slice_add_fusion.refs_1_), channel_id=1, source_target_pairs={{0,24},{4,28},{8,16},{12,20},{16,8},{20,12},{24,0},{28,4},{1,25},{... | collective-permute-start | bytes 12296 | tf_op jit(solution)/shard_map/ppermute | solution.py:520
  49.5 4.4 %collective-permute-start.18 = (f32[8,128]{1,0:T(8,128)S(1)}, f32[8,128]{1,0:T(8,128)S(1)}, u32[]{:S(2)}, u32[]{:S(2)}) collective-permute-start(f32[8,128]{1,0:T(8,128)S(1)} %slice_add_fusion.refs_1_), channel_id=1, source_target_pairs={{0,16},{4,20},{8,24},{12,28},{16,0},{20,4},{24,8},{28,12},{1,17},{... | collective-permute-start | bytes 12296 | tf_op jit(solution)/shard_map/ppermute | solution.py:520
  50.5 5.6 %collective-permute-start.17 = (f32[8,128]{1,0:T(8,128)S(1)}, f32[8,128]{1,0:T(8,128)S(1)}, u32[]{:S(2)}, u32[]{:S(2)}) collective-permute-start(f32[8,128]{1,0:T(8,128)S(1)} %slice_add_fusion.refs_1_), channel_id=1, source_target_pairs={{0,8},{4,12},{8,0},{12,4},{16,24},{20,28},{24,16},{28,20},{1,9},{5... | collective-permute-start | bytes 12296 | tf_op jit(solution)/shard_map/ppermute | solution.py:520

commit v9 on v8

--- a/solution.py
+++ b/solution.py
@@ -583,7 +583,7 @@
     rotated, mate = place(tracks, where, columns, near, turns)
     if pair_count == 8:
         sums = sums + near[-LAST_ROWS:]
-        sums = [sums] + [swapped(sums, "pair", by) for by in (2, 4, 6)]
+        sums = [sums] + [swapped(sums, "pair", by) for by in (6, 4, 2)]
     else:
         sums = [lax.psum(sums, "pair")]
     rotated, off_ratio = finish(pair_count, where, far, mate, sums, rotated)

time: 57.7 us -> 57.7 us (level)
  transfers between devices with their start and end apart: 20 -> 20, of which waited for: 9 -> 8; matrix products, arithmetic and copies ran while one was open for 0% -> 0% of each run, Pallas kernels for 16% -> 16%
where the time goes in v9:
time: 57.7 us; the launch traced here: 57.5 us
  starting transfers between devices  23.5 us (41%)
  waiting for transfers between devices  16.9 us (29%)
  Pallas kernels  13.2 us (23%)
  local copies, waits for them, and re-layouts  2.35 us (4%)
  other arithmetic  0.76 us (1%)
  between operations  0.75 us (1%)
    ppermute x18, starting transfers between devices, swapped(): return lax.ppermute(value, axis, [(i, i ^ by) for i in range(count)])  22.8 us
    ppermute x18, waiting for transfers between devices, swapped(): return lax.ppermute(value, axis, [(i, i ^ by) for i in range(count)])  16.1 us
    pallas_call x1, Pallas kernels, solve(): pl.pallas_call(functools.partial(solve_kernel, len(parts)), out_shape=(ja...  5.29 us
    pallas_call x1, Pallas kernels, place(): pl.pallas_call(functools.partial(place_kernel, tracks), out_shape=(jax.Sh...  2.79 us
    unnamed x4, local copies, waits for them, and re-layouts  2.26 us
    pallas_call x1, Pallas kernels, gather(): pl.pallas_call(functools.partial(gather_kernel, tuple(((local, first, pos...  1.6 us
    pallas_call x1, Pallas kernels, finish(): pl.pallas_call(functools.partial(finish_kernel, blocks, len(far)), out_sh...  1.49 us
  transfers between devices with their start and end apart: 20, of which 8 were waited for; matrix products, arithmetic and copies ran while one was open for 0% of the time, Pallas kernels for 16%

profile of v9, /device:TPU:0, one launch (start us, length us, event | category | flops | bytes accessed | tf_op | source)
XLA Modules:
  0.0 57.5 jit_solution(2585607959828403939)
XLA Ops:
  0.6 0.7 %pad_add_fusion.slots = s32[65]{0:T(128)S(1)} fusion(s32[1]{0:T(128)} %bitcast, s32[64]{0:T(128)} %param.3), kind=kLoop, calls=%fused_computation.1 | loop fusion | flops 65 | bytes 520 | tf_op jit(solution)/shard_map/concatenate | solution.py:98
  1.4 0.0 copy-start
  1.4 1.6 %copy-done = f32[128,4096]{1,0:T(8,128)S(1)} copy-done((f32[128,4096]{1,0:T(8,128)S(1)}, f32[128,4096]{1,0:T(8,128)}, u32[]{:S(2)}) %copy-start) | copy-done | bytes 2097176
  3.0 1.6 %gather.1 = (f32[1,128,512]{2,1,0:T(8,128)S(1)}, f32[1,128,512]{2,1,0:T(8,128)S(1)}, f32[1,128,512]{2,1,0:T(8,128)S(1)}, f32[1,128,512]{2,1,0:T(8,128)S(1)}, f32...) custom-call(s32[65]{0:T(128)S(1)} %pad_add_fusion.slots, ...), custom_call_target="tpu_custom_call" | custom-call | tf_op jit(solution)/shard_map/gather/pallas_call | solution.py:91
  4.6 0.5 collective-permute-start
  5.1 0.1 collective-permute-start.1
  5.2 0.4 collective-permute-start.2
  5.6 0.1 collective-permute-start.3
  5.7 3.9 %collective-permute-start.4 = (f32[1,128,384]{2,1,0:T(8,128)S(1)}, f32[1,128,384]{2,1,0:T(8,128)S(1)}, u32[]{:S(2)}, u32[]{:S(2)}) collective-permute-start(f32[1,128,384]{2,1,0:T(8,128)S(1)} %get-tuple-element.42.refs_7_), channel_id=1, source_target_pairs={{0,24},{4,28},{8,16},{12,20},{16,8},{20,12},{24,0},{28,4},{1,25},{... | collective-permute-start | bytes 589832 | tf_op jit(solution)/shard_map/ppermute | solution.py:520
  9.5 0.0 collective-permute-done.refs_3_.refs_1_
  9.5 0.0 collective-permute-done.1.refs_4_.refs_2_
  9.5 0.0 collective-permute-done.2.refs_5_.refs_3_
  9.6 0.0 collective-permute-done.3.refs_6_.refs_4_
  9.6 0.9 %near_grams.1 = (f32[4,72,128]{2,1,0:T(8,128)S(1)}, f32[4,72,128]{2,1,0:T(8,128)S(1)}, f32[4,72,128]{2,1,0:T(8,128)S(1)}, f32[4,72,128]{2,1,0:T(8,128)S(1)}) custom-call(f32[1,128,512]{2,1,0:T(8,128)S(1)} %get-tuple-element.35.refs_0_, f32[1,128,512]{2,1,0:T(8,128)S(1)} %get-tuple-element.36.refs_1_.refs_0_, ...), custom_call_target="tpu_custom_call" | custom-call | tf_op jit(solution)/shard_map/near_grams/pallas_call | solution.py:176
  10.4 0.7 %collective-permute-start.6 = (f32[4,72,128]{2,1,0:T(8,128)S(1)}, f32[4,72,128]{2,1,0:T(8,128)S(1)}, u32[]{:S(2)}, u32[]{:S(2)}) collective-permute-start(f32[4,72,128]{2,1,0:T(8,128)S(1)} %get-tuple-element.48), channel_id=1, source_target_pairs={{0,16},{4,20},{8,24},{12,28},{16,0},{20,4},{24,8},{28,12},{1,17},{... | collective-permute-start | bytes 442376 | tf_op jit(solution)/shard_map/ppermute | solution.py:520
  11.2 1.4 %collective-permute-start.7 = (f32[4,72,128]{2,1,0:T(8,128)S(1)}, f32[4,72,128]{2,1,0:T(8,128)S(1)}, u32[]{:S(2)}, u32[]{:S(2)}) collective-permute-start(f32[4,72,128]{2,1,0:T(8,128)S(1)} %get-tuple-element.49), channel_id=1, source_target_pairs={{0,24},{4,28},{8,16},{12,20},{16,8},{20,12},{24,0},{28,4},{1,25},{... | collective-permute-start | bytes 442376 | tf_op jit(solution)/shard_map/ppermute | solution.py:520
  12.6 1.4 %collective-permute-start.5 = (f32[4,72,128]{2,1,0:T(8,128)S(1)}, f32[4,72,128]{2,1,0:T(8,128)S(1)}, u32[]{:S(2)}, u32[]{:S(2)}) collective-permute-start(f32[4,72,128]{2,1,0:T(8,128)S(1)} %get-tuple-element.45.after), channel_id=1, source_target_pairs={{0,8},{4,12},{8,0},{12,4},{16,24},{20,28},{24,16},{28,20},{1,9},{5... | collective-permute-start | bytes 442376 | tf_op jit(solution)/shard_map/ppermute | solution.py:520
  14.0 0.1 joined.1
  14.1 0.0 copy-start.1
  14.1 0.7 %copy-done.1 = f32[3,128,128]{2,1,0:T(8,128)} copy-done((f32[3,128,128]{2,1,0:T(8,128)}, f32[3,128,128]{2,1,0:T(8,128)S(1)}, u32[]{:S(2)}) %copy-start.1) | copy-done | bytes 196632
  14.8 0.1 collective-permute-done.4.refs_2_
  14.9 6.1 %collective-permute-done.6.refs_2_ = f32[4,72,128]{2,1,0:T(8,128)S(1)} collective-permute-done((f32[4,72,128]{2,1,0:T(8,128)S(1)}, f32[4,72,128]{2,1,0:T(8,128)S(1)}, u32[]{:S(2)}, u32[]{:S(2)}) %collective-permute-start.6) | collective-permute-done | bytes 147488 | tf_op jit(solution)/shard_map/ppermute | solution.py:520
  21.0 0.0 collective-permute-done.7.refs_3_
  21.0 0.3 collective-permute-done.5.refs_1_
  21.3 1.5 %collective-permute-start.11 = (f32[2,128,512]{2,1,0:T(8,128)S(1)}, f32[2,128,512]{2,1,0:T(8,128)S(1)}, u32[]{:S(2)}, u32[]{:S(2)}) collective-permute-start(f32[2,128,512]{2,1,0:T(8,128)S(1)} %get-tuple-element.58), channel_id=1, source_target_pairs={{0,8},{4,12},{8,0},{12,4},{16,24},{20,28},{24,16},{28,20},{1,9},{5... | collective-permute-start | bytes 1572872 | tf_op jit(solution)/shard_map/ppermute | solution.py:520
  22.8 1.4 %collective-permute-start.12 = (f32[2,128,512]{2,1,0:T(8,128)S(1)}, f32[2,128,512]{2,1,0:T(8,128)S(1)}, u32[]{:S(2)}, u32[]{:S(2)}) collective-permute-start(f32[2,128,512]{2,1,0:T(8,128)S(1)} %get-tuple-element.59), channel_id=1, source_target_pairs={{0,16},{4,20},{8,24},{12,28},{16,0},{20,4},{24,8},{28,12},{1,17},{... | collective-permute-start | bytes 1572872 | tf_op jit(solution)/shard_map/ppermute | solution.py:520
  24.3 1.6 %collective-permute-start.8 = (f32[2,72,128]{2,1,0:T(8,128)S(1)}, f32[2,72,128]{2,1,0:T(8,128)S(1)}, u32[]{:S(2)}, u32[]{:S(2)}) collective-permute-start(f32[2,72,128]{2,1,0:T(8,128)S(1)} %get-tuple-element.54), channel_id=1, source_target_pairs={{0,1},{1,0},{2,3},{3,2},{4,5},{5,4},{6,7},{7,6},{8,9},{9,8},{10,11... | collective-permute-start | bytes 221192 | tf_op jit(solution)/shard_map/ppermute | solution.py:520
  25.9 0.6 collective-permute-start.13
  26.5 2.2 %collective-permute-done.8 = f32[2,72,128]{2,1,0:T(8,128)S(1)} collective-permute-done((f32[2,72,128]{2,1,0:T(8,128)S(1)}, f32[2,72,128]{2,1,0:T(8,128)S(1)}, u32[]{:S(2)}, u32[]{:S(2)}) %collective-permute-start.8) | collective-permute-done | bytes 73760 | tf_op jit(solution)/shard_map/ppermute | solution.py:520
  28.7 2.7 %collective-permute-start.9 = (f32[2,72,128]{2,1,0:T(8,128)S(1)}, f32[2,72,128]{2,1,0:T(8,128)S(1)}, u32[]{:S(2)}, u32[]{:S(2)}) collective-permute-start(f32[2,72,128]{2,1,0:T(8,128)S(1)} %add.14), channel_id=1, source_target_pairs={{0,2},{1,3},{2,0},{3,1},{4,6},{5,7},{6,4},{7,5},{8,10},{9,11},{10,... | collective-permute-start | bytes 221192 | tf_op jit(solution)/shard_map/ppermute | solution.py:520
  31.4 0.6 collective-permute-start.14
  31.9 2.1 %collective-permute-done.9 = f32[2,72,128]{2,1,0:T(8,128)S(1)} collective-permute-done((f32[2,72,128]{2,1,0:T(8,128)S(1)}, f32[2,72,128]{2,1,0:T(8,128)S(1)}, u32[]{:S(2)}, u32[]{:S(2)}) %collective-permute-start.9) | collective-permute-done | bytes 73760 | tf_op jit(solution)/shard_map/ppermute | solution.py:520
  34.0 1.6 %collective-permute-start.10 = (f32[2,72,128]{2,1,0:T(8,128)S(1)}, f32[2,72,128]{2,1,0:T(8,128)S(1)}, u32[]{:S(2)}, u32[]{:S(2)}) collective-permute-start(f32[2,72,128]{2,1,0:T(8,128)S(1)} %add.15.refs_0_), channel_id=1, source_target_pairs={{0,1},{1,0},{2,3},{3,2},{4,5},{5,4},{6,7},{7,6},{8,9},{9,8},{10,11... | collective-permute-start | bytes 221192 | tf_op jit(solution)/shard_map/ppermute | solution.py:520
  35.7 0.1 stack.19.where
  35.8 2.7 %collective-permute-done.10.refs_1_ = f32[2,72,128]{2,1,0:T(8,128)S(1)} collective-permute-done((f32[2,72,128]{2,1,0:T(8,128)S(1)}, f32[2,72,128]{2,1,0:T(8,128)S(1)}, u32[]{:S(2)}, u32[]{:S(2)}) %collective-permute-start.10) | collective-permute-done | bytes 73760 | tf_op jit(solution)/shard_map/ppermute | solution.py:520
  38.4 5.3 %solve.1 = (f32[4,128,128]{2,1,0:T(8,128)S(1)}, f32[8,128]{1,0:T(8,128)S(1)}) custom-call(s32[1]{0:T(128)} %bitcast.4.row, f32[2,72,128]{2,1,0:T(8,128)S(1)} %add.15.refs_0_, f32[2,72,128]{2,1,0:T(8,128)S(1)} %collective-permute-done.10.refs_1_), custom_call_target="tpu_custom_call" | custom-call | tf_op jit(solution)/shard_map/solve/pallas_call | solution.py:340
  43.7 0.0 collective-permute-done.14.refs_6_
  43.8 0.0 collective-permute-done.13.refs_5_
  43.8 0.0 collective-permute-done.11.refs_3_
  43.8 0.0 collective-permute-done.12.refs_4_
  43.8 1.1 %edges.1 = (f32[520,128]{1,0:T(8,128)S(1)}, f32[512,128]{1,0:T(8,128)S(1)}) custom-call(s32[5]{0:T(128)S(1)} %stack.19.where, f32[8,128]{1,0:T(8,128)S(1)} %get-tuple-element.55.sums, f32[4,128,128]{2,1,0:T(8,128)S(1)} %get-tuple-element.56.held, f32[1,128,512]{2,1,0:T(8,128)S(1)} %get-tuple-element.35.refs_0_, ...), custom_call_target="tpu_custom_call" | custom-call | tf_op jit(solution)/shard_map/edges/pallas_call | solution.py:393
  44.9 0.1 collective-permute-start.15
  44.9 0.7 %collective-permute-start.16 = (f32[512,128]{1,0:T(8,128)S(1)}, f32[512,128]{1,0:T(8,128)S(1)}, u32[]{:S(2)}, u32[]{:S(2)}) collective-permute-start(f32[512,128]{1,0:T(8,128)S(1)} %get-tuple-element.64), channel_id=1, source_target_pairs={{4,8},{8,4},{12,16},{16,12},{20,24},{24,20},{5,9},{9,5},{13,17},{1... | collective-permute-start | bytes 786440 | tf_op jit(solution)/shard_map/ppermute | solution.py:515
  45.6 0.8 %collective-permute-done.15.near = f32[520,128]{1,0:T(8,128)S(1)} collective-permute-done((f32[520,128]{1,0:T(8,128)S(1)}, f32[520,128]{1,0:T(8,128)S(1)}, u32[]{:S(2)}, u32[]{:S(2)}) %collective-permute-start.15) | collective-permute-done | bytes 266272 | tf_op jit(solution)/shard_map/ppermute | solution.py:515
  46.5 2.6 %collective-permute-start.19 = (f32[8,128]{1,0:T(8,128)S(1)}, f32[8,128]{1,0:T(8,128)S(1)}, u32[]{:S(2)}, u32[]{:S(2)}) collective-permute-start(f32[8,128]{1,0:T(8,128)S(1)} %slice_add_fusion.refs_1_), channel_id=1, source_target_pairs={{0,8},{4,12},{8,0},{12,4},{16,24},{20,28},{24,16},{28,20},{1,9},{5... | collective-permute-start | bytes 12296 | tf_op jit(solution)/shard_map/ppermute | solution.py:520
  49.0 1.0 %collective-permute-start.18 = (f32[8,128]{1,0:T(8,128)S(1)}, f32[8,128]{1,0:T(8,128)S(1)}, u32[]{:S(2)}, u32[]{:S(2)}) collective-permute-start(f32[8,128]{1,0:T(8,128)S(1)} %slice_add_fusion.refs_1_), channel_id=1, source_target_pairs={{0,16},{4,20},{8,24},{12,28},{16,0},{20,4},{24,8},{28,12},{1,17},{... | collective-permute-start | bytes 12296 | tf_op jit(solution)/shard_map/ppermute | solution.py:520
  50.1 0.6 %collective-permute-start.17 = (f32[8,128]{1,0:T(8,128)S(1)}, f32[8,128]{1,0:T(8,128)S(1)}, u32[]{:S(2)}, u32[]{:S(2)}) collective-permute-start(f32[8,128]{1,0:T(8,128)S(1)} %slice_add_fusion.refs_1_), channel_id=1, source_target_pairs={{0,24},{4,28},{8,16},{12,20},{16,8},{20,12},{24,0},{28,4},{1,25},{... | collective-permute-start | bytes 12296 | tf_op jit(solution)/shard_map/ppermute | solution.py:520
  50.7 2.8 %place.1 = (f32[1024,512]{1,0:T(8,128)}, f32[1024,128]{1,0:T(8,128)S(1)}) custom-call(s32[5]{0:T(128)S(1)} %stack.19.where, f32[520,128]{1,0:T(8,128)S(1)} %collective-permute-done.15.near, f32[4,128,128]{2,1,0:T(8,128)S(1)} %get-tuple-element.56.held, f32[1,128,512]{2,1,0:T(8,128)S(1)} %get-tuple-element.35.refs_0_, ...), custom_call_target="tpu_custom_call" | custom-call | tf_op jit(solution)/shard_map/place/pallas_call | solution.py:445
  53.5 0.0 collective-permute-done.16.refs_0_
  53.5 2.5 %collective-permute-done.19.refs_4_ = f32[8,128]{1,0:T(8,128)S(1)} collective-permute-done((f32[8,128]{1,0:T(8,128)S(1)}, f32[8,128]{1,0:T(8,128)S(1)}, u32[]{:S(2)}, u32[]{:S(2)}) %collective-permute-start.19) | collective-permute-done | bytes 4128 | tf_op jit(solution)/shard_map/ppermute | solution.py:520
  56.0 0.0 collective-permute-done.18.refs_3_
  56.0 0.0 collective-permute-done.17.refs_2_
  56.0 1.5 %finish.1 = (f32[1024,512]{1,0:T(8,128)}, f32[1,1]{1,0:T(1,128)}) custom-call(s32[5]{0:T(128)S(1)} %stack.19.where, f32[1024,128]{1,0:T(8,128)S(1)} %get-tuple-element.63.mate, f32[512,128]{1,0:T(8,128)S(1)} %collective-permute-done.16.refs_0_, f32[8,128]{1,0:T(8,128)S(1)} %slice_add_fusion.refs_1_, ...), custom_call_target="tpu_custom_call", output_to_operand_aliasing={{0}: (7, {})} | custom-call | tf_op jit(solution)/shard_map/finish/pallas_call | solution.py:495
  (4 shorter events, 0.1 us)
Async XLA Ops:
  1.4 1.6 %copy-start = (f32[128,4096]{1,0:T(8,128)S(1)}, f32[128,4096]{1,0:T(8,128)}, u32[]{:S(2)}) copy-start(f32[128,4096]{1,0:T(8,128)} %source.1) | copy-start | bytes 6291460
  4.6 5.0 %collective-permute-start = (f32[1,128,512]{2,1,0:T(8,128)S(1)}, f32[1,128,512]{2,1,0:T(8,128)S(1)}, u32[]{:S(2)}, u32[]{:S(2)}) collective-permute-start(f32[1,128,512]{2,1,0:T(8,128)S(1)} %get-tuple-element.38), channel_id=1, source_target_pairs={{0,4},{4,0},{8,12},{12,8},{16,20},{20,16},{24,28},{28,24},{1,5},{5... | collective-permute-start | bytes 786440 | tf_op jit(solution)/shard_map/ppermute | solution.py:520
  5.1 4.5 %collective-permute-start.1 = (f32[1,128,512]{2,1,0:T(8,128)S(1)}, f32[1,128,512]{2,1,0:T(8,128)S(1)}, u32[]{:S(2)}, u32[]{:S(2)}) collective-permute-start(f32[1,128,512]{2,1,0:T(8,128)S(1)} %get-tuple-element.39), channel_id=1, source_target_pairs={{0,4},{4,0},{8,12},{12,8},{16,20},{20,16},{24,28},{28,24},{1,5},{5... | collective-permute-start | bytes 786440 | tf_op jit(solution)/shard_map/ppermute | solution.py:520
  5.2 4.4 %collective-permute-start.2 = (f32[1,128,512]{2,1,0:T(8,128)S(1)}, f32[1,128,512]{2,1,0:T(8,128)S(1)}, u32[]{:S(2)}, u32[]{:S(2)}) collective-permute-start(f32[1,128,512]{2,1,0:T(8,128)S(1)} %get-tuple-element.40), channel_id=1, source_target_pairs={{0,4},{4,0},{8,12},{12,8},{16,20},{20,16},{24,28},{28,24},{1,5},{5... | collective-permute-start | bytes 786440 | tf_op jit(solution)/shard_map/ppermute | solution.py:520
  5.6 4.0 %collective-permute-start.3 = (f32[1,128,512]{2,1,0:T(8,128)S(1)}, f32[1,128,512]{2,1,0:T(8,128)S(1)}, u32[]{:S(2)}, u32[]{:S(2)}) collective-permute-start(f32[1,128,512]{2,1,0:T(8,128)S(1)} %get-tuple-element.41), channel_id=1, source_target_pairs={{0,4},{4,0},{8,12},{12,8},{16,20},{20,16},{24,28},{28,24},{1,5},{5... | collective-permute-start | bytes 786440 | tf_op jit(solution)/shard_map/ppermute | solution.py:520
  5.7 9.2 %collective-permute-start.4 = (f32[1,128,384]{2,1,0:T(8,128)S(1)}, f32[1,128,384]{2,1,0:T(8,128)S(1)}, u32[]{:S(2)}, u32[]{:S(2)}) collective-permute-start(f32[1,128,384]{2,1,0:T(8,128)S(1)} %get-tuple-element.42.refs_7_), channel_id=1, source_target_pairs={{0,24},{4,28},{8,16},{12,20},{16,8},{20,12},{24,0},{28,4},{1,25},{... | collective-permute-start | bytes 589832 | tf_op jit(solution)/shard_map/ppermute | solution.py:520
  10.4 10.6 %collective-permute-start.6 = (f32[4,72,128]{2,1,0:T(8,128)S(1)}, f32[4,72,128]{2,1,0:T(8,128)S(1)}, u32[]{:S(2)}, u32[]{:S(2)}) collective-permute-start(f32[4,72,128]{2,1,0:T(8,128)S(1)} %get-tuple-element.48), channel_id=1, source_target_pairs={{0,16},{4,20},{8,24},{12,28},{16,0},{20,4},{24,8},{28,12},{1,17},{... | collective-permute-start | bytes 442376 | tf_op jit(solution)/shard_map/ppermute | solution.py:520
  11.2 9.8 %collective-permute-start.7 = (f32[4,72,128]{2,1,0:T(8,128)S(1)}, f32[4,72,128]{2,1,0:T(8,128)S(1)}, u32[]{:S(2)}, u32[]{:S(2)}) collective-permute-start(f32[4,72,128]{2,1,0:T(8,128)S(1)} %get-tuple-element.49), channel_id=1, source_target_pairs={{0,24},{4,28},{8,16},{12,20},{16,8},{20,12},{24,0},{28,4},{1,25},{... | collective-permute-start | bytes 442376 | tf_op jit(solution)/shard_map/ppermute | solution.py:520
  12.6 8.7 %collective-permute-start.5 = (f32[4,72,128]{2,1,0:T(8,128)S(1)}, f32[4,72,128]{2,1,0:T(8,128)S(1)}, u32[]{:S(2)}, u32[]{:S(2)}) collective-permute-start(f32[4,72,128]{2,1,0:T(8,128)S(1)} %get-tuple-element.45.after), channel_id=1, source_target_pairs={{0,8},{4,12},{8,0},{12,4},{16,24},{20,28},{24,16},{28,20},{1,9},{5... | collective-permute-start | bytes 442376 | tf_op jit(solution)/shard_map/ppermute | solution.py:520
  14.1 0.7 %copy-start.1 = (f32[3,128,128]{2,1,0:T(8,128)}, f32[3,128,128]{2,1,0:T(8,128)S(1)}, u32[]{:S(2)}) copy-start(f32[3,128,128]{2,1,0:T(8,128)S(1)} %get-tuple-element.60) | copy-start | bytes 589828
  21.3 22.5 %collective-permute-start.11 = (f32[2,128,512]{2,1,0:T(8,128)S(1)}, f32[2,128,512]{2,1,0:T(8,128)S(1)}, u32[]{:S(2)}, u32[]{:S(2)}) collective-permute-start(f32[2,128,512]{2,1,0:T(8,128)S(1)} %get-tuple-element.58), channel_id=1, source_target_pairs={{0,8},{4,12},{8,0},{12,4},{16,24},{20,28},{24,16},{28,20},{1,9},{5... | collective-permute-start | bytes 1572872 | tf_op jit(solution)/shard_map/ppermute | solution.py:520
  22.8 21.0 %collective-permute-start.12 = (f32[2,128,512]{2,1,0:T(8,128)S(1)}, f32[2,128,512]{2,1,0:T(8,128)S(1)}, u32[]{:S(2)}, u32[]{:S(2)}) collective-permute-start(f32[2,128,512]{2,1,0:T(8,128)S(1)} %get-tuple-element.59), channel_id=1, source_target_pairs={{0,16},{4,20},{8,24},{12,28},{16,0},{20,4},{24,8},{28,12},{1,17},{... | collective-permute-start | bytes 1572872 | tf_op jit(solution)/shard_map/ppermute | solution.py:520
  24.3 4.4 %collective-permute-start.8 = (f32[2,72,128]{2,1,0:T(8,128)S(1)}, f32[2,72,128]{2,1,0:T(8,128)S(1)}, u32[]{:S(2)}, u32[]{:S(2)}) collective-permute-start(f32[2,72,128]{2,1,0:T(8,128)S(1)} %get-tuple-element.54), channel_id=1, source_target_pairs={{0,1},{1,0},{2,3},{3,2},{4,5},{5,4},{6,7},{7,6},{8,9},{9,8},{10,11... | collective-permute-start | bytes 221192 | tf_op jit(solution)/shard_map/ppermute | solution.py:520
  25.9 17.8 %collective-permute-start.13 = (f32[3,128,128]{2,1,0:T(8,128)}, f32[3,128,128]{2,1,0:T(8,128)S(1)}, u32[]{:S(2)}, u32[]{:S(2)}) collective-permute-start(f32[3,128,128]{2,1,0:T(8,128)} %copy-done.1), channel_id=1, source_target_pairs={{0,24},{4,28},{8,16},{12,20},{16,8},{20,12},{24,0},{28,4},{1,25},{... | collective-permute-start | bytes 589832 | tf_op jit(solution)/shard_map/ppermute | solution.py:520
  28.7 5.3 %collective-permute-start.9 = (f32[2,72,128]{2,1,0:T(8,128)S(1)}, f32[2,72,128]{2,1,0:T(8,128)S(1)}, u32[]{:S(2)}, u32[]{:S(2)}) collective-permute-start(f32[2,72,128]{2,1,0:T(8,128)S(1)} %add.14), channel_id=1, source_target_pairs={{0,2},{1,3},{2,0},{3,1},{4,6},{5,7},{6,4},{7,5},{8,10},{9,11},{10,... | collective-permute-start | bytes 221192 | tf_op jit(solution)/shard_map/ppermute | solution.py:520
  31.4 12.4 %collective-permute-start.14 = (f32[2,128,128]{2,1,0:T(8,128)S(1)}, f32[2,128,128]{2,1,0:T(8,128)S(1)}, u32[]{:S(2)}, u32[]{:S(2)}) collective-permute-start(f32[2,128,128]{2,1,0:T(8,128)S(1)} %get-tuple-element.61), channel_id=1, source_target_pairs={{0,24},{4,28},{8,16},{12,20},{16,8},{20,12},{24,0},{28,4},{1,25},{... | collective-permute-start | bytes 393224 | tf_op jit(solution)/shard_map/ppermute | solution.py:520
  34.0 4.4 %collective-permute-start.10 = (f32[2,72,128]{2,1,0:T(8,128)S(1)}, f32[2,72,128]{2,1,0:T(8,128)S(1)}, u32[]{:S(2)}, u32[]{:S(2)}) collective-permute-start(f32[2,72,128]{2,1,0:T(8,128)S(1)} %add.15.refs_0_), channel_id=1, source_target_pairs={{0,1},{1,0},{2,3},{3,2},{4,5},{5,4},{6,7},{7,6},{8,9},{9,8},{10,11... | collective-permute-start | bytes 221192 | tf_op jit(solution)/shard_map/ppermute | solution.py:520
  44.9 1.6 %collective-permute-start.15 = (f32[520,128]{1,0:T(8,128)S(1)}, f32[520,128]{1,0:T(8,128)S(1)}, u32[]{:S(2)}, u32[]{:S(2)}) collective-permute-start(f32[520,128]{1,0:T(8,128)S(1)} %get-tuple-element.62), channel_id=1, source_target_pairs={{0,4},{4,0},{8,12},{12,8},{16,20},{20,16},{24,28},{28,24},{1,5},{5... | collective-permute-start | bytes 798728 | tf_op jit(solution)/shard_map/ppermute | solution.py:515
  44.9 8.6 %collective-permute-start.16 = (f32[512,128]{1,0:T(8,128)S(1)}, f32[512,128]{1,0:T(8,128)S(1)}, u32[]{:S(2)}, u32[]{:S(2)}) collective-permute-start(f32[512,128]{1,0:T(8,128)S(1)} %get-tuple-element.64), channel_id=1, source_target_pairs={{4,8},{8,4},{12,16},{16,12},{20,24},{24,20},{5,9},{9,5},{13,17},{1... | collective-permute-start | bytes 786440 | tf_op jit(solution)/shard_map/ppermute | solution.py:515
  46.5 9.6 %collective-permute-start.19 = (f32[8,128]{1,0:T(8,128)S(1)}, f32[8,128]{1,0:T(8,128)S(1)}, u32[]{:S(2)}, u32[]{:S(2)}) collective-permute-start(f32[8,128]{1,0:T(8,128)S(1)} %slice_add_fusion.refs_1_), channel_id=1, source_target_pairs={{0,8},{4,12},{8,0},{12,4},{16,24},{20,28},{24,16},{28,20},{1,9},{5... | collective-permute-start | bytes 12296 | tf_op jit(solution)/shard_map/ppermute | solution.py:520
  49.0 7.0 %collective-permute-start.18 = (f32[8,128]{1,0:T(8,128)S(1)}, f32[8,128]{1,0:T(8,128)S(1)}, u32[]{:S(2)}, u32[]{:S(2)}) collective-permute-start(f32[8,128]{1,0:T(8,128)S(1)} %slice_add_fusion.refs_1_), channel_id=1, source_target_pairs={{0,16},{4,20},{8,24},{12,28},{16,0},{20,4},{24,8},{28,12},{1,17},{... | collective-permute-start | bytes 12296 | tf_op jit(solution)/shard_map/ppermute | solution.py:520
  50.1 6.0 %collective-permute-start.17 = (f32[8,128]{1,0:T(8,128)S(1)}, f32[8,128]{1,0:T(8,128)S(1)}, u32[]{:S(2)}, u32[]{:S(2)}) collective-permute-start(f32[8,128]{1,0:T(8,128)S(1)} %slice_add_fusion.refs_1_), channel_id=1, source_target_pairs={{0,24},{4,28},{8,16},{12,20},{16,8},{20,12},{24,0},{28,4},{1,25},{... | collective-permute-start | bytes 12296 | tf_op jit(solution)/shard_map/ppermute | solution.py:520
